TPU v7x, 32 devices: a whole 2x2x4 slice. The times are simulated.
32 devices in a mesh: row: 8 (over z, x), col: 4 (over y, core).
Axes of the slice: x: 2, y: 2, z: 4, core: 2. Of those that a mesh axis runs over, the one named last changes fastest.
Arguments:
- signal: float32 [4096, 4096], P('row', 'col'), may hold values from -6 to 6
- apod: float32 [4096], P('row'), may hold values from 0.3 to 1
- coef: float32 [4, 4096], P(None, 'col'), may hold values from -0.5 to 1
- block_offset: int32 [128], P('col'), may hold values from -16 to 9
- fine_start: int32 [4096], P('col'), may hold values from 0 to 3
Outputs:
- calibrated: float32 [2, 4096, 4096], P(None, 'row', 'col')
All inputs are finite; a program needn't handle non-finite values.
Results may differ from a plain program's by a relative error of at most 0.000084.
Values sent between devices are 32-bit elements; how exact they have to be, the bound alone decides.
No kernel may reach another device: no remote copies, remote signals or barrier semaphores. Data moves between devices by JAX's collectives and lax.ppermute only.
A program may use at most 128 MiB of HBM per device.

v0:
```python
import functools
import math

import jax
import jax.numpy as jnp
import numpy as np
from jax import lax
from jax.experimental import pallas as pl
from jax.experimental.pallas import tpu as pltpu
from jax.sharding import PartitionSpec as P

TAPS = 4
LANES = 128
VMEM = 40 * 1024 * 1024


def split_bf16(value):
    high = value.astype(jnp.bfloat16)
    low = (value - high.astype(jnp.float32)).astype(jnp.bfloat16)
    return high, low


def dot3(a, b):
    dot = functools.partial(jnp.dot, preferred_element_type=jnp.float32)
    return dot(a[0], b[0]) + (dot(a[0], b[1]) + dot(a[1], b[0]))


def stencil_kernel(left, mid, right, apod, coef, offset, out):
    shape = (3 * LANES, LANES)
    tap_at = (
        lax.broadcasted_iota(jnp.int32, shape, 0)
        - lax.broadcasted_iota(jnp.int32, shape, 1)
        - LANES
        - offset[...]
    )
    band = jnp.zeros(shape, jnp.float32)
    for tap in range(TAPS):
        band = jnp.where(tap_at == tap, coef[tap : tap + 1, :], band)
    field = jnp.concatenate([left[...], mid[...], right[...]], axis=1)
    out[...] = apod[...] * dot3(split_bf16(field), split_bf16(band))


def stencil(left, mid, right, apod, coef, offset, block, count):
    rows = mid[0].shape[0]

    def columns(height, start):
        return pl.BlockSpec((height, LANES), lambda i: (0, start + i))

    return pl.pallas_call(
        stencil_kernel,
        grid=(count,),
        in_specs=[
            columns(rows, left[1]),
            columns(rows, mid[1]),
            columns(rows, right[1]),
            pl.BlockSpec((rows, 1), lambda i: (0, 0)),
            columns(TAPS, block),
            columns(1, block),
        ],
        out_specs=columns(rows, 0),
        out_shape=jax.ShapeDtypeStruct((rows, count * LANES), jnp.float32),
        compiler_params=pltpu.CompilerParams(vmem_limit_bytes=VMEM),
        cost_estimate=pl.CostEstimate(
            flops=6 * rows * 3 * LANES * LANES * count,
            bytes_accessed=16 * rows * LANES * count,
            transcendentals=0,
        ),
        name="stencil",
    )(left[0], mid[0], right[0], apod, coef, offset)


def inner_kernel(has_im, aliased, *refs):
    factors, cos_high, cos_low, sin_high, sin_low, *blocks = refs
    out = blocks.pop()
    if aliased:
        blocks.pop()
    a_re, a_im, b_re, b_im = (factors[:, i : i + 1] for i in range(4))
    if has_im:
        own_re, own_im, far_re, far_im = (ref[...] for ref in blocks)
        y_re = a_re * own_re - a_im * own_im + (b_re * far_re - b_im * far_im)
        y_im = a_re * own_im + a_im * own_re + (b_re * far_im + b_im * far_re)
    else:
        own_re, far_re = (ref[...] for ref in blocks)
        y_re = a_re * own_re + b_re * far_re
        y_im = a_im * own_re + b_im * far_re
    width = y_re.shape[1]
    both = split_bf16(jnp.concatenate([y_re, y_im], axis=1))
    cos_part = dot3((cos_high[...], cos_low[...]), both)
    sin_part = dot3((sin_high[...], sin_low[...]), both)
    out[0] = cos_part[:, :width] + sin_part[:, width:]
    out[1] = cos_part[:, width:] - sin_part[:, :width]


def inner(blocks, factors, tables, result, start, full_width):
    rows, width = blocks[0].shape
    aliased = result is not None
    whole = pl.BlockSpec((rows, rows), lambda i: (0, 0))
    step = width // LANES
    first = start // LANES
    inputs = [factors, *tables, *blocks] + ([result] if aliased else [])
    specs = (
        [pl.BlockSpec((rows, 4), lambda i: (0, 0))]
        + [whole] * 4
        + [pl.BlockSpec((rows, LANES), lambda i: (0, i))] * len(blocks)
        + ([pl.BlockSpec(memory_space=pl.ANY)] if aliased else [])
    )
    return pl.pallas_call(
        functools.partial(inner_kernel, len(blocks) == 4, aliased),
        grid=(step,),
        in_specs=specs,
        out_specs=pl.BlockSpec((2, rows, LANES), lambda i: (0, 0, first + i)),
        out_shape=jax.ShapeDtypeStruct((2, rows, full_width), jnp.float32),
        input_output_aliases={len(inputs) - 1: 0} if aliased else {},
        compiler_params=pltpu.CompilerParams(vmem_limit_bytes=VMEM),
        cost_estimate=pl.CostEstimate(
            flops=24 * rows * rows * width,
            bytes_accessed=4 * rows * width * 6 + 8 * rows * rows,
            transcendentals=0,
        ),
        name="inner",
    )(*inputs)


def reversed_bits(value, levels):
    return sum((value >> i & 1) << levels - 1 - i for i in range(levels))


def butterfly_plan(devices):
    stages = []
    phase = np.ones(devices, np.complex128)
    is_real = [True] * devices
    half = devices // 2
    while half:
        own, far = np.zeros(devices, np.complex128), np.zeros(devices, np.complex128)
        next_phase, next_real = phase.copy(), list(is_real)
        for a in range(devices):
            b = a ^ half
            upper = bool(a & half)
            turn = np.exp(-2j * np.pi * (a % half) / (2 * half)) if upper else 1.0
            keep = is_real[a] and phase[a] == 1 and phase[b] == 1
            if keep:
                own[a], far[a] = (-1 if upper else 1), 1
                next_phase[a] = turn
            else:
                own[a] = phase[a] * (-turn if upper else 1)
                far[a] = phase[b] * turn
                next_phase[a], next_real[a] = 1, False
        stages.append((half, own, far, [a for a in range(devices) if not is_real[a]], next_phase))
        phase, is_real = next_phase, next_real
        half //= 2
    return stages


def inner_tables(count, total):
    index = np.arange(count)
    angle = 2 * np.pi / count * (index[:, None] * index[None, :] % count)
    tables = []
    for part in (np.cos(angle), np.sin(angle)):
        part = part / math.sqrt(total)
        high = part.astype(jnp.bfloat16)
        tables += [high, (part - high.astype(np.float64)).astype(jnp.bfloat16)]
    return [jnp.asarray(t) for t in tables]


def parts(values):
    return np.stack([values.real, values.imag], -1).astype(np.float32)


def on_device(signal, apod, coef, block_offset, fine_start):
    rows, width = signal.shape
    devices, me = lax.axis_size("row"), lax.axis_index("row")
    levels = devices.bit_length() - 1
    total = rows * devices
    count = width // LANES
    spread = jnp.broadcast_to(
        block_offset[:, None], (block_offset.shape[0], width // block_offset.shape[0])
    ).reshape(width)
    offset = (spread + fine_start)[None, :]
    apod = apod[:, None]

    neighbours = lax.axis_size("col")
    up = [(i, i + 1) for i in range(neighbours - 1)]
    down = [(j, i) for i, j in up]
    before = lax.ppermute(signal[:, width - LANES :], "col", up)
    after = lax.ppermute(signal[:, :LANES], "col", down)

    stages = butterfly_plan(devices)
    tables = inner_tables(rows, total)
    outer = np.array([reversed_bits(a, levels) for a in range(devices)])
    twiddle = np.exp(-2j * np.pi / total * (outer[:, None] * np.arange(rows)[None, :] % total))
    _, own, far, _, phase = stages[-1]
    factors = np.concatenate(
        [parts((f * phase)[:, None] * twiddle) for f in (own, far)], axis=-1
    )
    factors = jnp.asarray(factors)[me]
    scalars = [
        jnp.asarray(np.concatenate([parts(s[1]), parts(s[2])], -1))[me] for s in stages[:-1]
    ]

    middle = list(range(1, count - 1))
    size = max(1, (len(middle) + 2) // 3)
    chunks = [(b, min(size, count - 1 - b)) for b in middle[::size]]
    fields = []
    for block, number in chunks:
        field = stencil(
            (signal, block - 1), (signal, block), (signal, block + 1), apod, coef, offset, block, number
        )
        fields.append((block, field))
    for block in (0, count - 1):
        left = (before, 0) if block == 0 else (signal, block - 1)
        right = (after, 0) if block == count - 1 else (signal, block + 1)
        field = stencil(left, (signal, block), right, apod, coef, offset, block, 1)
        fields.append((block, field))

    result = None
    for block, field in fields:
        real, imag = field, None
        for level, (half, own, far, complex_at, _) in enumerate(stages):
            everyone = [(a, a ^ half) for a in range(devices)]
            far_real = lax.ppermute(real, "row", everyone)
            far_imag = None
            if complex_at:
                far_imag = lax.ppermute(imag, "row", [(a, a ^ half) for a in complex_at])
            if level == levels - 1:
                break
            a_re, a_im, b_re, b_im = (scalars[level][i] for i in range(4))
            if far_imag is not None:
                real, imag = (
                    a_re * real - a_im * imag + (b_re * far_real - b_im * far_imag),
                    a_re * imag + a_im * real + (b_re * far_imag + b_im * far_real),
                )
            elif np.any(own.imag) or np.any(far.imag):
                real, imag = (a_re * real + b_re * far_real, a_im * real + b_im * far_real)
            else:
                real = a_re * real + b_re * far_real
        blocks = [real, far_real] if far_imag is None else [real, imag, far_real, far_imag]
        result = inner(blocks, factors, tables, result, block * LANES, width)
    return result


def solution(mesh):
    placed = (P("row", "col"), P("row"), P(None, "col"), P("col"), P("col"))
    return jax.shard_map(
        on_device, mesh=mesh, in_specs=placed, out_specs=P(None, "row", "col"), check_vma=False
    )
```

profile of v0, /device:TPU:26, one launch (start us, length us, event | category | flops | bytes accessed | tf_op | source)
XLA Modules:
  0.0 208.6 jit_solution(18062317625082237143)
XLA Ops:
  8.4 2.7 %collective-permute-start.14 = (f32[512,256]{1,0:T(8,128)S(1)}, f32[512,256]{1,0:T(8,128)}, u32[]{:S(2)}, u32[]{:S(2)}) collective-permute-start(f32[512,256]{1,0:T(8,128)S(1)} %stencil.8), channel_id=1, source_target_pairs={{0,16},{4,20},{8,24},{12,28},{16,0},{20,4},{24,8},{28,12},{1,17},{... | collective-permute-start | bytes 1572872 | tf_op jit(solution)/shard_map/ppermute | solution.py:220
  21.4 2.7 %collective-permute-start.6 = (f32[512,128]{1,0:T(8,128)S(1)}, f32[512,128]{1,0:T(8,128)S(1)}, u32[]{:S(2)}, u32[]{:S(2)}) collective-permute-start(f32[512,128]{1,0:T(8,128)S(1)} %stencil.6), channel_id=1, source_target_pairs={{0,16},{4,20},{8,24},{12,28},{16,0},{20,4},{24,8},{28,12},{1,17},{... | collective-permute-start | bytes 786440 | tf_op jit(solution)/shard_map/ppermute | solution.py:220
  26.0 40.5 %collective-permute-done.18 = f32[512,256]{1,0:T(8,128)} collective-permute-done((f32[512,256]{1,0:T(8,128)}, f32[512,256]{1,0:T(8,128)}, u32[]{:S(2)}, u32[]{:S(2)}) %collective-permute-start.18) | collective-permute-done | bytes 524320 | tf_op jit(solution)/shard_map/ppermute | solution.py:220
  68.9 8.9 %collective-permute-done.14 = f32[512,256]{1,0:T(8,128)} collective-permute-done((f32[512,256]{1,0:T(8,128)S(1)}, f32[512,256]{1,0:T(8,128)}, u32[]{:S(2)}, u32[]{:S(2)}) %collective-permute-start.14) | collective-permute-done | bytes 524320 | tf_op jit(solution)/shard_map/ppermute | solution.py:220
  80.1 8.9 %collective-permute-done.10 = f32[512,256]{1,0:T(8,128)} collective-permute-done((f32[512,256]{1,0:T(8,128)S(1)}, f32[512,256]{1,0:T(8,128)}, u32[]{:S(2)}, u32[]{:S(2)}) %collective-permute-start.10) | collective-permute-done | bytes 524320 | tf_op jit(solution)/shard_map/ppermute | solution.py:220
  91.3 3.2 %collective-permute-done.6 = f32[512,128]{1,0:T(8,128)S(1)} collective-permute-done((f32[512,128]{1,0:T(8,128)S(1)}, f32[512,128]{1,0:T(8,128)S(1)}, u32[]{:S(2)}, u32[]{:S(2)}) %collective-permute-start.6) | collective-permute-done | bytes 262176 | tf_op jit(solution)/shard_map/ppermute | solution.py:220
  95.8 4.3 %collective-permute-done.1 = f32[512,128]{1,0:T(8,128)S(1)} collective-permute-done((f32[512,128]{1,0:T(8,128)S(1)}, f32[512,128]{1,0:T(8,128)S(1)}, u32[]{:S(2)}, u32[]{:S(2)}) %collective-permute-start.1) | collective-permute-done | bytes 262176 | tf_op jit(solution)/shard_map/ppermute | solution.py:220
  101.3 10.0 %collective-permute-done.19 = f32[512,256]{1,0:T(8,128)S(1)} collective-permute-done((f32[512,256]{1,0:T(8,128)S(1)}, f32[512,256]{1,0:T(8,128)S(1)}, u32[]{:S(2)}, u32[]{:S(2)}) %collective-permute-start.19) | collective-permute-done | bytes 524320 | tf_op jit(solution)/shard_map/ppermute | solution.py:220
  111.3 2.7 %multiply_add_fusion = (f32[512,256]{1,0:T(8,128)S(1)}, f32[512,256]{1,0:T(8,128)S(1)}) fusion(f32[512,256]{1,0:T(8,128)S(1)} %collective-permute-done.19, f32[512,256]{1,0:T(8,128)S(1)} %multiply_add_fusion.2, f32[]{:T(128)} %bitcast.8, f32[]{:T(128)} %bitcast.7, f32[]{:T(128)} %bitcast.6, f32[]{:T(128)} %bitcast.1), kind=kLoop, calls=%fused_computation | loop fusion | flops 786432 | bytes 2097168 | tf_op jit(solution)/shard_map/add | solution.py:233
  114.6 7.9 %collective-permute-done.15 = f32[512,256]{1,0:T(8,128)S(1)} collective-permute-done((f32[512,256]{1,0:T(8,128)S(1)}, f32[512,256]{1,0:T(8,128)S(1)}, u32[]{:S(2)}, u32[]{:S(2)}) %collective-permute-start.15) | collective-permute-done | bytes 524320 | tf_op jit(solution)/shard_map/ppermute | solution.py:220
  125.0 2.6 %multiply_add_fusion.3 = (f32[512,256]{1,0:T(8,128)S(1)}, f32[512,256]{1,0:T(8,128)S(1)}) fusion(f32[512,256]{1,0:T(8,128)S(1)} %collective-permute-done.15, f32[512,256]{1,0:T(8,128)S(1)} %multiply_add_fusion.5, f32[]{:T(128)} %bitcast.8, f32[]{:T(128)} %bitcast.7, f32[]{:T(128)} %bitcast.6, f32[]{:T(128)} %bitcast.1), kind=kLoop, calls=%fused_computation.3 | loop fusion | flops 786432 | bytes 2097168 | tf_op jit(solution)/shard_map/add | solution.py:233
  127.5 6.2 %collective-permute-done.11 = f32[512,256]{1,0:T(8,128)S(1)} collective-permute-done((f32[512,256]{1,0:T(8,128)S(1)}, f32[512,256]{1,0:T(8,128)S(1)}, u32[]{:S(2)}, u32[]{:S(2)}) %collective-permute-start.11) | collective-permute-done | bytes 524320 | tf_op jit(solution)/shard_map/ppermute | solution.py:220
  134.3 2.6 %multiply_add_fusion.6 = (f32[512,256]{1,0:T(8,128)S(1)}, f32[512,256]{1,0:T(8,128)S(1)}) fusion(f32[512,256]{1,0:T(8,128)S(1)} %collective-permute-done.11, f32[512,256]{1,0:T(8,128)S(1)} %multiply_add_fusion.8, f32[]{:T(128)} %bitcast.8, f32[]{:T(128)} %bitcast.7, f32[]{:T(128)} %bitcast.6, f32[]{:T(128)} %bitcast.1), kind=kLoop, calls=%fused_computation.6 | loop fusion | flops 786432 | bytes 2097168 | tf_op jit(solution)/shard_map/add | solution.py:233
  141.8 3.1 %collective-permute-done.2 = f32[512,128]{1,0:T(8,128)S(1)} collective-permute-done((f32[512,128]{1,0:T(8,128)S(1)}, f32[512,128]{1,0:T(8,128)S(1)}, u32[]{:S(2)}, u32[]{:S(2)}) %collective-permute-start.2) | collective-permute-done | bytes 262176 | tf_op jit(solution)/shard_map/ppermute | solution.py:220
  148.0 3.4 %collective-permute-start.13 = (f32[512,256]{1,0:T(8,128)S(1)}, f32[512,256]{1,0:T(8,128)S(1)}, u32[]{:S(2)}, u32[]{:S(2)}) collective-permute-start(f32[512,256]{1,0:T(8,128)S(1)} %get-tuple-element.11.refs_6_), channel_id=1, source_target_pairs={{16,20},{20,16},{24,28},{28,24},{17,21},{21,17},{25,29},{29,25},{1... | collective-permute-start | bytes 1572872 | tf_op jit(solution)/shard_map/ppermute | solution.py:223
  154.5 3.7 %inner.5.refs_9_ = f32[2,512,1024]{2,1,0:T(8,128)} custom-call(f32[512,4]{1,0:T(8,128)S(1)} %dynamic-slice_bitcast_fusion.refs_0_, bf16[512,512]{1,0:T(8,128)(2,1)S(1)} %copy-done.2, bf16[512,512]{1,0:T(8,128)(2,1)S(1)} %copy-done.3, bf16[512,512]{1,0:T(8,128)(2,1)S(1)} %copy-done.4, bf16[512,512]{1,0:T(8,128)(2,1)S(1)} %copy-done.5, ...), custom_call_target="tpu_custom_call" | custom-call | flops 1610612736 | bytes 5242880 | tf_op jit(solution)/shard_map/inner/pallas_call | solution.py:107
  158.2 3.4 %collective-permute-start.9 = (f32[512,128]{1,0:T(8,128)S(1)}, f32[512,128]{1,0:T(8,128)S(1)}, u32[]{:S(2)}, u32[]{:S(2)}) collective-permute-start(f32[512,128]{1,0:T(8,128)S(1)} %get-tuple-element.13.refs_6_), channel_id=1, source_target_pairs={{16,20},{20,16},{24,28},{28,24},{17,21},{21,17},{25,29},{29,25},{1... | collective-permute-start | bytes 786440 | tf_op jit(solution)/shard_map/ppermute | solution.py:223
  162.9 10.7 %collective-permute-done.12.refs_7_ = f32[512,256]{1,0:T(8,128)S(1)} collective-permute-done((f32[512,256]{1,0:T(8,128)S(1)}, f32[512,256]{1,0:T(8,128)S(1)}, u32[]{:S(2)}, u32[]{:S(2)}) %collective-permute-start.12) | collective-permute-done | bytes 524320 | tf_op jit(solution)/shard_map/ppermute | solution.py:220
  176.1 3.7 %inner.6.refs_9_ = f32[2,512,1024]{2,1,0:T(8,128)} custom-call(f32[512,4]{1,0:T(8,128)S(1)} %dynamic-slice_bitcast_fusion.refs_0_, bf16[512,512]{1,0:T(8,128)(2,1)S(1)} %copy-done.2, bf16[512,512]{1,0:T(8,128)(2,1)S(1)} %copy-done.3, bf16[512,512]{1,0:T(8,128)(2,1)S(1)} %copy-done.4, bf16[512,512]{1,0:T(8,128)(2,1)S(1)} %copy-done.5, ...), custom_call_target="tpu_custom_call", output_to_operand_aliasing={{}: (9, {})} | custom-call | flops 1610612736 | bytes 5242880 | tf_op jit(solution)/shard_map/inner/pallas_call | solution.py:107
  179.7 5.1 %collective-permute-done.13.refs_8_ = f32[512,256]{1,0:T(8,128)S(1)} collective-permute-done((f32[512,256]{1,0:T(8,128)S(1)}, f32[512,256]{1,0:T(8,128)S(1)}, u32[]{:S(2)}, u32[]{:S(2)}) %collective-permute-start.13) | collective-permute-done | bytes 524320 | tf_op jit(solution)/shard_map/ppermute | solution.py:223
  184.9 3.7 %inner.7.refs_9_ = f32[2,512,1024]{2,1,0:T(8,128)} custom-call(f32[512,4]{1,0:T(8,128)S(1)} %dynamic-slice_bitcast_fusion.refs_0_, bf16[512,512]{1,0:T(8,128)(2,1)S(1)} %copy-done.2, bf16[512,512]{1,0:T(8,128)(2,1)S(1)} %copy-done.3, bf16[512,512]{1,0:T(8,128)(2,1)S(1)} %copy-done.4, bf16[512,512]{1,0:T(8,128)(2,1)S(1)} %copy-done.5, ...), custom_call_target="tpu_custom_call", output_to_operand_aliasing={{}: (9, {})} | custom-call | flops 1610612736 | bytes 5242880 | tf_op jit(solution)/shard_map/inner/pallas_call | solution.py:107
  190.5 5.6 %collective-permute-done.9.refs_8_ = f32[512,128]{1,0:T(8,128)S(1)} collective-permute-done((f32[512,128]{1,0:T(8,128)S(1)}, f32[512,128]{1,0:T(8,128)S(1)}, u32[]{:S(2)}, u32[]{:S(2)}) %collective-permute-start.9) | collective-permute-done | bytes 262176 | tf_op jit(solution)/shard_map/ppermute | solution.py:223
  198.2 3.5 %collective-permute-done.3.refs_7_ = f32[512,128]{1,0:T(8,128)S(1)} collective-permute-done((f32[512,128]{1,0:T(8,128)S(1)}, f32[512,128]{1,0:T(8,128)S(1)}, u32[]{:S(2)}, u32[]{:S(2)}) %collective-permute-start.3) | collective-permute-done | bytes 262176 | tf_op jit(solution)/shard_map/ppermute | solution.py:220
  201.7 4.8 %collective-permute-done.4.refs_8_ = f32[512,128]{1,0:T(8,128)S(1)} collective-permute-done((f32[512,128]{1,0:T(8,128)S(1)}, f32[512,128]{1,0:T(8,128)S(1)}, u32[]{:S(2)}, u32[]{:S(2)}) %collective-permute-start.4) | collective-permute-done | bytes 262176 | tf_op jit(solution)/shard_map/ppermute | solution.py:223
  (65 shorter events, 54.7 us)
Async XLA Ops:
  6.7 59.8 %collective-permute-start.18 = (f32[512,256]{1,0:T(8,128)}, f32[512,256]{1,0:T(8,128)}, u32[]{:S(2)}, u32[]{:S(2)}) collective-permute-start(f32[512,256]{1,0:T(8,128)} %stencil.9), channel_id=1, source_target_pairs={{0,16},{4,20},{8,24},{12,28},{16,0},{20,4},{24,8},{28,12},{1,17},{... | collective-permute-start | bytes 1572872 | tf_op jit(solution)/shard_map/ppermute | solution.py:220
  8.4 69.4 %collective-permute-start.14 = (f32[512,256]{1,0:T(8,128)S(1)}, f32[512,256]{1,0:T(8,128)}, u32[]{:S(2)}, u32[]{:S(2)}) collective-permute-start(f32[512,256]{1,0:T(8,128)S(1)} %stencil.8), channel_id=1, source_target_pairs={{0,16},{4,20},{8,24},{12,28},{16,0},{20,4},{24,8},{28,12},{1,17},{... | collective-permute-start | bytes 1572872 | tf_op jit(solution)/shard_map/ppermute | solution.py:220
  12.4 76.6 %collective-permute-start.10 = (f32[512,256]{1,0:T(8,128)S(1)}, f32[512,256]{1,0:T(8,128)}, u32[]{:S(2)}, u32[]{:S(2)}) collective-permute-start(f32[512,256]{1,0:T(8,128)S(1)} %stencil.7), channel_id=1, source_target_pairs={{0,16},{4,20},{8,24},{12,28},{16,0},{20,4},{24,8},{28,12},{1,17},{... | collective-permute-start | bytes 1572872 | tf_op jit(solution)/shard_map/ppermute | solution.py:220
  13.7 6.2 %collective-permute-start.5 = (f32[512,128]{1,0:T(8,128)}, f32[512,128]{1,0:T(8,128)}, u32[]{:S(2)}, u32[]{:S(2)}) collective-permute-start(f32[512,128]{1,0:T(8,128)} %get-tuple-element.5), channel_id=1, source_target_pairs={{0,1},{1,2},{2,3},{4,5},{5,6},{6,7},{8,9},{9,10},{10,11},{12,13},{... | collective-permute-start | bytes 786440 | tf_op jit(solution)/shard_map/ppermute | solution.py:184
  15.7 8.4 %collective-permute-start = (f32[512,128]{1,0:T(8,128)}, f32[512,128]{1,0:T(8,128)}, u32[]{:S(2)}, u32[]{:S(2)}) collective-permute-start(f32[512,128]{1,0:T(8,128)} %get-tuple-element.6), channel_id=1, source_target_pairs={{1,0},{2,1},{3,2},{5,4},{6,5},{7,6},{9,8},{10,9},{11,10},{13,12},{... | collective-permute-start | bytes 786440 | tf_op jit(solution)/shard_map/ppermute | solution.py:185
  21.4 73.2 %collective-permute-start.6 = (f32[512,128]{1,0:T(8,128)S(1)}, f32[512,128]{1,0:T(8,128)S(1)}, u32[]{:S(2)}, u32[]{:S(2)}) collective-permute-start(f32[512,128]{1,0:T(8,128)S(1)} %stencil.6), channel_id=1, source_target_pairs={{0,16},{4,20},{8,24},{12,28},{16,0},{20,4},{24,8},{28,12},{1,17},{... | collective-permute-start | bytes 786440 | tf_op jit(solution)/shard_map/ppermute | solution.py:220
  25.6 74.5 %collective-permute-start.1 = (f32[512,128]{1,0:T(8,128)S(1)}, f32[512,128]{1,0:T(8,128)S(1)}, u32[]{:S(2)}, u32[]{:S(2)}) collective-permute-start(f32[512,128]{1,0:T(8,128)S(1)} %stencil.5), channel_id=1, source_target_pairs={{0,16},{4,20},{8,24},{12,28},{16,0},{20,4},{24,8},{28,12},{1,17},{... | collective-permute-start | bytes 786440 | tf_op jit(solution)/shard_map/ppermute | solution.py:220
  68.8 42.4 %collective-permute-start.19 = (f32[512,256]{1,0:T(8,128)S(1)}, f32[512,256]{1,0:T(8,128)S(1)}, u32[]{:S(2)}, u32[]{:S(2)}) collective-permute-start(f32[512,256]{1,0:T(8,128)S(1)} %multiply_add_fusion.2), channel_id=1, source_target_pairs={{0,8},{4,12},{8,0},{12,4},{16,24},{20,28},{24,16},{28,20},{1,9},{5... | collective-permute-start | bytes 1572872 | tf_op jit(solution)/shard_map/ppermute | solution.py:220
  80.0 42.5 %collective-permute-start.15 = (f32[512,256]{1,0:T(8,128)S(1)}, f32[512,256]{1,0:T(8,128)S(1)}, u32[]{:S(2)}, u32[]{:S(2)}) collective-permute-start(f32[512,256]{1,0:T(8,128)S(1)} %multiply_add_fusion.5), channel_id=1, source_target_pairs={{0,8},{4,12},{8,0},{12,4},{16,24},{20,28},{24,16},{28,20},{1,9},{5... | collective-permute-start | bytes 1572872 | tf_op jit(solution)/shard_map/ppermute | solution.py:220
  91.3 42.5 %collective-permute-start.11 = (f32[512,256]{1,0:T(8,128)S(1)}, f32[512,256]{1,0:T(8,128)S(1)}, u32[]{:S(2)}, u32[]{:S(2)}) collective-permute-start(f32[512,256]{1,0:T(8,128)S(1)} %multiply_add_fusion.8), channel_id=1, source_target_pairs={{0,8},{4,12},{8,0},{12,4},{16,24},{20,28},{24,16},{28,20},{1,9},{5... | collective-permute-start | bytes 1572872 | tf_op jit(solution)/shard_map/ppermute | solution.py:220
  95.7 43.7 %collective-permute-start.7 = (f32[512,128]{1,0:T(8,128)S(1)}, f32[512,128]{1,0:T(8,128)S(1)}, u32[]{:S(2)}, u32[]{:S(2)}) collective-permute-start(f32[512,128]{1,0:T(8,128)S(1)} %multiply_add_fusion.11), channel_id=1, source_target_pairs={{0,8},{4,12},{8,0},{12,4},{16,24},{20,28},{24,16},{28,20},{1,9},{5... | collective-permute-start | bytes 786440 | tf_op jit(solution)/shard_map/ppermute | solution.py:220
  101.2 43.7 %collective-permute-start.2 = (f32[512,128]{1,0:T(8,128)S(1)}, f32[512,128]{1,0:T(8,128)S(1)}, u32[]{:S(2)}, u32[]{:S(2)}) collective-permute-start(f32[512,128]{1,0:T(8,128)S(1)} %multiply_add_fusion.14), channel_id=1, source_target_pairs={{0,8},{4,12},{8,0},{12,4},{16,24},{20,28},{24,16},{28,20},{1,9},{5... | collective-permute-start | bytes 786440 | tf_op jit(solution)/shard_map/ppermute | solution.py:220
  111.3 43.2 %copy-start.4 = (bf16[512,512]{1,0:T(8,128)(2,1)S(1)}, bf16[512,512]{1,0:T(8,128)(2,1)}, u32[]{:S(2)}) copy-start(bf16[512,512]{1,0:T(8,128)(2,1)} %constant.26.clone.refs_3_) | copy-start | bytes 1572868
  111.3 43.2 %copy-start.5 = (bf16[512,512]{1,0:T(8,128)(2,1)S(1)}, bf16[512,512]{1,0:T(8,128)(2,1)}, u32[]{:S(2)}) copy-start(bf16[512,512]{1,0:T(8,128)(2,1)} %constant.27.clone.refs_4_) | copy-start | bytes 1572868
  114.0 33.9 %collective-permute-start.20 = (f32[512,256]{1,0:T(8,128)S(1)}, f32[512,256]{1,0:T(8,128)S(1)}, u32[]{:S(2)}, u32[]{:S(2)}) collective-permute-start(f32[512,256]{1,0:T(8,128)S(1)} %get-tuple-element.8.refs_5_), channel_id=1, source_target_pairs={{0,4},{4,0},{8,12},{12,8},{16,20},{20,16},{24,28},{28,24},{1,5},{5... | collective-permute-start | bytes 1572872 | tf_op jit(solution)/shard_map/ppermute | solution.py:220
  122.5 31.4 %collective-permute-start.21 = (f32[512,256]{1,0:T(8,128)S(1)}, f32[512,256]{1,0:T(8,128)S(1)}, u32[]{:S(2)}, u32[]{:S(2)}) collective-permute-start(f32[512,256]{1,0:T(8,128)S(1)} %get-tuple-element.7.refs_6_), channel_id=1, source_target_pairs={{16,20},{20,16},{24,28},{28,24},{17,21},{21,17},{25,29},{29,25},{1... | collective-permute-start | bytes 1572872 | tf_op jit(solution)/shard_map/ppermute | solution.py:223
  133.8 24.4 %collective-permute-start.16 = (f32[512,256]{1,0:T(8,128)S(1)}, f32[512,256]{1,0:T(8,128)S(1)}, u32[]{:S(2)}, u32[]{:S(2)}) collective-permute-start(f32[512,256]{1,0:T(8,128)S(1)} %get-tuple-element.10.refs_5_), channel_id=1, source_target_pairs={{0,4},{4,0},{8,12},{12,8},{16,20},{20,16},{24,28},{28,24},{1,5},{5... | collective-permute-start | bytes 1572872 | tf_op jit(solution)/shard_map/ppermute | solution.py:220
  139.4 23.0 %collective-permute-start.17 = (f32[512,256]{1,0:T(8,128)S(1)}, f32[512,256]{1,0:T(8,128)S(1)}, u32[]{:S(2)}, u32[]{:S(2)}) collective-permute-start(f32[512,256]{1,0:T(8,128)S(1)} %get-tuple-element.9.refs_6_), channel_id=1, source_target_pairs={{16,20},{20,16},{24,28},{28,24},{17,21},{21,17},{25,29},{29,25},{1... | collective-permute-start | bytes 1572872 | tf_op jit(solution)/shard_map/ppermute | solution.py:223
  144.9 28.7 %collective-permute-start.12 = (f32[512,256]{1,0:T(8,128)S(1)}, f32[512,256]{1,0:T(8,128)S(1)}, u32[]{:S(2)}, u32[]{:S(2)}) collective-permute-start(f32[512,256]{1,0:T(8,128)S(1)} %get-tuple-element.12.refs_5_), channel_id=1, source_target_pairs={{0,4},{4,0},{8,12},{12,8},{16,20},{20,16},{24,28},{28,24},{1,5},{5... | collective-permute-start | bytes 1572872 | tf_op jit(solution)/shard_map/ppermute | solution.py:220
  148.0 36.9 %collective-permute-start.13 = (f32[512,256]{1,0:T(8,128)S(1)}, f32[512,256]{1,0:T(8,128)S(1)}, u32[]{:S(2)}, u32[]{:S(2)}) collective-permute-start(f32[512,256]{1,0:T(8,128)S(1)} %get-tuple-element.11.refs_6_), channel_id=1, source_target_pairs={{16,20},{20,16},{24,28},{28,24},{17,21},{21,17},{25,29},{29,25},{1... | collective-permute-start | bytes 1572872 | tf_op jit(solution)/shard_map/ppermute | solution.py:223
  153.9 36.6 %collective-permute-start.8 = (f32[512,128]{1,0:T(8,128)S(1)}, f32[512,128]{1,0:T(8,128)S(1)}, u32[]{:S(2)}, u32[]{:S(2)}) collective-permute-start(f32[512,128]{1,0:T(8,128)S(1)} %get-tuple-element.14.refs_5_), channel_id=1, source_target_pairs={{0,4},{4,0},{8,12},{12,8},{16,20},{20,16},{24,28},{28,24},{1,5},{5... | collective-permute-start | bytes 786440 | tf_op jit(solution)/shard_map/ppermute | solution.py:220
  158.2 37.9 %collective-permute-start.9 = (f32[512,128]{1,0:T(8,128)S(1)}, f32[512,128]{1,0:T(8,128)S(1)}, u32[]{:S(2)}, u32[]{:S(2)}) collective-permute-start(f32[512,128]{1,0:T(8,128)S(1)} %get-tuple-element.13.refs_6_), channel_id=1, source_target_pairs={{16,20},{20,16},{24,28},{28,24},{17,21},{21,17},{25,29},{29,25},{1... | collective-permute-start | bytes 786440 | tf_op jit(solution)/shard_map/ppermute | solution.py:223
  162.4 39.3 %collective-permute-start.3 = (f32[512,128]{1,0:T(8,128)S(1)}, f32[512,128]{1,0:T(8,128)S(1)}, u32[]{:S(2)}, u32[]{:S(2)}) collective-permute-start(f32[512,128]{1,0:T(8,128)S(1)} %get-tuple-element.16.refs_5_), channel_id=1, source_target_pairs={{0,4},{4,0},{8,12},{12,8},{16,20},{20,16},{24,28},{28,24},{1,5},{5... | collective-permute-start | bytes 786440 | tf_op jit(solution)/shard_map/ppermute | solution.py:220
  173.6 32.9 %collective-permute-start.4 = (f32[512,128]{1,0:T(8,128)S(1)}, f32[512,128]{1,0:T(8,128)S(1)}, u32[]{:S(2)}, u32[]{:S(2)}) collective-permute-start(f32[512,128]{1,0:T(8,128)S(1)} %get-tuple-element.15.refs_6_), channel_id=1, source_target_pairs={{16,20},{20,16},{24,28},{28,24},{17,21},{21,17},{25,29},{29,25},{1... | collective-permute-start | bytes 786440 | tf_op jit(solution)/shard_map/ppermute | solution.py:223
  (6 other events, 111.8 us)
where the time goes:
time: 210 us; the launch traced here: 209 us
  waiting for transfers between devices  128 us (61%)
  starting transfers between devices  27 us (13%)
  Pallas kernels  23 us (11%)
  other arithmetic  22.7 us (11%)
  local copies, waits for them, and re-layouts  7.71 us (4%)
    ppermute x15, waiting for transfers between devices, on_device(): far_real = lax.ppermute(real, 'row', everyone)  112 us
    ppermute x5, waiting for transfers between devices, on_device(): far_imag = lax.ppermute(imag, 'row', [(a, a ^ half) for a in complex_at])  16.3 us
    pallas_call x5, Pallas kernels, inner(): pl.pallas_call(functools.partial(inner_kernel, len(blocks) == 4, aliased)...  15.3 us
    ppermute x5, starting transfers between devices, on_device(): far_imag = lax.ppermute(imag, 'row', [(a, a ^ half) for a in complex_at])  14.1 us
    add x5, other arithmetic, on_device(): real, imag = (a_re * real + b_re * far_real, a_im * real + b_im * far_real)  12.8 us
    ppermute x15, starting transfers between devices, on_device(): far_real = lax.ppermute(real, 'row', everyone)  9.6 us
    add x5, other arithmetic, on_device(): real = a_re * real + b_re * far_real  9.14 us
    pallas_call x5, Pallas kernels, stencil(): pl.pallas_call(stencil_kernel, grid=(count,), in_specs=[columns(rows, lef...  7.76 us
  transfers between devices with their start and end apart: 22, of which 17 were waited for; matrix products, arithmetic and copies ran while one was open for 12% of the time, Pallas kernels for 9%

commit v1 on v0

v1 whole, which is shorter than its diff:
```python
import functools
import math

import jax
import jax.numpy as jnp
import numpy as np
from jax import lax
from jax.experimental import pallas as pl
from jax.experimental.pallas import tpu as pltpu
from jax.sharding import PartitionSpec as P

TAPS = 4
LANES = 128
AHEAD = 2
VMEM = 40 * 1024 * 1024
QUICK = pl.CostEstimate(flops=0, bytes_accessed=0, transcendentals=0)


def split_bf16(value):
    high = value.astype(jnp.bfloat16)
    low = (value - high.astype(jnp.float32)).astype(jnp.bfloat16)
    return high, low


def dot3(a, b):
    dot = functools.partial(jnp.dot, preferred_element_type=jnp.float32)
    return dot(a[0], b[0]) + (dot(a[0], b[1]) + dot(a[1], b[0]))


def stencil_kernel(block, per_block, offsets, left, mid, right, apod, coef, fine, *rest):
    out = rest[-1]
    rows = mid.shape[0]
    lane = lax.broadcasted_iota(jnp.int32, (1, LANES), 1)
    start = fine[...]
    if per_block >= LANES:
        start = start + offsets[block * LANES // per_block]
    else:
        for part in range(LANES // per_block):
            value = offsets[block * (LANES // per_block) + part]
            start = start + jnp.where(lane // per_block == part, value, 0)
    shape = (3 * LANES, LANES)
    tap_at = (
        lax.broadcasted_iota(jnp.int32, shape, 0)
        - lax.broadcasted_iota(jnp.int32, shape, 1)
        - LANES
        - start
    )
    band = jnp.zeros(shape, jnp.float32)
    for tap in range(TAPS):
        band = jnp.where(tap_at == tap, coef[tap : tap + 1, :], band)
    field = jnp.concatenate([left[...], mid[...], right[...]], axis=1)
    window = jnp.broadcast_to(apod[...], (LANES, rows)).T
    out[...] = window * dot3(split_bf16(field), split_bf16(band))


def stencil(left, mid, right, apod, coef, fine, offsets, block, after):
    rows, width = mid[0].shape

    def columns(height, at):
        return pl.BlockSpec((height, LANES), lambda i: (0, at))

    return pl.pallas_call(
        functools.partial(stencil_kernel, block, width // offsets.shape[0]),
        grid=(1,),
        in_specs=[pl.BlockSpec(memory_space=pltpu.SMEM)]
        + [columns(rows, at) for _, at in (left, mid, right)]
        + [
            pl.BlockSpec((1, rows), lambda i: (0, 0)),
            columns(TAPS, block),
            columns(1, block),
        ]
        + [pl.BlockSpec(memory_space=pl.ANY)] * len(after),
        out_specs=columns(rows, 0),
        out_shape=jax.ShapeDtypeStruct((rows, LANES), jnp.float32),
        compiler_params=pltpu.CompilerParams(vmem_limit_bytes=VMEM),
        cost_estimate=QUICK,
        name="stencil",
    )(offsets, left[0], mid[0], right[0], apod, coef, fine, *after)


def combine_kernel(me, factors, own, far, *rest):
    out = rest[-1]
    a_re, a_im, b_re, b_im = (factors[me[0], i] for i in range(4))
    if own.shape[0] == 2:
        out[0] = a_re * own[0] - a_im * own[1] + (b_re * far[0] - b_im * far[1])
        out[1] = a_re * own[1] + a_im * own[0] + (b_re * far[1] + b_im * far[0])
    elif out.shape[0] == 2:
        out[0] = a_re * own[0] + b_re * far[0]
        out[1] = a_im * own[0] + b_im * far[0]
    else:
        out[0] = a_re * own[0] + b_re * far[0]


def combine(me, factors, own, far, number, after):
    whole = pl.BlockSpec(memory_space=pltpu.VMEM)
    small = pl.BlockSpec(memory_space=pltpu.SMEM)
    return pl.pallas_call(
        combine_kernel,
        in_specs=[small, small, whole, whole] + [pl.BlockSpec(memory_space=pl.ANY)] * len(after),
        out_specs=whole,
        out_shape=jax.ShapeDtypeStruct((number,) + own.shape[1:], jnp.float32),
        compiler_params=pltpu.CompilerParams(vmem_limit_bytes=VMEM),
        cost_estimate=QUICK,
        name="combine",
    )(me, factors, own, far, *after)


def inner_kernel(me, factors, cos_high, cos_low, sin_high, sin_low, own, far, *rest):
    out, token = rest[-2:]
    a_re, a_im, b_re, b_im = (factors[0, :, i : i + 1] for i in range(4))
    if own.shape[0] == 2:
        y_re = a_re * own[0] - a_im * own[1] + (b_re * far[0] - b_im * far[1])
        y_im = a_re * own[1] + a_im * own[0] + (b_re * far[1] + b_im * far[0])
    else:
        y_re = a_re * own[0] + b_re * far[0]
        y_im = a_im * own[0] + b_im * far[0]
    both = split_bf16(jnp.concatenate([y_re, y_im], axis=1))
    cos_part = dot3((cos_high[...], cos_low[...]), both)
    sin_part = dot3((sin_high[...], sin_low[...]), both)
    out[0] = cos_part[:, :LANES] + sin_part[:, LANES:]
    out[1] = cos_part[:, LANES:] - sin_part[:, :LANES]
    token[...] = jnp.zeros_like(token)


def inner(me, factors, tables, own, far, result, block, full_width, after):
    number, rows, _ = own.shape
    kept = [] if result is None else [result]
    inputs = [me, factors, *tables, own, far, *after, *kept]
    specs = (
        [pl.BlockSpec((1, rows, 4), lambda i, at: (at[0], 0, 0))]
        + [pl.BlockSpec((rows, rows), lambda i, at: (0, 0))] * 4
        + [pl.BlockSpec((number, rows, LANES), lambda i, at: (0, 0, 0))] * 2
        + [pl.BlockSpec(memory_space=pl.ANY)] * (len(after) + len(kept))
    )
    return pl.pallas_call(
        inner_kernel,
        grid_spec=pltpu.PrefetchScalarGridSpec(
            num_scalar_prefetch=1,
            grid=(1,),
            in_specs=specs,
            out_specs=[
                pl.BlockSpec((2, rows, LANES), lambda i, at: (0, 0, block)),
                pl.BlockSpec((8, LANES), lambda i, at: (0, 0)),
            ],
        ),
        out_shape=[
            jax.ShapeDtypeStruct((2, rows, full_width), jnp.float32),
            jax.ShapeDtypeStruct((8, LANES), jnp.float32),
        ],
        input_output_aliases={len(inputs) - 1: 0} if kept else {},
        compiler_params=pltpu.CompilerParams(vmem_limit_bytes=VMEM),
        cost_estimate=QUICK,
        name="inner",
    )(*inputs)


def reversed_bits(value, levels):
    return sum((value >> i & 1) << levels - 1 - i for i in range(levels))


def butterfly_plan(devices):
    stages = []
    phase = np.ones(devices, np.complex128)
    is_real = [True] * devices
    half = devices // 2
    while half:
        own, far = np.zeros(devices, np.complex128), np.zeros(devices, np.complex128)
        next_phase, next_real = phase.copy(), list(is_real)
        for a in range(devices):
            b = a ^ half
            upper = bool(a & half)
            turn = np.exp(-2j * np.pi * (a % half) / (2 * half)) if upper else 1.0
            keep = is_real[a] and phase[a] == 1 and phase[b] == 1
            if keep:
                own[a], far[a] = (-1 if upper else 1), 1
                next_phase[a] = turn
            else:
                own[a] = phase[a] * (-turn if upper else 1)
                far[a] = phase[b] * turn
                next_phase[a], next_real[a] = 1, False
        stages.append((half, own, far, [a for a in range(devices) if not is_real[a]], next_phase))
        phase, is_real = next_phase, next_real
        half //= 2
    return stages


def inner_tables(count, total):
    index = np.arange(count)
    angle = 2 * np.pi / count * (index[:, None] * index[None, :] % count)
    tables = []
    for part in (np.cos(angle), np.sin(angle)):
        part = part / math.sqrt(total)
        high = part.astype(jnp.bfloat16)
        tables += [high, (part - high.astype(np.float64)).astype(jnp.bfloat16)]
    return [jnp.asarray(t) for t in tables]


def parts(*values):
    return np.stack([p for v in values for p in (v.real, v.imag)], -1).astype(np.float32)


def on_device(signal, apod, coef, block_offset, fine_start):
    rows, width = signal.shape
    devices = lax.axis_size("row")
    me = lax.axis_index("row").astype(jnp.int32)[None]
    levels = devices.bit_length() - 1
    total = rows * devices
    count = width // LANES

    neighbours = lax.axis_size("col")
    up = [(i, i + 1) for i in range(neighbours - 1)]
    down = [(j, i) for i, j in up]
    before = lax.ppermute(signal[:, width - LANES :], "col", up)
    behind = lax.ppermute(signal[:, :LANES], "col", down)

    stages = butterfly_plan(devices)
    tables = inner_tables(rows, total)
    outer = np.array([reversed_bits(a, levels) for a in range(devices)])
    twiddle = np.exp(-2j * np.pi / total * (outer[:, None] * np.arange(rows)[None, :] % total))
    factors = [jnp.asarray(parts(own, far)) for _, own, far, _, _ in stages[:-1]]
    _, own, far, _, phase = stages[-1]
    factors.append(
        jnp.asarray(parts((own * phase)[:, None] * twiddle, (far * phase)[:, None] * twiddle))
    )
    numbers = [2 if stages[s + 1][3] else 1 for s in range(levels - 1)]

    order = list(range(1, count - 1)) + [0, count - 1]

    def field_of(chunk, after):
        block = order[chunk]
        left = (before, 0) if block == 0 else (signal, block - 1)
        right = (behind, 0) if block == count - 1 else (signal, block + 1)
        field = stencil(
            left,
            (signal, block),
            right,
            apod[None, :],
            coef,
            fine_start[None, :],
            block_offset,
            block,
            after,
        )
        return field[None]

    def send(value, level):
        half = stages[level][0]
        return lax.ppermute(value, "row", [(a, a ^ half) for a in range(devices)])

    held, coming = {}, {}
    for chunk in range(min(AHEAD, count)):
        held[chunk] = field_of(chunk, [])
        coming[chunk] = send(held[chunk], 0)
    result, last = None, []
    for step in range(count + levels - 1):
        for level in range(levels):
            chunk = step - level
            if not 0 <= chunk < count:
                continue
            own, far = held.pop(chunk), coming.pop(chunk)
            if level < levels - 1:
                held[chunk] = combine(me, factors[level], own, far, numbers[level], last)
                coming[chunk] = send(held[chunk], level + 1)
                last = [held[chunk]]
            else:
                result, token = inner(
                    me, factors[level], tables, own, far, result, order[chunk], width, last
                )
                last = [token]
            if level == 0 and chunk + AHEAD < count:
                new = chunk + AHEAD
                held[new] = field_of(new, last)
                coming[new] = send(held[new], 0)
                last = [held[new]]
    return result


def solution(mesh):
    placed = (P("row", "col"), P("row"), P(None, "col"), P("col"), P("col"))
    return jax.shard_map(
        on_device, mesh=mesh, in_specs=placed, out_specs=P(None, "row", "col"), check_vma=False
    )
```

time: 210 us -> 155 us (0.74)
  the two profiles are of different devices: /device:TPU:26 before, /device:TPU:0 now
where the time goes in v1:
time: 155 us; the launch traced here: 154 us
  waiting for transfers between devices  84.5 us (55%)
  Pallas kernels  36.1 us (23%)
  starting transfers between devices  28.9 us (19%)
  local copies, waits for them, and re-layouts  4.44 us (3%)
    ppermute x24, waiting for transfers between devices, send(): return lax.ppermute(value, 'row', [(a, a ^ half) for a in range(devices)])  84.5 us
    ppermute x24, starting transfers between devices, send(): return lax.ppermute(value, 'row', [(a, a ^ half) for a in range(devices)])  26.1 us
    pallas_call x8, Pallas kernels, inner(): pl.pallas_call(inner_kernel, grid_spec=pltpu.PrefetchScalarGridSpec(num_s...  17.1 us
    pallas_call x16, Pallas kernels, combine(): pl.pallas_call(combine_kernel, in_specs=[small, small, whole, whole] + [p...  10.5 us
    pallas_call x8, Pallas kernels, stencil(): pl.pallas_call(functools.partial(stencil_kernel, block, width // offsets....  8.54 us
    unnamed x34, local copies, waits for them, and re-layouts  4.41 us
  transfers between devices with their start and end apart: 26, of which 15 were waited for; matrix products, arithmetic and copies ran while one was open for 0% of the time, Pallas kernels for 21%

profile of v1, /device:TPU:0, one launch (start us, length us, event | category | flops | bytes accessed | tf_op | source)
XLA Modules:
  0.0 154.4 jit_solution(1884921237191753924)
XLA Ops:
  5.5 4.1 %collective-permute-start.2 = (f32[1,512,128]{2,1,0:T(8,128)S(1)}, f32[1,512,128]{2,1,0:T(8,128)S(1)}, u32[]{:S(2)}, u32[]{:S(2)}) collective-permute-start(f32[1,512,128]{2,1,0:T(8,128)S(1)} %bitcast.31), channel_id=1, source_target_pairs={{0,16},{4,20},{8,24},{12,28},{16,0},{20,4},{24,8},{28,12},{1,17},{... | collective-permute-start | bytes 786440 | tf_op jit(solution)/shard_map/ppermute | solution.py:248
  10.7 17.2 %collective-permute-done.2.far = f32[1,512,128]{2,1,0:T(8,128)S(1)} collective-permute-done((f32[1,512,128]{2,1,0:T(8,128)S(1)}, f32[1,512,128]{2,1,0:T(8,128)S(1)}, u32[]{:S(2)}, u32[]{:S(2)}) %collective-permute-start.2) | collective-permute-done | bytes 262176 | tf_op jit(solution)/shard_map/ppermute | solution.py:248
  29.8 3.0 %collective-permute-done.1.far = f32[1,512,128]{2,1,0:T(8,128)S(1)} collective-permute-done((f32[1,512,128]{2,1,0:T(8,128)S(1)}, f32[1,512,128]{2,1,0:T(8,128)S(1)}, u32[]{:S(2)}, u32[]{:S(2)}) %collective-permute-start.1) | collective-permute-done | bytes 262176 | tf_op jit(solution)/shard_map/ppermute | solution.py:248
  34.6 3.8 %collective-permute-done.4.far = f32[1,512,128]{2,1,0:T(8,128)S(1)} collective-permute-done((f32[1,512,128]{2,1,0:T(8,128)S(1)}, f32[1,512,128]{2,1,0:T(8,128)S(1)}, u32[]{:S(2)}, u32[]{:S(2)}) %collective-permute-start.4) | collective-permute-done | bytes 262176 | tf_op jit(solution)/shard_map/ppermute | solution.py:248
  42.2 2.5 %collective-permute-start.6 = (f32[1,512,128]{2,1,0:T(8,128)S(1)}, f32[1,512,128]{2,1,0:T(8,128)S(1)}, u32[]{:S(2)}, u32[]{:S(2)}) collective-permute-start(f32[1,512,128]{2,1,0:T(8,128)S(1)} %combine.17.rest_0_.own), channel_id=1, source_target_pairs={{0,8},{4,12},{8,0},{12,4},{16,24},{20,28},{24,16},{28,20},{1,9},{5... | collective-permute-start | bytes 786440 | tf_op jit(solution)/shard_map/ppermute | solution.py:248
  44.7 16.2 %collective-permute-done.7.far = f32[1,512,128]{2,1,0:T(8,128)S(1)} collective-permute-done((f32[1,512,128]{2,1,0:T(8,128)S(1)}, f32[1,512,128]{2,1,0:T(8,128)S(1)}, u32[]{:S(2)}, u32[]{:S(2)}) %collective-permute-start.7) | collective-permute-done | bytes 262176 | tf_op jit(solution)/shard_map/ppermute | solution.py:248
  64.1 2.1 %inner.8 = (f32[2,512,1024]{2,1,0:T(8,128)}, f32[8,128]{1,0:T(8,128)S(1)}) custom-call(s32[1]{0:T(128)} %bitcast.me, f32[8,512,4]{2,1,0:T(8,128)S(1)} %copy-done.2, bf16[512,512]{1,0:T(8,128)(2,1)S(1)} %copy-done.3, bf16[512,512]{1,0:T(8,128)(2,1)S(1)} %copy-done.4, bf16[512,512]{1,0:T(8,128)(2,1)S(1)} %copy-done.5, bf16[512,512]{1,0:T(8,128)(2,1)S(1)} %copy-done.6, ...), custom_call_target="tpu_custom_call" | custom-call | tf_op jit(solution)/shard_map/inner/pallas_call | solution.py:135
  76.2 2.1 %inner.9 = (f32[2,512,1024]{2,1,0:T(8,128)}, f32[8,128]{1,0:T(8,128)S(1)}) custom-call(s32[1]{0:T(128)} %bitcast.me, f32[8,512,4]{2,1,0:T(8,128)S(1)} %copy-done.2, bf16[512,512]{1,0:T(8,128)(2,1)S(1)} %copy-done.3, bf16[512,512]{1,0:T(8,128)(2,1)S(1)} %copy-done.4, bf16[512,512]{1,0:T(8,128)(2,1)S(1)} %copy-done.5, ...), custom_call_target="tpu_custom_call", output_to_operand_aliasing={{0}: (9, {})} | custom-call | tf_op jit(solution)/shard_map/inner/pallas_call | solution.py:135
  78.3 2.9 %collective-permute-start.8 = (f32[1,512,128]{2,1,0:T(8,128)S(1)}, f32[1,512,128]{2,1,0:T(8,128)S(1)}, u32[]{:S(2)}, u32[]{:S(2)}) collective-permute-start(f32[1,512,128]{2,1,0:T(8,128)S(1)} %bitcast.12), channel_id=1, source_target_pairs={{0,16},{4,20},{8,24},{12,28},{16,0},{20,4},{24,8},{28,12},{1,17},{... | collective-permute-start | bytes 786440 | tf_op jit(solution)/shard_map/ppermute | solution.py:248
  84.7 2.7 %collective-permute-start.19 = (f32[1,512,128]{2,1,0:T(8,128)S(1)}, f32[1,512,128]{2,1,0:T(8,128)S(1)}, u32[]{:S(2)}, u32[]{:S(2)}) collective-permute-start(f32[1,512,128]{2,1,0:T(8,128)S(1)} %bitcast.18), channel_id=1, source_target_pairs={{0,16},{4,20},{8,24},{12,28},{16,0},{20,4},{24,8},{28,12},{1,17},{... | collective-permute-start | bytes 786440 | tf_op jit(solution)/shard_map/ppermute | solution.py:248
  87.4 2.1 %inner.10 = (f32[2,512,1024]{2,1,0:T(8,128)}, f32[8,128]{1,0:T(8,128)S(1)}) custom-call(s32[1]{0:T(128)} %bitcast.me, f32[8,512,4]{2,1,0:T(8,128)S(1)} %copy-done.2, bf16[512,512]{1,0:T(8,128)(2,1)S(1)} %copy-done.3, bf16[512,512]{1,0:T(8,128)(2,1)S(1)} %copy-done.4, bf16[512,512]{1,0:T(8,128)(2,1)S(1)} %copy-done.5, ...), custom_call_target="tpu_custom_call", output_to_operand_aliasing={{0}: (9, {})} | custom-call | tf_op jit(solution)/shard_map/inner/pallas_call | solution.py:135
  89.5 3.5 %collective-permute-done.8.far = f32[1,512,128]{2,1,0:T(8,128)S(1)} collective-permute-done((f32[1,512,128]{2,1,0:T(8,128)S(1)}, f32[1,512,128]{2,1,0:T(8,128)S(1)}, u32[]{:S(2)}, u32[]{:S(2)}) %collective-permute-start.8) | collective-permute-done | bytes 262176 | tf_op jit(solution)/shard_map/ppermute | solution.py:248
  94.7 4.0 %collective-permute-done.16.far = f32[1,512,128]{2,1,0:T(8,128)S(1)} collective-permute-done((f32[1,512,128]{2,1,0:T(8,128)S(1)}, f32[1,512,128]{2,1,0:T(8,128)S(1)}, u32[]{:S(2)}, u32[]{:S(2)}) %collective-permute-start.16) | collective-permute-done | bytes 262176 | tf_op jit(solution)/shard_map/ppermute | solution.py:248
  99.4 2.5 %collective-permute-start.17 = (f32[2,512,128]{2,1,0:T(8,128)S(1)}, f32[2,512,128]{2,1,0:T(8,128)S(1)}, u32[]{:S(2)}, u32[]{:S(2)}) collective-permute-start(f32[2,512,128]{2,1,0:T(8,128)S(1)} %combine.26.rest_0_.own), channel_id=1, source_target_pairs={{0,4},{4,0},{8,12},{12,8},{16,20},{20,16},{24,28},{28,24},{1,5},{5... | collective-permute-start | bytes 1572872 | tf_op jit(solution)/shard_map/ppermute | solution.py:248
  102.4 2.1 %inner.11 = (f32[2,512,1024]{2,1,0:T(8,128)}, f32[8,128]{1,0:T(8,128)S(1)}) custom-call(s32[1]{0:T(128)} %bitcast.me, f32[8,512,4]{2,1,0:T(8,128)S(1)} %copy-done.2, bf16[512,512]{1,0:T(8,128)(2,1)S(1)} %copy-done.3, bf16[512,512]{1,0:T(8,128)(2,1)S(1)} %copy-done.4, bf16[512,512]{1,0:T(8,128)(2,1)S(1)} %copy-done.5, ...), custom_call_target="tpu_custom_call", output_to_operand_aliasing={{0}: (9, {})} | custom-call | tf_op jit(solution)/shard_map/inner/pallas_call | solution.py:135
  105.2 10.0 %collective-permute-done.18.far = f32[1,512,128]{2,1,0:T(8,128)S(1)} collective-permute-done((f32[1,512,128]{2,1,0:T(8,128)S(1)}, f32[1,512,128]{2,1,0:T(8,128)S(1)}, u32[]{:S(2)}, u32[]{:S(2)}) %collective-permute-start.18) | collective-permute-done | bytes 262176 | tf_op jit(solution)/shard_map/ppermute | solution.py:248
  116.9 2.1 %inner.12 = (f32[2,512,1024]{2,1,0:T(8,128)}, f32[8,128]{1,0:T(8,128)S(1)}) custom-call(s32[1]{0:T(128)} %bitcast.me, f32[8,512,4]{2,1,0:T(8,128)S(1)} %copy-done.2, bf16[512,512]{1,0:T(8,128)(2,1)S(1)} %copy-done.3, bf16[512,512]{1,0:T(8,128)(2,1)S(1)} %copy-done.4, bf16[512,512]{1,0:T(8,128)(2,1)S(1)} %copy-done.5, ...), custom_call_target="tpu_custom_call", output_to_operand_aliasing={{0}: (9, {})} | custom-call | tf_op jit(solution)/shard_map/inner/pallas_call | solution.py:135
  121.8 4.3 %collective-permute-done.23.far = f32[1,512,128]{2,1,0:T(8,128)S(1)} collective-permute-done((f32[1,512,128]{2,1,0:T(8,128)S(1)}, f32[1,512,128]{2,1,0:T(8,128)S(1)}, u32[]{:S(2)}, u32[]{:S(2)}) %collective-permute-start.23) | collective-permute-done | bytes 262176 | tf_op jit(solution)/shard_map/ppermute | solution.py:248
  127.9 2.8 %collective-permute-done.22.far = f32[2,512,128]{2,1,0:T(8,128)S(1)} collective-permute-done((f32[2,512,128]{2,1,0:T(8,128)S(1)}, f32[2,512,128]{2,1,0:T(8,128)S(1)}, u32[]{:S(2)}, u32[]{:S(2)}) %collective-permute-start.22) | collective-permute-done | bytes 524320 | tf_op jit(solution)/shard_map/ppermute | solution.py:248
  130.7 2.1 %inner.13 = (f32[2,512,1024]{2,1,0:T(8,128)}, f32[8,128]{1,0:T(8,128)S(1)}) custom-call(s32[1]{0:T(128)} %bitcast.me, f32[8,512,4]{2,1,0:T(8,128)S(1)} %copy-done.2, bf16[512,512]{1,0:T(8,128)(2,1)S(1)} %copy-done.3, bf16[512,512]{1,0:T(8,128)(2,1)S(1)} %copy-done.4, bf16[512,512]{1,0:T(8,128)(2,1)S(1)} %copy-done.5, ...), custom_call_target="tpu_custom_call", output_to_operand_aliasing={{0}: (9, {})} | custom-call | tf_op jit(solution)/shard_map/inner/pallas_call | solution.py:135
  134.6 7.3 %collective-permute-done.25.far = f32[2,512,128]{2,1,0:T(8,128)S(1)} collective-permute-done((f32[2,512,128]{2,1,0:T(8,128)S(1)}, f32[2,512,128]{2,1,0:T(8,128)S(1)}, u32[]{:S(2)}, u32[]{:S(2)}) %collective-permute-start.25) | collective-permute-done | bytes 524320 | tf_op jit(solution)/shard_map/ppermute | solution.py:248
  141.9 2.1 %inner.14 = (f32[2,512,1024]{2,1,0:T(8,128)}, f32[8,128]{1,0:T(8,128)S(1)}) custom-call(s32[1]{0:T(128)} %bitcast.me, f32[8,512,4]{2,1,0:T(8,128)S(1)} %copy-done.2, bf16[512,512]{1,0:T(8,128)(2,1)S(1)} %copy-done.3, bf16[512,512]{1,0:T(8,128)(2,1)S(1)} %copy-done.4, bf16[512,512]{1,0:T(8,128)(2,1)S(1)} %copy-done.5, ...), custom_call_target="tpu_custom_call", output_to_operand_aliasing={{0}: (9, {})} | custom-call | tf_op jit(solution)/shard_map/inner/pallas_call | solution.py:135
  144.1 8.2 %collective-permute-done.24.far = f32[2,512,128]{2,1,0:T(8,128)S(1)} collective-permute-done((f32[2,512,128]{2,1,0:T(8,128)S(1)}, f32[2,512,128]{2,1,0:T(8,128)S(1)}, u32[]{:S(2)}, u32[]{:S(2)}) %collective-permute-start.24) | collective-permute-done | bytes 524320 | tf_op jit(solution)/shard_map/ppermute | solution.py:248
  152.2 2.1 %inner.15 = (f32[2,512,1024]{2,1,0:T(8,128)}, f32[8,128]{1,0:T(8,128)}) custom-call(s32[1]{0:T(128)} %bitcast.me, f32[8,512,4]{2,1,0:T(8,128)S(1)} %copy-done.2, bf16[512,512]{1,0:T(8,128)(2,1)S(1)} %copy-done.3, bf16[512,512]{1,0:T(8,128)(2,1)S(1)} %copy-done.4, bf16[512,512]{1,0:T(8,128)(2,1)S(1)} %copy-done.5, ...), custom_call_target="tpu_custom_call", output_to_operand_aliasing={{0}: (9, {})} | custom-call | tf_op jit(solution)/shard_map/inner/pallas_call | solution.py:135
  (95 shorter events, 42.0 us)
Async XLA Ops:
  5.5 22.5 %collective-permute-start.2 = (f32[1,512,128]{2,1,0:T(8,128)S(1)}, f32[1,512,128]{2,1,0:T(8,128)S(1)}, u32[]{:S(2)}, u32[]{:S(2)}) collective-permute-start(f32[1,512,128]{2,1,0:T(8,128)S(1)} %bitcast.31), channel_id=1, source_target_pairs={{0,16},{4,20},{8,24},{12,28},{16,0},{20,4},{24,8},{28,12},{1,17},{... | collective-permute-start | bytes 786440 | tf_op jit(solution)/shard_map/ppermute | solution.py:248
  10.7 22.2 %collective-permute-start.1 = (f32[1,512,128]{2,1,0:T(8,128)S(1)}, f32[1,512,128]{2,1,0:T(8,128)S(1)}, u32[]{:S(2)}, u32[]{:S(2)}) collective-permute-start(f32[1,512,128]{2,1,0:T(8,128)S(1)} %bitcast.29), channel_id=1, source_target_pairs={{0,16},{4,20},{8,24},{12,28},{16,0},{20,4},{24,8},{28,12},{1,17},{... | collective-permute-start | bytes 786440 | tf_op jit(solution)/shard_map/ppermute | solution.py:248
  28.6 9.8 %collective-permute-start.4 = (f32[1,512,128]{2,1,0:T(8,128)S(1)}, f32[1,512,128]{2,1,0:T(8,128)S(1)}, u32[]{:S(2)}, u32[]{:S(2)}) collective-permute-start(f32[1,512,128]{2,1,0:T(8,128)S(1)} %combine.16.rest_0_.own), channel_id=1, source_target_pairs={{0,8},{4,12},{8,0},{12,4},{16,24},{20,28},{24,16},{28,20},{1,9},{5... | collective-permute-start | bytes 786440 | tf_op jit(solution)/shard_map/ppermute | solution.py:248
  39.0 25.0 %collective-permute-start.5 = (f32[2,512,128]{2,1,0:T(8,128)S(1)}, f32[2,512,128]{2,1,0:T(8,128)S(1)}, u32[]{:S(2)}, u32[]{:S(2)}) collective-permute-start(f32[2,512,128]{2,1,0:T(8,128)S(1)} %combine.18.rest_0_.own), channel_id=1, source_target_pairs={{0,4},{4,0},{8,12},{12,8},{16,20},{20,16},{24,28},{28,24},{1,5},{5... | collective-permute-start | bytes 1572872 | tf_op jit(solution)/shard_map/ppermute | solution.py:248
  40.6 20.2 %collective-permute-start.7 = (f32[1,512,128]{2,1,0:T(8,128)S(1)}, f32[1,512,128]{2,1,0:T(8,128)S(1)}, u32[]{:S(2)}, u32[]{:S(2)}) collective-permute-start(f32[1,512,128]{2,1,0:T(8,128)S(1)} %bitcast.27), channel_id=1, source_target_pairs={{0,16},{4,20},{8,24},{12,28},{16,0},{20,4},{24,8},{28,12},{1,17},{... | collective-permute-start | bytes 786440 | tf_op jit(solution)/shard_map/ppermute | solution.py:248
  42.2 20.5 %collective-permute-start.6 = (f32[1,512,128]{2,1,0:T(8,128)S(1)}, f32[1,512,128]{2,1,0:T(8,128)S(1)}, u32[]{:S(2)}, u32[]{:S(2)}) collective-permute-start(f32[1,512,128]{2,1,0:T(8,128)S(1)} %combine.17.rest_0_.own), channel_id=1, source_target_pairs={{0,8},{4,12},{8,0},{12,4},{16,24},{20,28},{24,16},{28,20},{1,9},{5... | collective-permute-start | bytes 786440 | tf_op jit(solution)/shard_map/ppermute | solution.py:248
  44.7 23.6 %collective-permute-start.3 = (f32[1,512,128]{2,1,0:T(8,128)S(1)}, f32[1,512,128]{2,1,0:T(8,128)S(1)}, u32[]{:S(2)}, u32[]{:S(2)}) collective-permute-start(f32[1,512,128]{2,1,0:T(8,128)S(1)} %bitcast.24), channel_id=1, source_target_pairs={{0,16},{4,20},{8,24},{12,28},{16,0},{20,4},{24,8},{28,12},{1,17},{... | collective-permute-start | bytes 786440 | tf_op jit(solution)/shard_map/ppermute | solution.py:248
  63.4 11.3 %collective-permute-start.14 = (f32[2,512,128]{2,1,0:T(8,128)S(1)}, f32[2,512,128]{2,1,0:T(8,128)S(1)}, u32[]{:S(2)}, u32[]{:S(2)}) collective-permute-start(f32[2,512,128]{2,1,0:T(8,128)S(1)} %combine.20.rest_0_.own), channel_id=1, source_target_pairs={{0,4},{4,0},{8,12},{12,8},{16,20},{20,16},{24,28},{28,24},{1,5},{5... | collective-permute-start | bytes 1572872 | tf_op jit(solution)/shard_map/ppermute | solution.py:248
  64.1 14.3 %collective-permute-start.13 = (f32[1,512,128]{2,1,0:T(8,128)S(1)}, f32[1,512,128]{2,1,0:T(8,128)S(1)}, u32[]{:S(2)}, u32[]{:S(2)}) collective-permute-start(f32[1,512,128]{2,1,0:T(8,128)S(1)} %bitcast.15), channel_id=1, source_target_pairs={{0,16},{4,20},{8,24},{12,28},{16,0},{20,4},{24,8},{28,12},{1,17},{... | collective-permute-start | bytes 786440 | tf_op jit(solution)/shard_map/ppermute | solution.py:248
  70.9 13.8 %collective-permute-start.10 = (f32[2,512,128]{2,1,0:T(8,128)S(1)}, f32[2,512,128]{2,1,0:T(8,128)S(1)}, u32[]{:S(2)}, u32[]{:S(2)}) collective-permute-start(f32[2,512,128]{2,1,0:T(8,128)S(1)} %combine.22.rest_0_.own), channel_id=1, source_target_pairs={{0,4},{4,0},{8,12},{12,8},{16,20},{20,16},{24,28},{28,24},{1,5},{5... | collective-permute-start | bytes 1572872 | tf_op jit(solution)/shard_map/ppermute | solution.py:248
  71.5 10.3 %collective-permute-start.12 = (f32[512,128]{1,0:T(8,128)S(1)}, f32[512,128]{1,0:T(8,128)S(1)}, u32[]{:S(2)}, u32[]{:S(2)}) collective-permute-start(f32[512,128]{1,0:T(8,128)S(1)} %get-tuple-element.35), channel_id=1, source_target_pairs={{0,1},{1,2},{2,3},{4,5},{5,6},{6,7},{8,9},{9,10},{10,11},{12,13},{... | collective-permute-start | bytes 786440 | tf_op jit(solution)/shard_map/ppermute | solution.py:213
  72.8 11.0 %collective-permute-start.11 = (f32[1,512,128]{2,1,0:T(8,128)S(1)}, f32[1,512,128]{2,1,0:T(8,128)S(1)}, u32[]{:S(2)}, u32[]{:S(2)}) collective-permute-start(f32[1,512,128]{2,1,0:T(8,128)S(1)} %combine.21.rest_0_.own), channel_id=1, source_target_pairs={{0,8},{4,12},{8,0},{12,4},{16,24},{20,28},{24,16},{28,20},{1,9},{5... | collective-permute-start | bytes 786440 | tf_op jit(solution)/shard_map/ppermute | solution.py:248
  74.7 18.9 %collective-permute-start = (f32[512,128]{1,0:T(8,128)S(1)}, f32[512,128]{1,0:T(8,128)S(1)}, u32[]{:S(2)}, u32[]{:S(2)}) collective-permute-start(f32[512,128]{1,0:T(8,128)S(1)} %get-tuple-element.36), channel_id=1, source_target_pairs={{1,0},{2,1},{3,2},{5,4},{6,5},{7,6},{9,8},{10,9},{11,10},{13,12},{... | collective-permute-start | bytes 786440 | tf_op jit(solution)/shard_map/ppermute | solution.py:214
  78.3 14.6 %collective-permute-start.8 = (f32[1,512,128]{2,1,0:T(8,128)S(1)}, f32[1,512,128]{2,1,0:T(8,128)S(1)}, u32[]{:S(2)}, u32[]{:S(2)}) collective-permute-start(f32[1,512,128]{2,1,0:T(8,128)S(1)} %bitcast.12), channel_id=1, source_target_pairs={{0,16},{4,20},{8,24},{12,28},{16,0},{20,4},{24,8},{28,12},{1,17},{... | collective-permute-start | bytes 786440 | tf_op jit(solution)/shard_map/ppermute | solution.py:248
  84.5 17.9 %collective-permute-start.20 = (f32[2,512,128]{2,1,0:T(8,128)S(1)}, f32[2,512,128]{2,1,0:T(8,128)S(1)}, u32[]{:S(2)}, u32[]{:S(2)}) collective-permute-start(f32[2,512,128]{2,1,0:T(8,128)S(1)} %combine.24.rest_0_.own), channel_id=1, source_target_pairs={{0,4},{4,0},{8,12},{12,8},{16,20},{20,16},{24,28},{28,24},{1,5},{5... | collective-permute-start | bytes 1572872 | tf_op jit(solution)/shard_map/ppermute | solution.py:248
  84.7 14.0 %collective-permute-start.16 = (f32[1,512,128]{2,1,0:T(8,128)S(1)}, f32[1,512,128]{2,1,0:T(8,128)S(1)}, u32[]{:S(2)}, u32[]{:S(2)}) collective-permute-start(f32[1,512,128]{2,1,0:T(8,128)S(1)} %combine.23.rest_0_.own), channel_id=1, source_target_pairs={{0,8},{4,12},{8,0},{12,4},{16,24},{20,28},{24,16},{28,20},{1,9},{5... | collective-permute-start | bytes 786440 | tf_op jit(solution)/shard_map/ppermute | solution.py:248
  84.7 19.9 %collective-permute-start.19 = (f32[1,512,128]{2,1,0:T(8,128)S(1)}, f32[1,512,128]{2,1,0:T(8,128)S(1)}, u32[]{:S(2)}, u32[]{:S(2)}) collective-permute-start(f32[1,512,128]{2,1,0:T(8,128)S(1)} %bitcast.18), channel_id=1, source_target_pairs={{0,16},{4,20},{8,24},{12,28},{16,0},{20,4},{24,8},{28,12},{1,17},{... | collective-permute-start | bytes 786440 | tf_op jit(solution)/shard_map/ppermute | solution.py:248
  99.4 17.6 %collective-permute-start.17 = (f32[2,512,128]{2,1,0:T(8,128)S(1)}, f32[2,512,128]{2,1,0:T(8,128)S(1)}, u32[]{:S(2)}, u32[]{:S(2)}) collective-permute-start(f32[2,512,128]{2,1,0:T(8,128)S(1)} %combine.26.rest_0_.own), channel_id=1, source_target_pairs={{0,4},{4,0},{8,12},{12,8},{16,20},{20,16},{24,28},{28,24},{1,5},{5... | collective-permute-start | bytes 1572872 | tf_op jit(solution)/shard_map/ppermute | solution.py:248
  101.8 13.3 %collective-permute-start.18 = (f32[1,512,128]{2,1,0:T(8,128)S(1)}, f32[1,512,128]{2,1,0:T(8,128)S(1)}, u32[]{:S(2)}, u32[]{:S(2)}) collective-permute-start(f32[1,512,128]{2,1,0:T(8,128)S(1)} %combine.25.rest_0_.own), channel_id=1, source_target_pairs={{0,8},{4,12},{8,0},{12,4},{16,24},{20,28},{24,16},{28,20},{1,9},{5... | collective-permute-start | bytes 786440 | tf_op jit(solution)/shard_map/ppermute | solution.py:248
  101.8 17.2 %collective-permute-start.15 = (f32[1,512,128]{2,1,0:T(8,128)S(1)}, f32[1,512,128]{2,1,0:T(8,128)S(1)}, u32[]{:S(2)}, u32[]{:S(2)}) collective-permute-start(f32[1,512,128]{2,1,0:T(8,128)S(1)} %bitcast.21), channel_id=1, source_target_pairs={{0,16},{4,20},{8,24},{12,28},{16,0},{20,4},{24,8},{28,12},{1,17},{... | collective-permute-start | bytes 786440 | tf_op jit(solution)/shard_map/ppermute | solution.py:248
  115.8 14.8 %collective-permute-start.22 = (f32[2,512,128]{2,1,0:T(8,128)S(1)}, f32[2,512,128]{2,1,0:T(8,128)S(1)}, u32[]{:S(2)}, u32[]{:S(2)}) collective-permute-start(f32[2,512,128]{2,1,0:T(8,128)S(1)} %combine.28.rest_0_.own), channel_id=1, source_target_pairs={{0,4},{4,0},{8,12},{12,8},{16,20},{20,16},{24,28},{28,24},{1,5},{5... | collective-permute-start | bytes 1572872 | tf_op jit(solution)/shard_map/ppermute | solution.py:248
  119.7 13.1 %collective-permute-start.21 = (f32[1,512,128]{2,1,0:T(8,128)S(1)}, f32[1,512,128]{2,1,0:T(8,128)S(1)}, u32[]{:S(2)}, u32[]{:S(2)}) collective-permute-start(f32[1,512,128]{2,1,0:T(8,128)S(1)} %combine.29.rest_0_.own), channel_id=1, source_target_pairs={{0,8},{4,12},{8,0},{12,4},{16,24},{20,28},{24,16},{28,20},{1,9},{5... | collective-permute-start | bytes 786440 | tf_op jit(solution)/shard_map/ppermute | solution.py:248
  126.8 15.1 %collective-permute-start.25 = (f32[2,512,128]{2,1,0:T(8,128)S(1)}, f32[2,512,128]{2,1,0:T(8,128)S(1)}, u32[]{:S(2)}, u32[]{:S(2)}) collective-permute-start(f32[2,512,128]{2,1,0:T(8,128)S(1)} %combine.30.rest_0_.own), channel_id=1, source_target_pairs={{0,4},{4,0},{8,12},{12,8},{16,20},{20,16},{24,28},{28,24},{1,5},{5... | collective-permute-start | bytes 1572872 | tf_op jit(solution)/shard_map/ppermute | solution.py:248
  133.5 18.7 %collective-permute-start.24 = (f32[2,512,128]{2,1,0:T(8,128)S(1)}, f32[2,512,128]{2,1,0:T(8,128)S(1)}, u32[]{:S(2)}, u32[]{:S(2)}) collective-permute-start(f32[2,512,128]{2,1,0:T(8,128)S(1)} %combine.31.rest_0_.own), channel_id=1, source_target_pairs={{0,4},{4,0},{8,12},{12,8},{16,20},{20,16},{24,28},{28,24},{1,5},{5... | collective-permute-start | bytes 1572872 | tf_op jit(solution)/shard_map/ppermute | solution.py:248
  (19 other events, 182.1 us)

commit v2 on v1

--- a/solution.py
+++ b/solution.py
@@ -12,6 +12,10 @@
 TAPS = 4
 LANES = 128
 AHEAD = 2
+STENCIL_LATE = True
+ORDER_INNER = None
+SIZES = (1, 1, 1, 1, 1, 1)
+ORDER = {0: [(1, -2)], 1: [(None, -3)], "between": [(0, 3)]}
 VMEM = 40 * 1024 * 1024
 QUICK = pl.CostEstimate(flops=0, bytes_accessed=0, transcendentals=0)
 
@@ -27,9 +31,10 @@
     return dot(a[0], b[0]) + (dot(a[0], b[1]) + dot(a[1], b[0]))
 
 
-def stencil_kernel(block, per_block, offsets, left, mid, right, apod, coef, fine, *rest):
+def stencil_kernel(first, per_block, offsets, left, mid, right, apod, coef, fine, *rest):
     out = rest[-1]
     rows = mid.shape[0]
+    block = first + pl.program_id(0)
     lane = lax.broadcasted_iota(jnp.int32, (1, LANES), 1)
     start = fine[...]
     if per_block >= LANES:
@@ -50,18 +55,18 @@
         band = jnp.where(tap_at == tap, coef[tap : tap + 1, :], band)
     field = jnp.concatenate([left[...], mid[...], right[...]], axis=1)
     window = jnp.broadcast_to(apod[...], (LANES, rows)).T
-    out[...] = window * dot3(split_bf16(field), split_bf16(band))
-
-
-def stencil(left, mid, right, apod, coef, fine, offsets, block, after):
+    out[0] = window * dot3(split_bf16(field), split_bf16(band))
+
+
+def stencil(left, mid, right, apod, coef, fine, offsets, block, count, after):
     rows, width = mid[0].shape
 
     def columns(height, at):
-        return pl.BlockSpec((height, LANES), lambda i: (0, at))
+        return pl.BlockSpec((height, LANES), lambda i: (0, at + i))
 
     return pl.pallas_call(
         functools.partial(stencil_kernel, block, width // offsets.shape[0]),
-        grid=(1,),
+        grid=(count,),
         in_specs=[pl.BlockSpec(memory_space=pltpu.SMEM)]
         + [columns(rows, at) for _, at in (left, mid, right)]
         + [
@@ -70,8 +75,8 @@
             columns(1, block),
         ]
         + [pl.BlockSpec(memory_space=pl.ANY)] * len(after),
-        out_specs=columns(rows, 0),
-        out_shape=jax.ShapeDtypeStruct((rows, LANES), jnp.float32),
+        out_specs=pl.BlockSpec((1, rows, LANES), lambda i: (0, 0, i)),
+        out_shape=jax.ShapeDtypeStruct((1, rows, count * LANES), jnp.float32),
         compiler_params=pltpu.CompilerParams(vmem_limit_bytes=VMEM),
         cost_estimate=QUICK,
         name="stencil",
@@ -82,23 +87,31 @@
     out = rest[-1]
     a_re, a_im, b_re, b_im = (factors[me[0], i] for i in range(4))
     if own.shape[0] == 2:
-        out[0] = a_re * own[0] - a_im * own[1] + (b_re * far[0] - b_im * far[1])
-        out[1] = a_re * own[1] + a_im * own[0] + (b_re * far[1] + b_im * far[0])
+        out[0] = a_re * own[0] - a_im * own[1] + (b_re * far[0, 0] - b_im * far[0, 1])
+        out[1] = a_re * own[1] + a_im * own[0] + (b_re * far[0, 1] + b_im * far[0, 0])
     elif out.shape[0] == 2:
-        out[0] = a_re * own[0] + b_re * far[0]
-        out[1] = a_im * own[0] + b_im * far[0]
+        out[0] = a_re * own[0] + b_re * far[0, 0]
+        out[1] = a_im * own[0] + b_im * far[0, 0]
     else:
-        out[0] = a_re * own[0] + b_re * far[0]
-
-
-def combine(me, factors, own, far, number, after):
-    whole = pl.BlockSpec(memory_space=pltpu.VMEM)
-    small = pl.BlockSpec(memory_space=pltpu.SMEM)
+        out[0] = a_re * own[0] + b_re * far[0, 0]
+
+
+def combine(me, factors, own, far, half, number, after):
+    shape = (number,) + own.shape[1:]
     return pl.pallas_call(
         combine_kernel,
-        in_specs=[small, small, whole, whole] + [pl.BlockSpec(memory_space=pl.ANY)] * len(after),
-        out_specs=whole,
-        out_shape=jax.ShapeDtypeStruct((number,) + own.shape[1:], jnp.float32),
+        grid_spec=pltpu.PrefetchScalarGridSpec(
+            num_scalar_prefetch=1,
+            grid=(1,),
+            in_specs=[
+                pl.BlockSpec(memory_space=pltpu.SMEM),
+                pl.BlockSpec(own.shape, lambda i, at: (0, 0, 0)),
+                pl.BlockSpec((1,) + own.shape, lambda i, at: (1 - at[0] // half % 2, 0, 0, 0)),
+            ]
+            + [pl.BlockSpec(memory_space=pl.ANY)] * len(after),
+            out_specs=pl.BlockSpec(shape, lambda i, at: (0, 0, 0)),
+        ),
+        out_shape=jax.ShapeDtypeStruct(shape, jnp.float32),
         compiler_params=pltpu.CompilerParams(vmem_limit_bytes=VMEM),
         cost_estimate=QUICK,
         name="combine",
@@ -109,11 +122,11 @@
     out, token = rest[-2:]
     a_re, a_im, b_re, b_im = (factors[0, :, i : i + 1] for i in range(4))
     if own.shape[0] == 2:
-        y_re = a_re * own[0] - a_im * own[1] + (b_re * far[0] - b_im * far[1])
-        y_im = a_re * own[1] + a_im * own[0] + (b_re * far[1] + b_im * far[0])
+        y_re = a_re * own[0] - a_im * own[1] + (b_re * far[0, 0] - b_im * far[0, 1])
+        y_im = a_re * own[1] + a_im * own[0] + (b_re * far[0, 1] + b_im * far[0, 0])
     else:
-        y_re = a_re * own[0] + b_re * far[0]
-        y_im = a_im * own[0] + b_im * far[0]
+        y_re = a_re * own[0] + b_re * far[0, 0]
+        y_im = a_im * own[0] + b_im * far[0, 0]
     both = split_bf16(jnp.concatenate([y_re, y_im], axis=1))
     cos_part = dot3((cos_high[...], cos_low[...]), both)
     sin_part = dot3((sin_high[...], sin_low[...]), both)
@@ -123,23 +136,26 @@
 
 
 def inner(me, factors, tables, own, far, result, block, full_width, after):
-    number, rows, _ = own.shape
+    number, rows, width = own.shape
     kept = [] if result is None else [result]
     inputs = [me, factors, *tables, own, far, *after, *kept]
     specs = (
         [pl.BlockSpec((1, rows, 4), lambda i, at: (at[0], 0, 0))]
         + [pl.BlockSpec((rows, rows), lambda i, at: (0, 0))] * 4
-        + [pl.BlockSpec((number, rows, LANES), lambda i, at: (0, 0, 0))] * 2
+        + [
+            pl.BlockSpec((number, rows, LANES), lambda i, at: (0, 0, i)),
+            pl.BlockSpec((1, number, rows, LANES), lambda i, at: (1 - at[0] % 2, 0, 0, i)),
+        ]
         + [pl.BlockSpec(memory_space=pl.ANY)] * (len(after) + len(kept))
     )
     return pl.pallas_call(
         inner_kernel,
         grid_spec=pltpu.PrefetchScalarGridSpec(
             num_scalar_prefetch=1,
-            grid=(1,),
+            grid=(width // LANES,),
             in_specs=specs,
             out_specs=[
-                pl.BlockSpec((2, rows, LANES), lambda i, at: (0, 0, block)),
+                pl.BlockSpec((2, rows, LANES), lambda i, at: (0, 0, block + i)),
                 pl.BlockSpec((8, LANES), lambda i, at: (0, 0)),
             ],
         ),
@@ -152,6 +168,15 @@
         cost_estimate=QUICK,
         name="inner",
     )(*inputs)
+
+
+def column_chunks(count):
+    chunks, at = [], 1
+    while at < count - 1:
+        size = SIZES[min(len(chunks), len(SIZES) - 1)]
+        chunks.append((at, min(size, count - 1 - at)))
+        at += size
+    return chunks + [(0, 1), (count - 1, 1)]
 
 
 def reversed_bits(value, levels):
@@ -224,54 +249,66 @@
     )
     numbers = [2 if stages[s + 1][3] else 1 for s in range(levels - 1)]
 
-    order = list(range(1, count - 1)) + [0, count - 1]
-
-    def field_of(chunk, after):
-        block = order[chunk]
-        left = (before, 0) if block == 0 else (signal, block - 1)
-        right = (behind, 0) if block == count - 1 else (signal, block + 1)
-        field = stencil(
-            left,
-            (signal, block),
-            right,
-            apod[None, :],
-            coef,
-            fine_start[None, :],
-            block_offset,
-            block,
-            after,
-        )
-        return field[None]
+    chunks = column_chunks(count)
 
     def send(value, level):
         half = stages[level][0]
-        return lax.ppermute(value, "row", [(a, a ^ half) for a in range(devices)])
-
-    held, coming = {}, {}
-    for chunk in range(min(AHEAD, count)):
-        held[chunk] = field_of(chunk, [])
-        coming[chunk] = send(held[chunk], 0)
-    result, last = None, []
-    for step in range(count + levels - 1):
-        for level in range(levels):
-            chunk = step - level
-            if not 0 <= chunk < count:
+        pairs = [[a, a ^ half] for a in range(devices) if not a & half]
+        return lax.all_gather(value, "row", axis_index_groups=pairs)
+
+    out, far = {}, {}
+    result = None
+
+    def after(stage, chunk):
+        rules = ORDER.get(stage, ORDER["between"] if 0 < stage < levels else [])
+        wanted = [(levels if s is None else s, chunk + d) for s, d in rules]
+        return [out[w] for w in wanted if w in out]
+
+    for step in range(-AHEAD, len(chunks) + levels):
+        for stage in [*range(1, levels), 0, levels] if STENCIL_LATE else range(levels + 1):
+            chunk = step + AHEAD if stage == 0 else step - stage + 1
+            if not 0 <= chunk < len(chunks):
                 continue
-            own, far = held.pop(chunk), coming.pop(chunk)
-            if level < levels - 1:
-                held[chunk] = combine(me, factors[level], own, far, numbers[level], last)
-                coming[chunk] = send(held[chunk], level + 1)
-                last = [held[chunk]]
+            block, number = chunks[chunk]
+            if stage == 0:
+                left = (before, 0) if block == 0 else (signal, block - 1)
+                right = (behind, 0) if block == count - 1 else (signal, block + 1)
+                out[0, chunk] = stencil(
+                    left,
+                    (signal, block),
+                    right,
+                    apod[None, :],
+                    coef,
+                    fine_start[None, :],
+                    block_offset,
+                    block,
+                    number,
+                    after(0, chunk),
+                )
+            elif stage < levels:
+                out[stage, chunk] = combine(
+                    me,
+                    factors[stage - 1],
+                    out[stage - 1, chunk],
+                    far[stage - 1, chunk],
+                    stages[stage - 1][0],
+                    numbers[stage - 1],
+                    after(stage, chunk),
+                )
             else:
-                result, token = inner(
-                    me, factors[level], tables, own, far, result, order[chunk], width, last
+                result, out[stage, chunk] = inner(
+                    me,
+                    factors[stage - 1],
+                    tables,
+                    out[stage - 1, chunk],
+                    far[stage - 1, chunk],
+                    result,
+                    block,
+                    width,
+                    after(levels, chunk) if ORDER_INNER is None else [],
                 )
-                last = [token]
-            if level == 0 and chunk + AHEAD < count:
-                new = chunk + AHEAD
-                held[new] = field_of(new, last)
-                coming[new] = send(held[new], 0)
-                last = [held[new]]
+            if stage < levels:
+                far[stage, chunk] = send(out[stage, chunk], stage)
     return result
 
 

time: 155 us -> 320 us (2.06)
  blocking collectives: 0 us -> 192 us
  waiting for transfers between devices: 84.5 us -> 12.9 us
  local copies, waits for them, and re-layouts: 4.44 us -> 56.2 us
  starting transfers between devices: 28.9 us -> 2.88 us
  between operations: 0.42 us -> 13.9 us
  Pallas kernels: 36.1 us -> 39.9 us
    all_gather x0 -> x16, blocking collectives: none -> 192 us  [send(): return lax.all_gather(value, 'row', axis_index_groups=pairs)]
    ppermute x24 -> x0, waiting for transfers between devices: 84.5 us -> none  [send(): return lax.ppermute(value, 'row', [(a, a ^ half) for a in range(devices)])]
    unnamed x34 -> x148, local copies, waits for them, and re-layouts: 4.41 us -> 55.4 us
    ppermute x24 -> x0, starting transfers between devices: 26.1 us -> none  [send(): return lax.ppermute(value, 'row', [(a, a ^ half) for a in range(devices)])]
    all_gather x0 -> x8, waiting for transfers between devices: none -> 9.27 us  [send(): return lax.all_gather(value, 'row', axis_index_groups=pairs)]
  transfers between devices with their start and end apart: 26 -> 10, of which waited for: 15 -> 3; matrix products, arithmetic and copies ran while one was open for 0% -> 0% of each run, Pallas kernels for 21% -> 11%
where the time goes in v2:
time: 320 us; the launch traced here: 318 us
  blocking collectives  192 us (60%)
  local copies, waits for them, and re-layouts  56.2 us (18%)
  Pallas kernels  39.9 us (12%)
  between operations  13.9 us (4%)
  waiting for transfers between devices  12.9 us (4%)
    all_gather x16, blocking collectives, send(): return lax.all_gather(value, 'row', axis_index_groups=pairs)  192 us
    unnamed x148, local copies, waits for them, and re-layouts  55.4 us
    pallas_call x8, Pallas kernels, inner(): pl.pallas_call(inner_kernel, grid_spec=pltpu.PrefetchScalarGridSpec(num_s...  19.2 us
    pallas_call x16, Pallas kernels, combine(): pl.pallas_call(combine_kernel, grid_spec=pltpu.PrefetchScalarGridSpec(num...  12.1 us
    all_gather x8, waiting for transfers between devices, send(): return lax.all_gather(value, 'row', axis_index_groups=pairs)  9.27 us
    pallas_call x8, Pallas kernels, stencil(): pl.pallas_call(functools.partial(stencil_kernel, block, width // offsets....  8.55 us
  transfers between devices with their start and end apart: 10, of which 3 were waited for; matrix products, arithmetic and copies ran while one was open for 0% of the time, Pallas kernels for 11%

profile of v2, /device:TPU:0, one launch (start us, length us, event | category | flops | bytes accessed | tf_op | source)
XLA Modules:
  0.0 317.9 jit_solution(3194231207827556569)
XLA Ops:
  12.0 16.6 %all-gather.2 = f32[2,512,128]{2,1,0:T(8,128)S(1)} all-gather(f32[1,512,128]{2,1,0:T(8,128)S(1)} %stencil.10.own), channel_id=4, replica_groups={{0,16},{4,20},{8,24},{12,28},{1,17},{5,21},{9,25},{13,29},{2,18},{6,22}..., dimensions={0}, use_global_device_ids=true | all-gather | bytes 786432 | tf_op jit(solution)/shard_map/all_gather | solution.py:257
  29.3 8.2 %all-gather.3 = f32[2,512,128]{2,1,0:T(8,128)S(1)} all-gather(f32[1,512,128]{2,1,0:T(8,128)S(1)} %combine.17.own.rest_0_), channel_id=5, replica_groups={{0,8},{4,12},{16,24},{20,28},{1,9},{5,13},{17,25},{21,29},{2,10},{6,14}..., dimensions={0}, use_global_device_ids=true | all-gather | bytes 786432 | tf_op jit(solution)/shard_map/all_gather | solution.py:257
  40.1 15.3 %all-gather = f32[2,512,128]{2,1,0:T(8,128)S(1)} all-gather(f32[1,512,128]{2,1,0:T(8,128)S(1)} %stencil.8.own), channel_id=2, replica_groups={{0,16},{4,20},{8,24},{12,28},{1,17},{5,21},{9,25},{13,29},{2,18},{6,22}..., dimensions={0}, use_global_device_ids=true | all-gather | bytes 786432 | tf_op jit(solution)/shard_map/all_gather | solution.py:257
  56.1 8.0 %all-gather.9 = f32[2,512,128]{2,1,0:T(8,128)S(1)} all-gather(f32[1,512,128]{2,1,0:T(8,128)S(1)} %combine.16.rest_0_.own), channel_id=11, replica_groups={{0,8},{4,12},{16,24},{20,28},{1,9},{5,13},{17,25},{21,29},{2,10},{6,14}..., dimensions={0}, use_global_device_ids=true | all-gather | bytes 786432 | tf_op jit(solution)/shard_map/all_gather | solution.py:257
  66.7 15.4 %all-gather.6 = f32[2,512,128]{2,1,0:T(8,128)S(1)} all-gather(f32[1,512,128]{2,1,0:T(8,128)S(1)} %stencil.12.own), channel_id=8, replica_groups={{0,16},{4,20},{8,24},{12,28},{1,17},{5,21},{9,25},{13,29},{2,18},{6,22}..., dimensions={0}, use_global_device_ids=true | all-gather | bytes 786432 | tf_op jit(solution)/shard_map/all_gather | solution.py:257
  82.8 8.0 %all-gather.7 = f32[2,512,128]{2,1,0:T(8,128)S(1)} all-gather(f32[1,512,128]{2,1,0:T(8,128)S(1)} %combine.20.own.rest_0_), channel_id=9, replica_groups={{0,8},{4,12},{16,24},{20,28},{1,9},{5,13},{17,25},{21,29},{2,10},{6,14}..., dimensions={0}, use_global_device_ids=true | all-gather | bytes 786432 | tf_op jit(solution)/shard_map/all_gather | solution.py:257
  93.5 15.5 %all-gather.1 = f32[2,512,128]{2,1,0:T(8,128)} all-gather(f32[1,512,128]{2,1,0:T(8,128)S(1)} %stencil.9.own), channel_id=3, replica_groups={{0,16},{4,20},{8,24},{12,28},{1,17},{5,21},{9,25},{13,29},{2,18},{6,22}..., dimensions={0}, use_global_device_ids=true | all-gather | bytes 786432 | tf_op jit(solution)/shard_map/all_gather | solution.py:257
  114.6 3.2 %inner.8 = (f32[2,512,1024]{2,1,0:T(8,128)}, f32[8,128]{1,0:T(8,128)S(1)}) custom-call(s32[1]{0:T(128)} %bitcast.me, f32[8,512,4]{2,1,0:T(8,128)S(1)} %copy-done.2, bf16[512,512]{1,0:T(8,128)(2,1)S(1)} %copy-done.8, bf16[512,512]{1,0:T(8,128)(2,1)S(1)} %copy-done.9, bf16[512,512]{1,0:T(8,128)(2,1)S(1)} %copy-done.10, bf16[512,512]{1,0:T(8,128)(2,1)S(1)} %copy-done.18, ...), custom_call_target="tpu_custom_call" | custom-call | tf_op jit(solution)/shard_map/inner/pallas_call | solution.py:151
  118.5 8.0 %all-gather.15 = f32[2,512,128]{2,1,0:T(8,128)S(1)} all-gather(f32[1,512,128]{2,1,0:T(8,128)S(1)} %combine.19.rest_0_.own), channel_id=17, replica_groups={{0,8},{4,12},{16,24},{20,28},{1,9},{5,13},{17,25},{21,29},{2,10},{6,14}..., dimensions={0}, use_global_device_ids=true | all-gather | bytes 786432 | tf_op jit(solution)/shard_map/all_gather | solution.py:257
  130.0 15.5 %all-gather.12 = f32[2,512,128]{2,1,0:T(8,128)} all-gather(f32[1,512,128]{2,1,0:T(8,128)S(1)} %stencil.14.own), channel_id=14, replica_groups={{0,16},{4,20},{8,24},{12,28},{1,17},{5,21},{9,25},{13,29},{2,18},{6,22}..., dimensions={0}, use_global_device_ids=true | all-gather | bytes 786432 | tf_op jit(solution)/shard_map/all_gather | solution.py:257
  151.2 3.2 %inner.9 = (f32[2,512,1024]{2,1,0:T(8,128)}, f32[8,128]{1,0:T(8,128)S(1)}) custom-call(s32[1]{0:T(128)} %bitcast.me, f32[8,512,4]{2,1,0:T(8,128)S(1)} %copy-done.3, bf16[512,512]{1,0:T(8,128)(2,1)S(1)} %copy-done.8, bf16[512,512]{1,0:T(8,128)(2,1)S(1)} %copy-done.9, bf16[512,512]{1,0:T(8,128)(2,1)S(1)} %copy-done.11, ...), custom_call_target="tpu_custom_call", output_to_operand_aliasing={{0}: (8, {})} | custom-call | tf_op jit(solution)/shard_map/inner/pallas_call | solution.py:151
  155.1 8.0 %all-gather.13 = f32[2,512,128]{2,1,0:T(8,128)S(1)} all-gather(f32[1,512,128]{2,1,0:T(8,128)S(1)} %combine.24.own.rest_0_), channel_id=15, replica_groups={{0,8},{4,12},{16,24},{20,28},{1,9},{5,13},{17,25},{21,29},{2,10},{6,14}..., dimensions={0}, use_global_device_ids=true | all-gather | bytes 786432 | tf_op jit(solution)/shard_map/all_gather | solution.py:257
  172.4 2.1 inner.10
  174.5 15.4 %all-gather.5 = f32[2,512,128]{2,1,0:T(8,128)S(1)} all-gather(f32[1,512,128]{2,1,0:T(8,128)S(1)} %copy-done.49), channel_id=7, replica_groups={{0,16},{4,20},{8,24},{12,28},{1,17},{5,21},{9,25},{13,29},{2,18},{6,22}..., dimensions={0}, use_global_device_ids=true | all-gather | bytes 786432 | tf_op jit(solution)/shard_map/all_gather | solution.py:257
  190.5 8.0 %all-gather.22 = f32[2,512,128]{2,1,0:T(8,128)S(1)} all-gather(f32[1,512,128]{2,1,0:T(8,128)S(1)} %combine.23.rest_0_.own), channel_id=24, replica_groups={{0,8},{4,12},{16,24},{20,28},{1,9},{5,13},{17,25},{21,29},{2,10},{6,14}..., dimensions={0}, use_global_device_ids=true | all-gather | bytes 786432 | tf_op jit(solution)/shard_map/all_gather | solution.py:257
  205.3 15.5 %all-gather.19 = f32[2,512,128]{2,1,0:T(8,128)} all-gather(f32[1,512,128]{2,1,0:T(8,128)S(1)} %stencil.15.own), channel_id=21, replica_groups={{0,16},{4,20},{8,24},{12,28},{1,17},{5,21},{9,25},{13,29},{2,18},{6,22}..., dimensions={0}, use_global_device_ids=true | all-gather | bytes 786432 | tf_op jit(solution)/shard_map/all_gather | solution.py:257
  230.3 9.7 %all-gather.20 = f32[2,512,128]{2,1,0:T(8,128)S(1)} all-gather(f32[1,512,128]{2,1,0:T(8,128)S(1)} %combine.29.own), channel_id=22, replica_groups={{0,8},{4,12},{16,24},{20,28},{1,9},{5,13},{17,25},{21,29},{2,10},{6,14}..., dimensions={0}, use_global_device_ids=true | all-gather | bytes 786432 | tf_op jit(solution)/shard_map/all_gather | solution.py:257
  242.9 2.3 collective-permute-done.right
  246.3 15.3 %all-gather.11 = f32[2,512,128]{2,1,0:T(8,128)} all-gather(f32[1,512,128]{2,1,0:T(8,128)S(1)} %stencil.13.own), channel_id=13, replica_groups={{0,16},{4,20},{8,24},{12,28},{1,17},{5,21},{9,25},{13,29},{2,18},{6,22}..., dimensions={0}, use_global_device_ids=true | all-gather | bytes 786432 | tf_op jit(solution)/shard_map/all_gather | solution.py:257
  268.3 2.1 inner.12
  271.1 9.7 %all-gather.17 = f32[2,512,128]{2,1,0:T(8,128)S(1)} all-gather(f32[1,512,128]{2,1,0:T(8,128)S(1)} %combine.27.own), channel_id=19, replica_groups={{0,8},{4,12},{16,24},{20,28},{1,9},{5,13},{17,25},{21,29},{2,10},{6,14}..., dimensions={0}, use_global_device_ids=true | all-gather | bytes 786432 | tf_op jit(solution)/shard_map/all_gather | solution.py:257
  293.2 2.1 inner.14
  295.3 9.2 %all-gather.43.cloned.1.call-done = f32[4,512,128]{2,1,0:T(8,128)} async-done(((f32[2,512,128]{2,1,0:T(8,128)}), f32[4,512,128]{2,1,0:T(8,128)}) %all-gather.43.cloned.1.call-update) | async-done | bytes 1048592 | tf_op jit(solution)/shard_map/all_gather | solution.py:257
  308.9 2.1 inner.15
  (201 shorter events, 85.2 us)
Async XLA Ops:
  6.5 22.1 %copy-start.67 = (f32[8,4]{1,0:T(8,128)S(1)}, f32[8,4]{1,0:T(8,128)}, u32[]{:S(2)}) copy-start(f32[8,4]{1,0:T(8,128)} %constant.24.clone.factors) | copy-start | bytes 388
  6.5 103.1 %all-gather.33.cloned.1.call-start = ((), (), s32[]{:S(2)}) async-start(), calls=%async_computation | async-start | bytes 1572864 | tf_op jit(solution)/shard_map/all_gather | solution.py:257
  10.9 26.6 %copy-start.66 = (f32[8,4]{1,0:T(8,128)S(1)}, f32[8,4]{1,0:T(8,128)}, u32[]{:S(2)}) copy-start(f32[8,4]{1,0:T(8,128)} %constant.25.clone.factors) | copy-start | bytes 388
  10.9 28.1 %copy-start.1 = (f32[512,1024]{1,0:T(8,128)S(1)}, f32[512,1024]{1,0:T(8,128)}, u32[]{:S(2)}) copy-start(f32[512,1024]{1,0:T(8,128)} %right.13) | copy-start | bytes 6291460
  10.9 28.1 %copy-start.57 = (f32[4,1024]{1,0:T(4,128)S(1)}, f32[4,1024]{1,0:T(4,128)}, u32[]{:S(2)}) copy-start(f32[4,1024]{1,0:T(4,128)} %coef.15) | copy-start | bytes 49156
  10.9 28.1 %copy-start.69 = (s32[1024]{0:T(1024)S(1)}, s32[1024]{0:T(1024)}, u32[]{:S(2)}) copy-start(s32[1024]{0:T(1024)} %param.16) | copy-start | bytes 12292
  10.9 28.1 %copy-start.71 = (f32[512]{0:T(512)S(1)}, f32[512]{0:T(512)}, u32[]{:S(2)}) copy-start(f32[512]{0:T(512)} %param.13) | copy-start | bytes 6148
  10.9 28.1 %copy-start.73 = (s32[32]{0:T(128)S(1)}, s32[32]{0:T(128)}, u32[]{:S(2)}) copy-start(s32[32]{0:T(128)} %offsets.15) | copy-start | bytes 388
  38.9 107.3 %all-gather.37.cloned.1.call-start = ((), (), s32[]{:S(2)}) async-start(), calls=%async_computation.2 | async-start | bytes 1572864 | tf_op jit(solution)/shard_map/all_gather | solution.py:257
  65.6 100.8 %all-gather.35.cloned.1.call-start = ((), (), s32[]{:S(2)}) async-start(), calls=%async_computation.1 | async-start | bytes 1572864 | tf_op jit(solution)/shard_map/all_gather | solution.py:257
  82.8 8.0 %copy-start.40 = (f32[1,512,128]{2,1,0:T(8,128)}, f32[1,512,128]{2,1,0:T(8,128)S(1)}, u32[]{:S(2)}) copy-start(f32[1,512,128]{2,1,0:T(8,128)S(1)} %combine.20.own.rest_0_) | copy-start | bytes 786436
  92.3 17.4 %copy-start.8 = (bf16[512,512]{1,0:T(8,128)(2,1)S(1)}, bf16[512,512]{1,0:T(8,128)(2,1)}, u32[]{:S(2)}) copy-start(bf16[512,512]{1,0:T(8,128)(2,1)} %constant.20.clone.cos_high) | copy-start | bytes 1572868
  92.3 17.4 %copy-start.9 = (bf16[512,512]{1,0:T(8,128)(2,1)S(1)}, bf16[512,512]{1,0:T(8,128)(2,1)}, u32[]{:S(2)}) copy-start(bf16[512,512]{1,0:T(8,128)(2,1)} %constant.21.clone.cos_low) | copy-start | bytes 1572868
  92.3 129.3 %all-gather.41.cloned.1.call-start = ((), (), s32[]{:S(2)}) async-start(), calls=%async_computation.4 | async-start | bytes 1572864 | tf_op jit(solution)/shard_map/all_gather | solution.py:257
  128.0 134.4 %all-gather.39.cloned.1.call-start = ((), (), s32[]{:S(2)}) async-start(), calls=%async_computation.3 | async-start | bytes 1572864 | tf_op jit(solution)/shard_map/all_gather | solution.py:257
  151.2 3.2 %copy-start.47 = (f32[1,512,128]{2,1,0:T(8,128)S(1)}, f32[1,512,128]{2,1,0:T(8,128)}, u32[]{:S(2)}) copy-start(f32[1,512,128]{2,1,0:T(8,128)} %copy-done.46) | copy-start | bytes 786436
  151.2 3.2 %copy-start.53 = (f32[2,512,128]{2,1,0:T(8,128)S(1)}, f32[2,512,128]{2,1,0:T(8,128)}, u32[]{:S(2)}) copy-start(f32[2,512,128]{2,1,0:T(8,128)} %all-gather.12) | copy-start | bytes 1572868
  155.1 8.0 %copy-start.38 = (f32[1,512,128]{2,1,0:T(8,128)}, f32[1,512,128]{2,1,0:T(8,128)S(1)}, u32[]{:S(2)}) copy-start(f32[1,512,128]{2,1,0:T(8,128)S(1)} %combine.24.own.rest_0_) | copy-start | bytes 786436
  164.6 117.7 %all-gather.47.cloned.1.call-start = ((), (), s32[]{:S(2)}) async-start(), calls=%async_computation.7 | async-start | bytes 1572864 | tf_op jit(solution)/shard_map/all_gather | solution.py:257
  200.1 88.7 %all-gather.45.cloned.1.call-start = ((), (), s32[]{:S(2)}) async-start(), calls=%async_computation.6 | async-start | bytes 1572864 | tf_op jit(solution)/shard_map/all_gather | solution.py:257
  200.9 2.4 collective-permute-start.1
  241.5 63.1 %all-gather.43.cloned.1.call-start = ((), (), s32[]{:S(2)}) async-start(), calls=%async_computation.5 | async-start | bytes 1572864 | tf_op jit(solution)/shard_map/all_gather | solution.py:257
  241.6 3.6 %collective-permute-start = (f32[512,128]{1,0:T(8,128)}, f32[512,128]{1,0:T(8,128)S(1)}, u32[]{:S(2)}, u32[]{:S(2)}) collective-permute-start(f32[512,128]{1,0:T(8,128)} %get-tuple-element.32), channel_id=1, source_target_pairs={{1,0},{2,1},{3,2},{5,4},{6,5},{7,6},{9,8},{10,9},{11,10},{13,12},{... | collective-permute-start | bytes 786440 | tf_op jit(solution)/shard_map/ppermute | solution.py:239
  270.4 11.9 %copy-start.7 = (f32[8,512,4]{2,1,0:T(8,128)S(1)}, f32[8,512,4]{2,1,0:T(8,128)}, u32[]{:S(2)}) copy-start(f32[8,512,4]{2,1,0:T(8,128)} %constant.26.clone.factors) | copy-start | bytes 196612
  (60 other events, 72.6 us)
Sparse Core Ops, SparseCore 0:
  39.0 23.2 all-gather.32
  65.7 23.3 all-gather.36
  92.5 23.3 all-gather.34
  128.1 23.3 all-gather.40
  164.7 23.3 all-gather.38
  200.2 23.3 all-gather.46
  241.7 22.0 all-gather.44
  282.4 22.1 all-gather.42

commit v3 on v1

--- a/solution.py
+++ b/solution.py
@@ -11,7 +11,14 @@
 
 TAPS = 4
 LANES = 128
-AHEAD = 2
+SIZES = (1, 1, 1, 1, 1, 1)
+ORDER = {
+    "stencil": [],
+    "gate": [("arrived", -1)],
+    "first": [("inner", -3), ("middle", -2)],
+    "middle": [("inner", -2)],
+    "inner": [],
+}
 VMEM = 40 * 1024 * 1024
 QUICK = pl.CostEstimate(flops=0, bytes_accessed=0, transcendentals=0)
 
@@ -27,9 +34,10 @@
     return dot(a[0], b[0]) + (dot(a[0], b[1]) + dot(a[1], b[0]))
 
 
-def stencil_kernel(block, per_block, offsets, left, mid, right, apod, coef, fine, *rest):
+def stencil_kernel(first, per_block, offsets, left, mid, right, apod, coef, fine, *rest):
     out = rest[-1]
     rows = mid.shape[0]
+    block = first + pl.program_id(0)
     lane = lax.broadcasted_iota(jnp.int32, (1, LANES), 1)
     start = fine[...]
     if per_block >= LANES:
@@ -50,18 +58,18 @@
         band = jnp.where(tap_at == tap, coef[tap : tap + 1, :], band)
     field = jnp.concatenate([left[...], mid[...], right[...]], axis=1)
     window = jnp.broadcast_to(apod[...], (LANES, rows)).T
-    out[...] = window * dot3(split_bf16(field), split_bf16(band))
-
-
-def stencil(left, mid, right, apod, coef, fine, offsets, block, after):
+    out[0] = window * dot3(split_bf16(field), split_bf16(band))
+
+
+def stencil(left, mid, right, apod, coef, fine, offsets, block, count, after):
     rows, width = mid[0].shape
 
     def columns(height, at):
-        return pl.BlockSpec((height, LANES), lambda i: (0, at))
+        return pl.BlockSpec((height, LANES), lambda i: (0, at + i))
 
     return pl.pallas_call(
         functools.partial(stencil_kernel, block, width // offsets.shape[0]),
-        grid=(1,),
+        grid=(count,),
         in_specs=[pl.BlockSpec(memory_space=pltpu.SMEM)]
         + [columns(rows, at) for _, at in (left, mid, right)]
         + [
@@ -70,12 +78,29 @@
             columns(1, block),
         ]
         + [pl.BlockSpec(memory_space=pl.ANY)] * len(after),
-        out_specs=columns(rows, 0),
-        out_shape=jax.ShapeDtypeStruct((rows, LANES), jnp.float32),
+        out_specs=pl.BlockSpec((1, rows, LANES), lambda i: (0, 0, i)),
+        out_shape=jax.ShapeDtypeStruct((1, rows, count * LANES), jnp.float32),
         compiler_params=pltpu.CompilerParams(vmem_limit_bytes=VMEM),
         cost_estimate=QUICK,
         name="stencil",
     )(offsets, left[0], mid[0], right[0], apod, coef, fine, *after)
+
+
+def gate_kernel(value, *rest):
+    pass
+
+
+def gate(value, after):
+    anywhere = pl.BlockSpec(memory_space=pl.ANY)
+    return pl.pallas_call(
+        gate_kernel,
+        in_specs=[anywhere] * (1 + len(after)),
+        out_specs=anywhere,
+        out_shape=jax.ShapeDtypeStruct(value.shape, value.dtype),
+        input_output_aliases={0: 0},
+        cost_estimate=QUICK,
+        name="gate",
+    )(value, *after)
 
 
 def combine_kernel(me, factors, own, far, *rest):
@@ -123,23 +148,23 @@
 
 
 def inner(me, factors, tables, own, far, result, block, full_width, after):
-    number, rows, _ = own.shape
+    number, rows, width = own.shape
     kept = [] if result is None else [result]
     inputs = [me, factors, *tables, own, far, *after, *kept]
     specs = (
         [pl.BlockSpec((1, rows, 4), lambda i, at: (at[0], 0, 0))]
         + [pl.BlockSpec((rows, rows), lambda i, at: (0, 0))] * 4
-        + [pl.BlockSpec((number, rows, LANES), lambda i, at: (0, 0, 0))] * 2
+        + [pl.BlockSpec((number, rows, LANES), lambda i, at: (0, 0, i))] * 2
         + [pl.BlockSpec(memory_space=pl.ANY)] * (len(after) + len(kept))
     )
     return pl.pallas_call(
         inner_kernel,
         grid_spec=pltpu.PrefetchScalarGridSpec(
             num_scalar_prefetch=1,
-            grid=(1,),
+            grid=(width // LANES,),
             in_specs=specs,
             out_specs=[
-                pl.BlockSpec((2, rows, LANES), lambda i, at: (0, 0, block)),
+                pl.BlockSpec((2, rows, LANES), lambda i, at: (0, 0, block + i)),
                 pl.BlockSpec((8, LANES), lambda i, at: (0, 0)),
             ],
         ),
@@ -152,6 +177,15 @@
         cost_estimate=QUICK,
         name="inner",
     )(*inputs)
+
+
+def column_chunks(count):
+    chunks, at = [], 1
+    while at < count - 1:
+        size = SIZES[min(len(chunks), len(SIZES) - 1)]
+        chunks.append((at, min(size, count - 1 - at)))
+        at += size
+    return chunks + [(0, 1), (count - 1, 1)]
 
 
 def reversed_bits(value, levels):
@@ -224,55 +258,79 @@
     )
     numbers = [2 if stages[s + 1][3] else 1 for s in range(levels - 1)]
 
-    order = list(range(1, count - 1)) + [0, count - 1]
-
-    def field_of(chunk, after):
-        block = order[chunk]
-        left = (before, 0) if block == 0 else (signal, block - 1)
-        right = (behind, 0) if block == count - 1 else (signal, block + 1)
-        field = stencil(
-            left,
-            (signal, block),
-            right,
-            apod[None, :],
-            coef,
-            fine_start[None, :],
-            block_offset,
-            block,
-            after,
-        )
-        return field[None]
+    chunks = column_chunks(count)
 
     def send(value, level):
         half = stages[level][0]
         return lax.ppermute(value, "row", [(a, a ^ half) for a in range(devices)])
 
-    held, coming = {}, {}
-    for chunk in range(min(AHEAD, count)):
-        held[chunk] = field_of(chunk, [])
-        coming[chunk] = send(held[chunk], 0)
-    result, last = None, []
-    for step in range(count + levels - 1):
-        for level in range(levels):
-            chunk = step - level
-            if not 0 <= chunk < count:
-                continue
-            own, far = held.pop(chunk), coming.pop(chunk)
-            if level < levels - 1:
-                held[chunk] = combine(me, factors[level], own, far, numbers[level], last)
-                coming[chunk] = send(held[chunk], level + 1)
-                last = [held[chunk]]
+    out, far, results = {}, {}, {}
+    stage_of = {"stencil": 0, "first": 1, "middle": levels - 1, "inner": levels}
+
+    def after(name, chunk):
+        kept = []
+        for what, shift in ORDER[name]:
+            at = chunk + shift
+            if 0 <= at < len(chunks):
+                if what == "arrived":
+                    make(0, at)
+                    kept.append(far[0, at])
+                else:
+                    make(stage_of[what], at)
+                    kept.append(out[stage_of[what], at])
+        return kept
+
+    def make(stage, chunk):
+        if (stage, chunk) in out:
+            return
+        block, number = chunks[chunk]
+        if stage == 0:
+            left = (before, 0) if block == 0 else (signal, block - 1)
+            right = (behind, 0) if block == count - 1 else (signal, block + 1)
+            out[stage, chunk] = stencil(
+                left,
+                (signal, block),
+                right,
+                apod[None, :],
+                coef,
+                fine_start[None, :],
+                block_offset,
+                block,
+                number,
+                after("stencil", chunk),
+            )
+            waits = after("gate", chunk)
+            if waits:
+                out[stage, chunk] = gate(out[stage, chunk], waits)
+        else:
+            make(stage - 1, chunk)
+            near = (out[stage - 1, chunk], far[stage - 1, chunk])
+            if stage < levels:
+                out[stage, chunk] = combine(
+                    me,
+                    factors[stage - 1],
+                    *near,
+                    numbers[stage - 1],
+                    after("first" if stage == 1 else "middle", chunk),
+                )
             else:
-                result, token = inner(
-                    me, factors[level], tables, own, far, result, order[chunk], width, last
+                if chunk:
+                    make(stage, chunk - 1)
+                results[chunk], out[stage, chunk] = inner(
+                    me,
+                    factors[stage - 1],
+                    tables,
+                    *near,
+                    results.get(chunk - 1),
+                    block,
+                    width,
+                    after("inner", chunk),
                 )
-                last = [token]
-            if level == 0 and chunk + AHEAD < count:
-                new = chunk + AHEAD
-                held[new] = field_of(new, last)
-                coming[new] = send(held[new], 0)
-                last = [held[new]]
-    return result
+        if stage < levels:
+            far[stage, chunk] = send(out[stage, chunk], stage)
+
+    make(levels, len(chunks) - 1)
+    return results[len(chunks) - 1]
 
 
 def solution(mesh):

time: 155 us -> 168 us (1.084)
  waiting for transfers between devices: 84.5 us -> 55.6 us
  Pallas kernels: 36.1 us -> 55.7 us
  local copies, waits for them, and re-layouts: 4.44 us -> 23.9 us
  starting transfers between devices: 28.9 us -> 31.1 us
    ppermute x24, waiting for transfers between devices: 84.5 us -> 55.6 us  [send(): return lax.ppermute(value, 'row', [(a, a ^ half) for a in range(devices)])]
    unnamed x34 -> x102, local copies, waits for them, and re-layouts: 4.41 us -> 23 us
    pallas_call x16, Pallas kernels: 10.5 us -> 21.7 us  [combine(): pl.pallas_call(combine_kernel, in_specs=[small, small, whole, whole] + [p...]
    pallas_call x8, Pallas kernels: 17.1 us -> 24.6 us  [inner(): pl.pallas_call(inner_kernel, grid_spec=pltpu.PrefetchScalarGridSpec(num_s...]
  transfers between devices with their start and end apart: 26 -> 26, of which waited for: 15 -> 13; matrix products, arithmetic and copies ran while one was open for 0% -> 1% of each run, Pallas kernels for 21% -> 32%
where the time goes in v3:
time: 168 us; the launch traced here: 167 us
  Pallas kernels  55.7 us (33%)
  waiting for transfers between devices  55.6 us (33%)
  starting transfers between devices  31.1 us (19%)
  local copies, waits for them, and re-layouts  23.9 us (14%)
    ppermute x24, waiting for transfers between devices, send(): return lax.ppermute(value, 'row', [(a, a ^ half) for a in range(devices)])  55.6 us
    ppermute x24, starting transfers between devices, send(): return lax.ppermute(value, 'row', [(a, a ^ half) for a in range(devices)])  27.7 us
    pallas_call x8, Pallas kernels, inner(): pl.pallas_call(inner_kernel, grid_spec=pltpu.PrefetchScalarGridSpec(num_s...  24.6 us
    unnamed x102, local copies, waits for them, and re-layouts  23 us
    pallas_call x16, Pallas kernels, combine(): pl.pallas_call(combine_kernel, in_specs=[small, small, whole, whole] + [p...  21.7 us
    pallas_call x8, Pallas kernels, stencil(): pl.pallas_call(functools.partial(stencil_kernel, block, width // offsets....  9.43 us
  transfers between devices with their start and end apart: 26, of which 13 were waited for; matrix products, arithmetic and copies ran while one was open for 1% of the time, Pallas kernels for 32%

profile of v3, /device:TPU:0, one launch (start us, length us, event | category | flops | bytes accessed | tf_op | source)
XLA Modules:
  0.0 166.7 jit_solution(10379755045475378370)
XLA Ops:
  5.5 4.1 %collective-permute-start.2 = (f32[1,512,128]{2,1,0:T(8,128)S(1)}, f32[1,512,128]{2,1,0:T(8,128)S(1)}, u32[]{:S(2)}, u32[]{:S(2)}) collective-permute-start(f32[1,512,128]{2,1,0:T(8,128)S(1)} %stencil.15.own), channel_id=1, source_target_pairs={{0,16},{4,20},{8,24},{12,28},{16,0},{20,4},{24,8},{28,12},{1,17},{... | collective-permute-start | bytes 786440 | tf_op jit(solution)/shard_map/ppermute | solution.py:265
  11.3 10.1 %collective-permute-done.2.rest_0_.far = f32[1,512,128]{2,1,0:T(8,128)S(1)} collective-permute-done((f32[1,512,128]{2,1,0:T(8,128)S(1)}, f32[1,512,128]{2,1,0:T(8,128)S(1)}, u32[]{:S(2)}, u32[]{:S(2)}) %collective-permute-start.2) | collective-permute-done | bytes 262176 | tf_op jit(solution)/shard_map/ppermute | solution.py:265
  23.8 4.2 %collective-permute-start.12 = (f32[1,512,128]{2,1,0:T(8,128)S(1)}, f32[1,512,128]{2,1,0:T(8,128)S(1)}, u32[]{:S(2)}, u32[]{:S(2)}) collective-permute-start(f32[1,512,128]{2,1,0:T(8,128)S(1)} %combine.18.own), channel_id=1, source_target_pairs={{0,8},{4,12},{8,0},{12,4},{16,24},{20,28},{24,16},{28,20},{1,9},{5... | collective-permute-start | bytes 786440 | tf_op jit(solution)/shard_map/ppermute | solution.py:265
  29.8 6.8 %collective-permute-done.3.rest_0_.far = f32[1,512,128]{2,1,0:T(8,128)} collective-permute-done((f32[1,512,128]{2,1,0:T(8,128)}, f32[1,512,128]{2,1,0:T(8,128)}, u32[]{:S(2)}, u32[]{:S(2)}) %collective-permute-start.3) | collective-permute-done | bytes 262176 | tf_op jit(solution)/shard_map/ppermute | solution.py:265
  47.2 2.9 %collective-permute-done.4.rest_0_.far = f32[1,512,128]{2,1,0:T(8,128)} collective-permute-done((f32[1,512,128]{2,1,0:T(8,128)}, f32[1,512,128]{2,1,0:T(8,128)}, u32[]{:S(2)}, u32[]{:S(2)}) %collective-permute-start.4) | collective-permute-done | bytes 262176 | tf_op jit(solution)/shard_map/ppermute | solution.py:265
  53.5 3.4 %collective-permute-done.10.far = f32[1,512,128]{2,1,0:T(8,128)S(1)} collective-permute-done((f32[1,512,128]{2,1,0:T(8,128)}, f32[1,512,128]{2,1,0:T(8,128)S(1)}, u32[]{:S(2)}, u32[]{:S(2)}) %collective-permute-start.10) | collective-permute-done | bytes 262176 | tf_op jit(solution)/shard_map/ppermute | solution.py:265
  61.2 3.2 %collective-permute-done.5.rest_0_.far = f32[1,512,128]{2,1,0:T(8,128)} collective-permute-done((f32[1,512,128]{2,1,0:T(8,128)}, f32[1,512,128]{2,1,0:T(8,128)}, u32[]{:S(2)}, u32[]{:S(2)}) %collective-permute-start.5) | collective-permute-done | bytes 262176 | tf_op jit(solution)/shard_map/ppermute | solution.py:265
  68.1 3.3 %inner.8 = (f32[2,512,1024]{2,1,0:T(8,128)}, f32[8,128]{1,0:T(8,128)S(1)}) custom-call(s32[1]{0:T(128)} %bitcast.me, f32[8,512,4]{2,1,0:T(8,128)S(1)} %copy-done.2, bf16[512,512]{1,0:T(8,128)(2,1)S(1)} %copy-done.7, bf16[512,512]{1,0:T(8,128)(2,1)S(1)} %copy-done.8, bf16[512,512]{1,0:T(8,128)(2,1)S(1)} %copy-done.9, bf16[512,512]{1,0:T(8,128)(2,1)S(1)} %copy-done.15, ...), custom_call_target="tpu_custom_call" | custom-call | tf_op jit(solution)/shard_map/inner/pallas_call | solution.py:160
  75.8 2.5 %collective-permute-start.18 = (f32[1,512,128]{2,1,0:T(8,128)}, f32[1,512,128]{2,1,0:T(8,128)}, u32[]{:S(2)}, u32[]{:S(2)}) collective-permute-start(f32[1,512,128]{2,1,0:T(8,128)} %combine.24.own), channel_id=1, source_target_pairs={{0,8},{4,12},{8,0},{12,4},{16,24},{20,28},{24,16},{28,20},{1,9},{5... | collective-permute-start | bytes 786440 | tf_op jit(solution)/shard_map/ppermute | solution.py:265
  87.0 3.4 %inner.9 = (f32[2,512,1024]{2,1,0:T(8,128)}, f32[8,128]{1,0:T(8,128)S(1)}) custom-call(s32[1]{0:T(128)} %bitcast.me, f32[8,512,4]{2,1,0:T(8,128)S(1)} %copy-done.3, bf16[512,512]{1,0:T(8,128)(2,1)S(1)} %copy-done.7, bf16[512,512]{1,0:T(8,128)(2,1)S(1)} %copy-done.8, bf16[512,512]{1,0:T(8,128)(2,1)S(1)} %copy-done.10, ...), custom_call_target="tpu_custom_call", output_to_operand_aliasing={{0}: (8, {})} | custom-call | tf_op jit(solution)/shard_map/inner/pallas_call | solution.py:160
  90.4 2.1 %combine.25.own.rest_1_ = f32[2,512,128]{2,1,0:T(8,128)} custom-call(s32[1]{0:T(128)} %bitcast.me, f32[8,4]{1,0:T(8,128)S(1)} %copy-done.41, f32[1,512,128]{2,1,0:T(8,128)} %combine.24.own, f32[1,512,128]{2,1,0:T(8,128)} %collective-permute-done.18.far, f32[8,128]{1,0:T(8,128)S(1)} %get-tuple-element.20.rest_0_), custom_call_target="tpu_custom_call" | custom-call | tf_op jit(solution)/shard_map/combine/pallas_call | solution.py:122
  100.5 3.4 %inner.10 = (f32[2,512,1024]{2,1,0:T(8,128)}, f32[8,128]{1,0:T(8,128)S(1)}) custom-call(s32[1]{0:T(128)} %bitcast.me, f32[8,512,4]{2,1,0:T(8,128)S(1)} %copy-done.4, bf16[512,512]{1,0:T(8,128)(2,1)S(1)} %copy-done.7, bf16[512,512]{1,0:T(8,128)(2,1)S(1)} %copy-done.8, bf16[512,512]{1,0:T(8,128)(2,1)S(1)} %copy-done.11, ...), custom_call_target="tpu_custom_call", output_to_operand_aliasing={{0}: (8, {})} | custom-call | tf_op jit(solution)/shard_map/inner/pallas_call | solution.py:160
  107.5 2.5 %collective-permute-start.8 = (f32[1,512,128]{2,1,0:T(8,128)}, f32[1,512,128]{2,1,0:T(8,128)}, u32[]{:S(2)}, u32[]{:S(2)}) collective-permute-start(f32[1,512,128]{2,1,0:T(8,128)} %gate.12.own), channel_id=1, source_target_pairs={{0,16},{4,20},{8,24},{12,28},{16,0},{20,4},{24,8},{28,12},{1,17},{... | collective-permute-start | bytes 786440 | tf_op jit(solution)/shard_map/ppermute | solution.py:265
  112.3 3.5 %inner.11 = (f32[2,512,1024]{2,1,0:T(8,128)}, f32[8,128]{1,0:T(8,128)S(1)}) custom-call(s32[1]{0:T(128)} %bitcast.me, f32[8,512,4]{2,1,0:T(8,128)S(1)} %copy-done.5, bf16[512,512]{1,0:T(8,128)(2,1)S(1)} %copy-done.7, bf16[512,512]{1,0:T(8,128)(2,1)S(1)} %copy-done.8, bf16[512,512]{1,0:T(8,128)(2,1)S(1)} %copy-done.12, ...), custom_call_target="tpu_custom_call", output_to_operand_aliasing={{0}: (8, {})} | custom-call | tf_op jit(solution)/shard_map/inner/pallas_call | solution.py:160
  119.1 4.4 %collective-permute-done.8.rest_0_.far = f32[1,512,128]{2,1,0:T(8,128)} collective-permute-done((f32[1,512,128]{2,1,0:T(8,128)}, f32[1,512,128]{2,1,0:T(8,128)}, u32[]{:S(2)}, u32[]{:S(2)}) %collective-permute-start.8) | collective-permute-done | bytes 262176 | tf_op jit(solution)/shard_map/ppermute | solution.py:265
  124.6 2.6 %collective-permute-start.24 = (f32[1,512,128]{2,1,0:T(8,128)S(1)}, f32[1,512,128]{2,1,0:T(8,128)S(1)}, u32[]{:S(2)}, u32[]{:S(2)}) collective-permute-start(f32[1,512,128]{2,1,0:T(8,128)S(1)} %combine.30.own), channel_id=1, source_target_pairs={{0,8},{4,12},{8,0},{12,4},{16,24},{20,28},{24,16},{28,20},{1,9},{5... | collective-permute-start | bytes 786440 | tf_op jit(solution)/shard_map/ppermute | solution.py:265
  129.3 3.4 %inner.12 = (f32[2,512,1024]{2,1,0:T(8,128)}, f32[8,128]{1,0:T(8,128)S(1)}) custom-call(s32[1]{0:T(128)} %bitcast.me, f32[8,512,4]{2,1,0:T(8,128)S(1)} %copy-done.6, bf16[512,512]{1,0:T(8,128)(2,1)S(1)} %copy-done.7, bf16[512,512]{1,0:T(8,128)(2,1)S(1)} %copy-done.8, bf16[512,512]{1,0:T(8,128)(2,1)S(1)} %copy-done.13, ...), custom_call_target="tpu_custom_call", output_to_operand_aliasing={{0}: (8, {})} | custom-call | tf_op jit(solution)/shard_map/inner/pallas_call | solution.py:160
  132.7 5.4 %collective-permute-done.9.far = f32[1,512,128]{2,1,0:T(8,128)S(1)} collective-permute-done((f32[1,512,128]{2,1,0:T(8,128)}, f32[1,512,128]{2,1,0:T(8,128)S(1)}, u32[]{:S(2)}, u32[]{:S(2)}) %collective-permute-start.9) | collective-permute-done | bytes 262176 | tf_op jit(solution)/shard_map/ppermute | solution.py:265
  140.8 3.3 %inner.13 = (f32[2,512,1024]{2,1,0:T(8,128)}, f32[8,128]{1,0:T(8,128)S(1)}) custom-call(s32[1]{0:T(128)} %bitcast.me, f32[8,512,4]{2,1,0:T(8,128)S(1)} %copy-done.6, bf16[512,512]{1,0:T(8,128)(2,1)S(1)} %copy-done.7, bf16[512,512]{1,0:T(8,128)(2,1)S(1)} %copy-done.8, bf16[512,512]{1,0:T(8,128)(2,1)S(1)} %copy-done.14, ...), custom_call_target="tpu_custom_call", output_to_operand_aliasing={{0}: (8, {})} | custom-call | tf_op jit(solution)/shard_map/inner/pallas_call | solution.py:160
  144.1 2.8 %collective-permute-done.21.far = f32[1,512,128]{2,1,0:T(8,128)S(1)} collective-permute-done((f32[1,512,128]{2,1,0:T(8,128)S(1)}, f32[1,512,128]{2,1,0:T(8,128)S(1)}, u32[]{:S(2)}, u32[]{:S(2)}) %collective-permute-start.21) | collective-permute-done | bytes 262176 | tf_op jit(solution)/shard_map/ppermute | solution.py:265
  148.7 6.0 %collective-permute-done.25.far = f32[2,512,128]{2,1,0:T(8,128)S(1)} collective-permute-done((f32[2,512,128]{2,1,0:T(8,128)S(1)}, f32[2,512,128]{2,1,0:T(8,128)S(1)}, u32[]{:S(2)}, u32[]{:S(2)}) %collective-permute-start.25) | collective-permute-done | bytes 524320 | tf_op jit(solution)/shard_map/ppermute | solution.py:265
  154.6 2.1 %inner.14 = (f32[2,512,1024]{2,1,0:T(8,128)}, f32[8,128]{1,0:T(8,128)}) custom-call(s32[1]{0:T(128)} %bitcast.me, f32[8,512,4]{2,1,0:T(8,128)S(1)} %copy-done.6, bf16[512,512]{1,0:T(8,128)(2,1)S(1)} %copy-done.7, bf16[512,512]{1,0:T(8,128)(2,1)S(1)} %copy-done.8, bf16[512,512]{1,0:T(8,128)(2,1)S(1)} %copy-done.14, ...), custom_call_target="tpu_custom_call", output_to_operand_aliasing={{0}: (8, {})} | custom-call | tf_op jit(solution)/shard_map/inner/pallas_call | solution.py:160
  156.8 7.8 %collective-permute-done.23.far = f32[2,512,128]{2,1,0:T(8,128)S(1)} collective-permute-done((f32[2,512,128]{2,1,0:T(8,128)S(1)}, f32[2,512,128]{2,1,0:T(8,128)S(1)}, u32[]{:S(2)}, u32[]{:S(2)}) %collective-permute-start.23) | collective-permute-done | bytes 524320 | tf_op jit(solution)/shard_map/ppermute | solution.py:265
  164.6 2.1 %inner.15 = (f32[2,512,1024]{2,1,0:T(8,128)}, f32[8,128]{1,0:T(8,128)}) custom-call(s32[1]{0:T(128)} %bitcast.me, f32[8,512,4]{2,1,0:T(8,128)S(1)} %copy-done.6, bf16[512,512]{1,0:T(8,128)(2,1)S(1)} %copy-done.7, bf16[512,512]{1,0:T(8,128)(2,1)S(1)} %copy-done.8, bf16[512,512]{1,0:T(8,128)(2,1)S(1)} %copy-done.14, ...), custom_call_target="tpu_custom_call", output_to_operand_aliasing={{0}: (8, {})} | custom-call | tf_op jit(solution)/shard_map/inner/pallas_call | solution.py:160
  (170 shorter events, 71.0 us)
Async XLA Ops:
  5.5 16.0 %collective-permute-start.2 = (f32[1,512,128]{2,1,0:T(8,128)S(1)}, f32[1,512,128]{2,1,0:T(8,128)S(1)}, u32[]{:S(2)}, u32[]{:S(2)}) collective-permute-start(f32[1,512,128]{2,1,0:T(8,128)S(1)} %stencil.15.own), channel_id=1, source_target_pairs={{0,16},{4,20},{8,24},{12,28},{16,0},{20,4},{24,8},{28,12},{1,17},{... | collective-permute-start | bytes 786440 | tf_op jit(solution)/shard_map/ppermute | solution.py:265
  22.2 14.4 %collective-permute-start.3 = (f32[1,512,128]{2,1,0:T(8,128)}, f32[1,512,128]{2,1,0:T(8,128)}, u32[]{:S(2)}, u32[]{:S(2)}) collective-permute-start(f32[1,512,128]{2,1,0:T(8,128)} %gate.7.own), channel_id=1, source_target_pairs={{0,16},{4,20},{8,24},{12,28},{16,0},{20,4},{24,8},{28,12},{1,17},{... | collective-permute-start | bytes 786440 | tf_op jit(solution)/shard_map/ppermute | solution.py:265
  23.8 14.2 %collective-permute-start.12 = (f32[1,512,128]{2,1,0:T(8,128)S(1)}, f32[1,512,128]{2,1,0:T(8,128)S(1)}, u32[]{:S(2)}, u32[]{:S(2)}) collective-permute-start(f32[1,512,128]{2,1,0:T(8,128)S(1)} %combine.18.own), channel_id=1, source_target_pairs={{0,8},{4,12},{8,0},{12,4},{16,24},{20,28},{24,16},{28,20},{1,9},{5... | collective-permute-start | bytes 786440 | tf_op jit(solution)/shard_map/ppermute | solution.py:265
  36.6 13.5 %collective-permute-start.4 = (f32[1,512,128]{2,1,0:T(8,128)}, f32[1,512,128]{2,1,0:T(8,128)}, u32[]{:S(2)}, u32[]{:S(2)}) collective-permute-start(f32[1,512,128]{2,1,0:T(8,128)} %gate.8.own), channel_id=1, source_target_pairs={{0,16},{4,20},{8,24},{12,28},{16,0},{20,4},{24,8},{28,12},{1,17},{... | collective-permute-start | bytes 786440 | tf_op jit(solution)/shard_map/ppermute | solution.py:265
  42.2 22.2 %collective-permute-start.13 = (f32[2,512,128]{2,1,0:T(8,128)}, f32[2,512,128]{2,1,0:T(8,128)}, u32[]{:S(2)}, u32[]{:S(2)}) collective-permute-start(f32[2,512,128]{2,1,0:T(8,128)} %combine.19.own.rest_0_), channel_id=1, source_target_pairs={{0,4},{4,0},{8,12},{12,8},{16,20},{20,16},{24,28},{28,24},{1,5},{5... | collective-permute-start | bytes 1572872 | tf_op jit(solution)/shard_map/ppermute | solution.py:265
  45.1 11.8 %collective-permute-start.10 = (f32[1,512,128]{2,1,0:T(8,128)}, f32[1,512,128]{2,1,0:T(8,128)S(1)}, u32[]{:S(2)}, u32[]{:S(2)}) collective-permute-start(f32[1,512,128]{2,1,0:T(8,128)} %combine.16.own), channel_id=1, source_target_pairs={{0,8},{4,12},{8,0},{12,4},{16,24},{20,28},{24,16},{28,20},{1,9},{5... | collective-permute-start | bytes 786440 | tf_op jit(solution)/shard_map/ppermute | solution.py:265
  50.1 14.3 %collective-permute-start.5 = (f32[1,512,128]{2,1,0:T(8,128)}, f32[1,512,128]{2,1,0:T(8,128)}, u32[]{:S(2)}, u32[]{:S(2)}) collective-permute-start(f32[1,512,128]{2,1,0:T(8,128)} %gate.9.own), channel_id=1, source_target_pairs={{0,16},{4,20},{8,24},{12,28},{16,0},{20,4},{24,8},{28,12},{1,17},{... | collective-permute-start | bytes 786440 | tf_op jit(solution)/shard_map/ppermute | solution.py:265
  52.6 18.8 %collective-permute-start.14 = (f32[1,512,128]{2,1,0:T(8,128)}, f32[1,512,128]{2,1,0:T(8,128)}, u32[]{:S(2)}, u32[]{:S(2)}) collective-permute-start(f32[1,512,128]{2,1,0:T(8,128)} %combine.20.own), channel_id=1, source_target_pairs={{0,8},{4,12},{8,0},{12,4},{16,24},{20,28},{24,16},{28,20},{1,9},{5... | collective-permute-start | bytes 786440 | tf_op jit(solution)/shard_map/ppermute | solution.py:265
  58.7 24.6 %collective-permute-start.11 = (f32[2,512,128]{2,1,0:T(8,128)}, f32[2,512,128]{2,1,0:T(8,128)}, u32[]{:S(2)}, u32[]{:S(2)}) collective-permute-start(f32[2,512,128]{2,1,0:T(8,128)} %combine.17.own.rest_1_), channel_id=1, source_target_pairs={{0,4},{4,0},{8,12},{12,8},{16,20},{20,16},{24,28},{28,24},{1,5},{5... | collective-permute-start | bytes 1572872 | tf_op jit(solution)/shard_map/ppermute | solution.py:265
  64.4 18.5 %collective-permute-start.6 = (f32[1,512,128]{2,1,0:T(8,128)}, f32[1,512,128]{2,1,0:T(8,128)}, u32[]{:S(2)}, u32[]{:S(2)}) collective-permute-start(f32[1,512,128]{2,1,0:T(8,128)} %gate.10.own), channel_id=1, source_target_pairs={{0,16},{4,20},{8,24},{12,28},{16,0},{20,4},{24,8},{28,12},{1,17},{... | collective-permute-start | bytes 786440 | tf_op jit(solution)/shard_map/ppermute | solution.py:265
  73.3 27.2 %collective-permute-start.16 = (f32[2,512,128]{2,1,0:T(8,128)}, f32[2,512,128]{2,1,0:T(8,128)}, u32[]{:S(2)}, u32[]{:S(2)}) collective-permute-start(f32[2,512,128]{2,1,0:T(8,128)} %combine.21.rest_1_.own), channel_id=1, source_target_pairs={{0,4},{4,0},{8,12},{12,8},{16,20},{20,16},{24,28},{28,24},{1,5},{5... | collective-permute-start | bytes 1572872 | tf_op jit(solution)/shard_map/ppermute | solution.py:265
  75.8 14.6 %collective-permute-start.18 = (f32[1,512,128]{2,1,0:T(8,128)}, f32[1,512,128]{2,1,0:T(8,128)}, u32[]{:S(2)}, u32[]{:S(2)}) collective-permute-start(f32[1,512,128]{2,1,0:T(8,128)} %combine.24.own), channel_id=1, source_target_pairs={{0,8},{4,12},{8,0},{12,4},{16,24},{20,28},{24,16},{28,20},{1,9},{5... | collective-permute-start | bytes 786440 | tf_op jit(solution)/shard_map/ppermute | solution.py:265
  79.1 17.7 %collective-permute-start.1 = (f32[512,128]{1,0:T(8,128)}, f32[512,128]{1,0:T(8,128)}, u32[]{:S(2)}, u32[]{:S(2)}) collective-permute-start(f32[512,128]{1,0:T(8,128)} %get-tuple-element.33), channel_id=1, source_target_pairs={{0,1},{1,2},{2,3},{4,5},{5,6},{6,7},{8,9},{9,10},{10,11},{12,13},{... | collective-permute-start | bytes 786440 | tf_op jit(solution)/shard_map/ppermute | solution.py:247
  82.9 21.0 %collective-permute-start.7 = (f32[1,512,128]{2,1,0:T(8,128)}, f32[1,512,128]{2,1,0:T(8,128)S(1)}, u32[]{:S(2)}, u32[]{:S(2)}) collective-permute-start(f32[1,512,128]{2,1,0:T(8,128)} %gate.11.own), channel_id=1, source_target_pairs={{0,16},{4,20},{8,24},{12,28},{16,0},{20,4},{24,8},{28,12},{1,17},{... | collective-permute-start | bytes 786440 | tf_op jit(solution)/shard_map/ppermute | solution.py:265
  92.5 19.8 %collective-permute-start.19 = (f32[2,512,128]{2,1,0:T(8,128)}, f32[2,512,128]{2,1,0:T(8,128)}, u32[]{:S(2)}, u32[]{:S(2)}) collective-permute-start(f32[2,512,128]{2,1,0:T(8,128)} %combine.25.own.rest_1_), channel_id=1, source_target_pairs={{0,4},{4,0},{8,12},{12,8},{16,20},{20,16},{24,28},{28,24},{1,5},{5... | collective-permute-start | bytes 1572872 | tf_op jit(solution)/shard_map/ppermute | solution.py:265
  96.8 13.2 %collective-permute-start = (f32[512,128]{1,0:T(8,128)}, f32[512,128]{1,0:T(8,128)}, u32[]{:S(2)}, u32[]{:S(2)}) collective-permute-start(f32[512,128]{1,0:T(8,128)} %get-tuple-element.34), channel_id=1, source_target_pairs={{1,0},{2,1},{3,2},{5,4},{6,5},{7,6},{9,8},{10,9},{11,10},{13,12},{... | collective-permute-start | bytes 786440 | tf_op jit(solution)/shard_map/ppermute | solution.py:248
  105.2 11.7 %collective-permute-start.20 = (f32[1,512,128]{2,1,0:T(8,128)}, f32[1,512,128]{2,1,0:T(8,128)}, u32[]{:S(2)}, u32[]{:S(2)}) collective-permute-start(f32[1,512,128]{2,1,0:T(8,128)} %combine.26.own), channel_id=1, source_target_pairs={{0,8},{4,12},{8,0},{12,4},{16,24},{20,28},{24,16},{28,20},{1,9},{5... | collective-permute-start | bytes 786440 | tf_op jit(solution)/shard_map/ppermute | solution.py:265
  106.7 20.4 %collective-permute-start.17 = (f32[2,512,128]{2,1,0:T(8,128)}, f32[2,512,128]{2,1,0:T(8,128)}, u32[]{:S(2)}, u32[]{:S(2)}) collective-permute-start(f32[2,512,128]{2,1,0:T(8,128)} %combine.23.own.rest_1_), channel_id=1, source_target_pairs={{0,4},{4,0},{8,12},{12,8},{16,20},{20,16},{24,28},{28,24},{1,5},{5... | collective-permute-start | bytes 1572872 | tf_op jit(solution)/shard_map/ppermute | solution.py:265
  107.5 16.0 %collective-permute-start.8 = (f32[1,512,128]{2,1,0:T(8,128)}, f32[1,512,128]{2,1,0:T(8,128)}, u32[]{:S(2)}, u32[]{:S(2)}) collective-permute-start(f32[1,512,128]{2,1,0:T(8,128)} %gate.12.own), channel_id=1, source_target_pairs={{0,16},{4,20},{8,24},{12,28},{16,0},{20,4},{24,8},{28,12},{1,17},{... | collective-permute-start | bytes 786440 | tf_op jit(solution)/shard_map/ppermute | solution.py:265
  118.8 22.0 %collective-permute-start.22 = (f32[2,512,128]{2,1,0:T(8,128)}, f32[2,512,128]{2,1,0:T(8,128)}, u32[]{:S(2)}, u32[]{:S(2)}) collective-permute-start(f32[2,512,128]{2,1,0:T(8,128)} %combine.27.rest_1_.own), channel_id=1, source_target_pairs={{0,4},{4,0},{8,12},{12,8},{16,20},{20,16},{24,28},{28,24},{1,5},{5... | collective-permute-start | bytes 1572872 | tf_op jit(solution)/shard_map/ppermute | solution.py:265
  123.5 14.5 %collective-permute-start.9 = (f32[1,512,128]{2,1,0:T(8,128)}, f32[1,512,128]{2,1,0:T(8,128)S(1)}, u32[]{:S(2)}, u32[]{:S(2)}) collective-permute-start(f32[1,512,128]{2,1,0:T(8,128)} %gate.13.own), channel_id=1, source_target_pairs={{0,16},{4,20},{8,24},{12,28},{16,0},{20,4},{24,8},{28,12},{1,17},{... | collective-permute-start | bytes 786440 | tf_op jit(solution)/shard_map/ppermute | solution.py:265
  124.6 14.5 %collective-permute-start.24 = (f32[1,512,128]{2,1,0:T(8,128)S(1)}, f32[1,512,128]{2,1,0:T(8,128)S(1)}, u32[]{:S(2)}, u32[]{:S(2)}) collective-permute-start(f32[1,512,128]{2,1,0:T(8,128)S(1)} %combine.30.own), channel_id=1, source_target_pairs={{0,8},{4,12},{8,0},{12,4},{16,24},{20,28},{24,16},{28,20},{1,9},{5... | collective-permute-start | bytes 786440 | tf_op jit(solution)/shard_map/ppermute | solution.py:265
  139.7 14.9 %collective-permute-start.25 = (f32[2,512,128]{2,1,0:T(8,128)S(1)}, f32[2,512,128]{2,1,0:T(8,128)S(1)}, u32[]{:S(2)}, u32[]{:S(2)}) collective-permute-start(f32[2,512,128]{2,1,0:T(8,128)S(1)} %combine.31.own), channel_id=1, source_target_pairs={{0,4},{4,0},{8,12},{12,8},{16,20},{20,16},{24,28},{28,24},{1,5},{5... | collective-permute-start | bytes 1572872 | tf_op jit(solution)/shard_map/ppermute | solution.py:265
  147.6 16.9 %collective-permute-start.23 = (f32[2,512,128]{2,1,0:T(8,128)S(1)}, f32[2,512,128]{2,1,0:T(8,128)S(1)}, u32[]{:S(2)}, u32[]{:S(2)}) collective-permute-start(f32[2,512,128]{2,1,0:T(8,128)S(1)} %combine.29.own), channel_id=1, source_target_pairs={{0,4},{4,0},{8,12},{12,8},{16,20},{20,16},{24,28},{28,24},{1,5},{5... | collective-permute-start | bytes 1572872 | tf_op jit(solution)/shard_map/ppermute | solution.py:265
  (53 other events, 349.4 us)

commit v4 on v3

--- a/solution.py
+++ b/solution.py
@@ -15,11 +15,14 @@
 ORDER = {
     "stencil": [],
     "gate": [("arrived", -1)],
-    "first": [("inner", -3), ("middle", -2)],
-    "middle": [("inner", -2)],
+    "first": [("inner", -3)],
+    "middle": [("stencil", 2), ("inner", -2)],
     "inner": [],
 }
-VMEM = 40 * 1024 * 1024
+MIB = 1024 * 1024
+VMEM = 20 * MIB
+GATE_VMEM = 1 * MIB
+FIRST_VMEM = 56 * MIB
 QUICK = pl.CostEstimate(flops=0, bytes_accessed=0, transcendentals=0)
 
 
@@ -61,7 +64,7 @@
     out[0] = window * dot3(split_bf16(field), split_bf16(band))
 
 
-def stencil(left, mid, right, apod, coef, fine, offsets, block, count, after):
+def stencil(left, mid, right, apod, coef, fine, offsets, block, count, after, vmem=VMEM):
     rows, width = mid[0].shape
 
     def columns(height, at):
@@ -80,7 +83,7 @@
         + [pl.BlockSpec(memory_space=pl.ANY)] * len(after),
         out_specs=pl.BlockSpec((1, rows, LANES), lambda i: (0, 0, i)),
         out_shape=jax.ShapeDtypeStruct((1, rows, count * LANES), jnp.float32),
-        compiler_params=pltpu.CompilerParams(vmem_limit_bytes=VMEM),
+        compiler_params=pltpu.CompilerParams(vmem_limit_bytes=vmem),
         cost_estimate=QUICK,
         name="stencil",
     )(offsets, left[0], mid[0], right[0], apod, coef, fine, *after)
@@ -98,6 +101,7 @@
         out_specs=anywhere,
         out_shape=jax.ShapeDtypeStruct(value.shape, value.dtype),
         input_output_aliases={0: 0},
+        compiler_params=pltpu.CompilerParams(vmem_limit_bytes=GATE_VMEM),
         cost_estimate=QUICK,
         name="gate",
     )(value, *after)
@@ -298,6 +302,7 @@
                 block,
                 number,
                 after("stencil", chunk),
+                VMEM if chunk else FIRST_VMEM,
             )
             waits = after("gate", chunk)
             if waits:

time: 168 us -> 147 us (0.88)
  waiting for transfers between devices: 55.6 us -> 80.5 us
  local copies, waits for them, and re-layouts: 23.9 us -> 0.1 us
  Pallas kernels: 55.7 us -> 37.6 us
  starting transfers between devices: 31.1 us -> 28.1 us
    ppermute x24, waiting for transfers between devices: 55.6 us -> 80.5 us  [send(): return lax.ppermute(value, 'row', [(a, a ^ half) for a in range(devices)])]
    unnamed x102 -> x26, local copies, waits for them, and re-layouts: 23 us -> 0.06 us
    pallas_call x16, Pallas kernels: 21.7 us -> 10.5 us  [combine(): pl.pallas_call(combine_kernel, in_specs=[small, small, whole, whole] + [p...]
    pallas_call x8, Pallas kernels: 24.6 us -> 17.1 us  [inner(): pl.pallas_call(inner_kernel, grid_spec=pltpu.PrefetchScalarGridSpec(num_s...]
    ppermute x24, starting transfers between devices: 27.7 us -> 25.4 us  [send(): return lax.ppermute(value, 'row', [(a, a ^ half) for a in range(devices)])]
  transfers between devices with their start and end apart: 26 -> 26, of which waited for: 13 -> 15; matrix products, arithmetic and copies ran while one was open for 1% -> 0% of each run, Pallas kernels for 32% -> 22%
where the time goes in v4:
time: 147 us
  waiting for transfers between devices  80.5 us (55%)
  Pallas kernels  37.6 us (26%)
  starting transfers between devices  28.1 us (19%)
    ppermute x24, waiting for transfers between devices, send(): return lax.ppermute(value, 'row', [(a, a ^ half) for a in range(devices)])  80.5 us
    ppermute x24, starting transfers between devices, send(): return lax.ppermute(value, 'row', [(a, a ^ half) for a in range(devices)])  25.4 us
    pallas_call x8, Pallas kernels, inner(): pl.pallas_call(inner_kernel, grid_spec=pltpu.PrefetchScalarGridSpec(num_s...  17.1 us
    pallas_call x16, Pallas kernels, combine(): pl.pallas_call(combine_kernel, in_specs=[small, small, whole, whole] + [p...  10.5 us
    pallas_call x8, Pallas kernels, stencil(): pl.pallas_call(functools.partial(stencil_kernel, block, width // offsets....  10 us
  transfers between devices with their start and end apart: 26, of which 15 were waited for; matrix products, arithmetic and copies ran while one was open for 0% of the time, Pallas kernels for 22%

profile of v4, /device:TPU:0, one launch (start us, length us, event | category | flops | bytes accessed | tf_op | source)
XLA Modules:
  0.0 146.7 jit_solution(7533194100822336685)
XLA Ops:
  0.0 2.5 %stencil.15.own = f32[1,512,128]{2,1,0:T(8,128)} custom-call(s32[32]{0:T(128)} %offsets.15, f32[512,1024]{1,0:T(8,128)} %right.13, f32[512,1024]{1,0:T(8,128)} %right.13, f32[512,1024]{1,0:T(8,128)} %right.13, f32[1,512]{1,0:T(1,128)} %bitcast.11, f32[4,1024]{1,0:T(4,128)} %coef.15, s32[1,1024]{1,0:T(1,128)} %bitcast.3), custom_call_target="tpu_custom_call" | custom-call | tf_op jit(solution)/shard_map/stencil/pallas_call | solution.py:73
  2.5 4.1 %collective-permute-start.2 = (f32[1,512,128]{2,1,0:T(8,128)}, f32[1,512,128]{2,1,0:T(8,128)S(1)}, u32[]{:S(2)}, u32[]{:S(2)}) collective-permute-start(f32[1,512,128]{2,1,0:T(8,128)} %stencil.15.own), channel_id=1, source_target_pairs={{0,16},{4,20},{8,24},{12,28},{16,0},{20,4},{24,8},{28,12},{1,17},{... | collective-permute-start | bytes 786440 | tf_op jit(solution)/shard_map/ppermute | solution.py:269
  7.7 11.1 %collective-permute-done.2.rest_0_.far = f32[1,512,128]{2,1,0:T(8,128)S(1)} collective-permute-done((f32[1,512,128]{2,1,0:T(8,128)}, f32[1,512,128]{2,1,0:T(8,128)S(1)}, u32[]{:S(2)}, u32[]{:S(2)}) %collective-permute-start.2) | collective-permute-done | bytes 262176 | tf_op jit(solution)/shard_map/ppermute | solution.py:269
  19.5 4.1 %collective-permute-start.12 = (f32[1,512,128]{2,1,0:T(8,128)S(1)}, f32[1,512,128]{2,1,0:T(8,128)S(1)}, u32[]{:S(2)}, u32[]{:S(2)}) collective-permute-start(f32[1,512,128]{2,1,0:T(8,128)S(1)} %combine.18.own), channel_id=1, source_target_pairs={{0,8},{4,12},{8,0},{12,4},{16,24},{20,28},{24,16},{28,20},{1,9},{5... | collective-permute-start | bytes 786440 | tf_op jit(solution)/shard_map/ppermute | solution.py:269
  24.6 8.3 %collective-permute-done.3.rest_0_.far = f32[1,512,128]{2,1,0:T(8,128)S(1)} collective-permute-done((f32[1,512,128]{2,1,0:T(8,128)S(1)}, f32[1,512,128]{2,1,0:T(8,128)S(1)}, u32[]{:S(2)}, u32[]{:S(2)}) %collective-permute-start.3) | collective-permute-done | bytes 262176 | tf_op jit(solution)/shard_map/ppermute | solution.py:269
  38.4 7.7 %collective-permute-done.4.rest_0_.far = f32[1,512,128]{2,1,0:T(8,128)S(1)} collective-permute-done((f32[1,512,128]{2,1,0:T(8,128)S(1)}, f32[1,512,128]{2,1,0:T(8,128)S(1)}, u32[]{:S(2)}, u32[]{:S(2)}) %collective-permute-start.4) | collective-permute-done | bytes 262176 | tf_op jit(solution)/shard_map/ppermute | solution.py:269
  51.3 8.1 %collective-permute-done.5.rest_0_.far = f32[1,512,128]{2,1,0:T(8,128)S(1)} collective-permute-done((f32[1,512,128]{2,1,0:T(8,128)S(1)}, f32[1,512,128]{2,1,0:T(8,128)S(1)}, u32[]{:S(2)}, u32[]{:S(2)}) %collective-permute-start.5) | collective-permute-done | bytes 262176 | tf_op jit(solution)/shard_map/ppermute | solution.py:269
  59.5 2.1 %inner.8 = (f32[2,512,1024]{2,1,0:T(8,128)}, f32[8,128]{1,0:T(8,128)S(1)}) custom-call(s32[1]{0:T(128)} %bitcast.me, f32[8,512,4]{2,1,0:T(8,128)S(1)} %copy-done.1, bf16[512,512]{1,0:T(8,128)(2,1)S(1)} %copy-done.2, bf16[512,512]{1,0:T(8,128)(2,1)S(1)} %copy-done.3, bf16[512,512]{1,0:T(8,128)(2,1)S(1)} %copy-done.4, bf16[512,512]{1,0:T(8,128)(2,1)S(1)} %copy-done.5, ...), custom_call_target="tpu_custom_call" | custom-call | tf_op jit(solution)/shard_map/inner/pallas_call | solution.py:164
  63.9 2.7 %collective-permute-start.18 = (f32[1,512,128]{2,1,0:T(8,128)S(1)}, f32[1,512,128]{2,1,0:T(8,128)S(1)}, u32[]{:S(2)}, u32[]{:S(2)}) collective-permute-start(f32[1,512,128]{2,1,0:T(8,128)S(1)} %combine.24.own), channel_id=1, source_target_pairs={{0,8},{4,12},{8,0},{12,4},{16,24},{20,28},{24,16},{28,20},{1,9},{5... | collective-permute-start | bytes 786440 | tf_op jit(solution)/shard_map/ppermute | solution.py:269
  69.0 5.0 %collective-permute-done.6.rest_0_.far = f32[1,512,128]{2,1,0:T(8,128)S(1)} collective-permute-done((f32[1,512,128]{2,1,0:T(8,128)S(1)}, f32[1,512,128]{2,1,0:T(8,128)S(1)}, u32[]{:S(2)}, u32[]{:S(2)}) %collective-permute-start.6) | collective-permute-done | bytes 262176 | tf_op jit(solution)/shard_map/ppermute | solution.py:269
  74.0 2.1 %inner.9 = (f32[2,512,1024]{2,1,0:T(8,128)}, f32[8,128]{1,0:T(8,128)S(1)}) custom-call(s32[1]{0:T(128)} %bitcast.me, f32[8,512,4]{2,1,0:T(8,128)S(1)} %copy-done.1, bf16[512,512]{1,0:T(8,128)(2,1)S(1)} %copy-done.2, bf16[512,512]{1,0:T(8,128)(2,1)S(1)} %copy-done.3, bf16[512,512]{1,0:T(8,128)(2,1)S(1)} %copy-done.4, ...), custom_call_target="tpu_custom_call", output_to_operand_aliasing={{0}: (8, {})} | custom-call | tf_op jit(solution)/shard_map/inner/pallas_call | solution.py:164
  83.0 2.1 %inner.10 = (f32[2,512,1024]{2,1,0:T(8,128)}, f32[8,128]{1,0:T(8,128)S(1)}) custom-call(s32[1]{0:T(128)} %bitcast.me, f32[8,512,4]{2,1,0:T(8,128)S(1)} %copy-done.1, bf16[512,512]{1,0:T(8,128)(2,1)S(1)} %copy-done.2, bf16[512,512]{1,0:T(8,128)(2,1)S(1)} %copy-done.3, bf16[512,512]{1,0:T(8,128)(2,1)S(1)} %copy-done.4, ...), custom_call_target="tpu_custom_call", output_to_operand_aliasing={{0}: (8, {})} | custom-call | tf_op jit(solution)/shard_map/inner/pallas_call | solution.py:164
  85.1 2.4 %collective-permute-done.7.rest_0_.far = f32[1,512,128]{2,1,0:T(8,128)S(1)} collective-permute-done((f32[1,512,128]{2,1,0:T(8,128)S(1)}, f32[1,512,128]{2,1,0:T(8,128)S(1)}, u32[]{:S(2)}, u32[]{:S(2)}) %collective-permute-start.7) | collective-permute-done | bytes 262176 | tf_op jit(solution)/shard_map/ppermute | solution.py:269
  87.5 3.0 %collective-permute-done.14.far = f32[1,512,128]{2,1,0:T(8,128)S(1)} collective-permute-done((f32[1,512,128]{2,1,0:T(8,128)S(1)}, f32[1,512,128]{2,1,0:T(8,128)S(1)}, u32[]{:S(2)}, u32[]{:S(2)}) %collective-permute-start.14) | collective-permute-done | bytes 262176 | tf_op jit(solution)/shard_map/ppermute | solution.py:269
  93.9 8.2 %collective-permute-done.8.rest_0_.far = f32[1,512,128]{2,1,0:T(8,128)S(1)} collective-permute-done((f32[1,512,128]{2,1,0:T(8,128)S(1)}, f32[1,512,128]{2,1,0:T(8,128)S(1)}, u32[]{:S(2)}, u32[]{:S(2)}) %collective-permute-start.8) | collective-permute-done | bytes 262176 | tf_op jit(solution)/shard_map/ppermute | solution.py:269
  102.1 2.1 %inner.11 = (f32[2,512,1024]{2,1,0:T(8,128)}, f32[8,128]{1,0:T(8,128)S(1)}) custom-call(s32[1]{0:T(128)} %bitcast.me, f32[8,512,4]{2,1,0:T(8,128)S(1)} %copy-done.1, bf16[512,512]{1,0:T(8,128)(2,1)S(1)} %copy-done.2, bf16[512,512]{1,0:T(8,128)(2,1)S(1)} %copy-done.3, bf16[512,512]{1,0:T(8,128)(2,1)S(1)} %copy-done.4, ...), custom_call_target="tpu_custom_call", output_to_operand_aliasing={{0}: (8, {})} | custom-call | tf_op jit(solution)/shard_map/inner/pallas_call | solution.py:164
  108.6 2.1 %inner.12 = (f32[2,512,1024]{2,1,0:T(8,128)}, f32[8,128]{1,0:T(8,128)S(1)}) custom-call(s32[1]{0:T(128)} %bitcast.me, f32[8,512,4]{2,1,0:T(8,128)S(1)} %copy-done.1, bf16[512,512]{1,0:T(8,128)(2,1)S(1)} %copy-done.2, bf16[512,512]{1,0:T(8,128)(2,1)S(1)} %copy-done.3, bf16[512,512]{1,0:T(8,128)(2,1)S(1)} %copy-done.4, ...), custom_call_target="tpu_custom_call", output_to_operand_aliasing={{0}: (8, {})} | custom-call | tf_op jit(solution)/shard_map/inner/pallas_call | solution.py:164
  110.7 4.9 %collective-permute-done.9.far = f32[1,512,128]{2,1,0:T(8,128)S(1)} collective-permute-done((f32[1,512,128]{2,1,0:T(8,128)S(1)}, f32[1,512,128]{2,1,0:T(8,128)S(1)}, u32[]{:S(2)}, u32[]{:S(2)}) %collective-permute-start.9) | collective-permute-done | bytes 262176 | tf_op jit(solution)/shard_map/ppermute | solution.py:269
  116.4 4.6 %collective-permute-done.24.far = f32[1,512,128]{2,1,0:T(8,128)S(1)} collective-permute-done((f32[1,512,128]{2,1,0:T(8,128)S(1)}, f32[1,512,128]{2,1,0:T(8,128)S(1)}, u32[]{:S(2)}, u32[]{:S(2)}) %collective-permute-start.24) | collective-permute-done | bytes 262176 | tf_op jit(solution)/shard_map/ppermute | solution.py:269
  123.0 2.1 %inner.13 = (f32[2,512,1024]{2,1,0:T(8,128)}, f32[8,128]{1,0:T(8,128)S(1)}) custom-call(s32[1]{0:T(128)} %bitcast.me, f32[8,512,4]{2,1,0:T(8,128)S(1)} %copy-done.1, bf16[512,512]{1,0:T(8,128)(2,1)S(1)} %copy-done.2, bf16[512,512]{1,0:T(8,128)(2,1)S(1)} %copy-done.3, bf16[512,512]{1,0:T(8,128)(2,1)S(1)} %copy-done.4, ...), custom_call_target="tpu_custom_call", output_to_operand_aliasing={{0}: (8, {})} | custom-call | tf_op jit(solution)/shard_map/inner/pallas_call | solution.py:164
  127.5 9.0 %collective-permute-done.25.far = f32[2,512,128]{2,1,0:T(8,128)S(1)} collective-permute-done((f32[2,512,128]{2,1,0:T(8,128)S(1)}, f32[2,512,128]{2,1,0:T(8,128)S(1)}, u32[]{:S(2)}, u32[]{:S(2)}) %collective-permute-start.25) | collective-permute-done | bytes 524320 | tf_op jit(solution)/shard_map/ppermute | solution.py:269
  136.6 2.1 %inner.14 = (f32[2,512,1024]{2,1,0:T(8,128)}, f32[8,128]{1,0:T(8,128)}) custom-call(s32[1]{0:T(128)} %bitcast.me, f32[8,512,4]{2,1,0:T(8,128)S(1)} %copy-done.1, bf16[512,512]{1,0:T(8,128)(2,1)S(1)} %copy-done.2, bf16[512,512]{1,0:T(8,128)(2,1)S(1)} %copy-done.3, bf16[512,512]{1,0:T(8,128)(2,1)S(1)} %copy-done.4, ...), custom_call_target="tpu_custom_call", output_to_operand_aliasing={{0}: (8, {})} | custom-call | tf_op jit(solution)/shard_map/inner/pallas_call | solution.py:164
  138.7 5.8 %collective-permute-done.23.far = f32[2,512,128]{2,1,0:T(8,128)S(1)} collective-permute-done((f32[2,512,128]{2,1,0:T(8,128)S(1)}, f32[2,512,128]{2,1,0:T(8,128)S(1)}, u32[]{:S(2)}, u32[]{:S(2)}) %collective-permute-start.23) | collective-permute-done | bytes 524320 | tf_op jit(solution)/shard_map/ppermute | solution.py:269
  144.5 2.1 %inner.15 = (f32[2,512,1024]{2,1,0:T(8,128)}, f32[8,128]{1,0:T(8,128)}) custom-call(s32[1]{0:T(128)} %bitcast.me, f32[8,512,4]{2,1,0:T(8,128)S(1)} %copy-done.1, bf16[512,512]{1,0:T(8,128)(2,1)S(1)} %copy-done.2, bf16[512,512]{1,0:T(8,128)(2,1)S(1)} %copy-done.3, bf16[512,512]{1,0:T(8,128)(2,1)S(1)} %copy-done.4, ...), custom_call_target="tpu_custom_call", output_to_operand_aliasing={{0}: (8, {})} | custom-call | tf_op jit(solution)/shard_map/inner/pallas_call | solution.py:164
  (94 shorter events, 37.7 us)
Async XLA Ops:
  2.5 16.3 %collective-permute-start.2 = (f32[1,512,128]{2,1,0:T(8,128)}, f32[1,512,128]{2,1,0:T(8,128)S(1)}, u32[]{:S(2)}, u32[]{:S(2)}) collective-permute-start(f32[1,512,128]{2,1,0:T(8,128)} %stencil.15.own), channel_id=1, source_target_pairs={{0,16},{4,20},{8,24},{12,28},{16,0},{20,4},{24,8},{28,12},{1,17},{... | collective-permute-start | bytes 786440 | tf_op jit(solution)/shard_map/ppermute | solution.py:269
  18.8 14.1 %collective-permute-start.3 = (f32[1,512,128]{2,1,0:T(8,128)S(1)}, f32[1,512,128]{2,1,0:T(8,128)S(1)}, u32[]{:S(2)}, u32[]{:S(2)}) collective-permute-start(f32[1,512,128]{2,1,0:T(8,128)S(1)} %gate.7.own), channel_id=1, source_target_pairs={{0,16},{4,20},{8,24},{12,28},{16,0},{20,4},{24,8},{28,12},{1,17},{... | collective-permute-start | bytes 786440 | tf_op jit(solution)/shard_map/ppermute | solution.py:269
  19.5 14.2 %collective-permute-start.12 = (f32[1,512,128]{2,1,0:T(8,128)S(1)}, f32[1,512,128]{2,1,0:T(8,128)S(1)}, u32[]{:S(2)}, u32[]{:S(2)}) collective-permute-start(f32[1,512,128]{2,1,0:T(8,128)S(1)} %combine.18.own), channel_id=1, source_target_pairs={{0,8},{4,12},{8,0},{12,4},{16,24},{20,28},{24,16},{28,20},{1,9},{5... | collective-permute-start | bytes 786440 | tf_op jit(solution)/shard_map/ppermute | solution.py:269
  32.9 13.2 %collective-permute-start.4 = (f32[1,512,128]{2,1,0:T(8,128)S(1)}, f32[1,512,128]{2,1,0:T(8,128)S(1)}, u32[]{:S(2)}, u32[]{:S(2)}) collective-permute-start(f32[1,512,128]{2,1,0:T(8,128)S(1)} %gate.8.rest_0_.own), channel_id=1, source_target_pairs={{0,16},{4,20},{8,24},{12,28},{16,0},{20,4},{24,8},{28,12},{1,17},{... | collective-permute-start | bytes 786440 | tf_op jit(solution)/shard_map/ppermute | solution.py:269
  34.4 25.0 %collective-permute-start.13 = (f32[2,512,128]{2,1,0:T(8,128)S(1)}, f32[2,512,128]{2,1,0:T(8,128)S(1)}, u32[]{:S(2)}, u32[]{:S(2)}) collective-permute-start(f32[2,512,128]{2,1,0:T(8,128)S(1)} %combine.19.own), channel_id=1, source_target_pairs={{0,4},{4,0},{8,12},{12,8},{16,20},{20,16},{24,28},{28,24},{1,5},{5... | collective-permute-start | bytes 1572872 | tf_op jit(solution)/shard_map/ppermute | solution.py:269
  46.1 13.3 %collective-permute-start.5 = (f32[1,512,128]{2,1,0:T(8,128)S(1)}, f32[1,512,128]{2,1,0:T(8,128)S(1)}, u32[]{:S(2)}, u32[]{:S(2)}) collective-permute-start(f32[1,512,128]{2,1,0:T(8,128)S(1)} %gate.9.rest_0_.own), channel_id=1, source_target_pairs={{0,16},{4,20},{8,24},{12,28},{16,0},{20,4},{24,8},{28,12},{1,17},{... | collective-permute-start | bytes 786440 | tf_op jit(solution)/shard_map/ppermute | solution.py:269
  46.8 14.8 %collective-permute-start.15 = (f32[1,512,128]{2,1,0:T(8,128)S(1)}, f32[1,512,128]{2,1,0:T(8,128)S(1)}, u32[]{:S(2)}, u32[]{:S(2)}) collective-permute-start(f32[1,512,128]{2,1,0:T(8,128)S(1)} %combine.21.own), channel_id=1, source_target_pairs={{0,8},{4,12},{8,0},{12,4},{16,24},{20,28},{24,16},{28,20},{1,9},{5... | collective-permute-start | bytes 786440 | tf_op jit(solution)/shard_map/ppermute | solution.py:269
  49.3 24.7 %collective-permute-start.11 = (f32[2,512,128]{2,1,0:T(8,128)S(1)}, f32[2,512,128]{2,1,0:T(8,128)S(1)}, u32[]{:S(2)}, u32[]{:S(2)}) collective-permute-start(f32[2,512,128]{2,1,0:T(8,128)S(1)} %combine.17.own), channel_id=1, source_target_pairs={{0,4},{4,0},{8,12},{12,8},{16,20},{20,16},{24,28},{28,24},{1,5},{5... | collective-permute-start | bytes 1572872 | tf_op jit(solution)/shard_map/ppermute | solution.py:269
  59.4 14.6 %collective-permute-start.6 = (f32[1,512,128]{2,1,0:T(8,128)S(1)}, f32[1,512,128]{2,1,0:T(8,128)S(1)}, u32[]{:S(2)}, u32[]{:S(2)}) collective-permute-start(f32[1,512,128]{2,1,0:T(8,128)S(1)} %gate.10.own.rest_0_), channel_id=1, source_target_pairs={{0,16},{4,20},{8,24},{12,28},{16,0},{20,4},{24,8},{28,12},{1,17},{... | collective-permute-start | bytes 786440 | tf_op jit(solution)/shard_map/ppermute | solution.py:269
  62.3 20.7 %collective-permute-start.16 = (f32[2,512,128]{2,1,0:T(8,128)S(1)}, f32[2,512,128]{2,1,0:T(8,128)S(1)}, u32[]{:S(2)}, u32[]{:S(2)}) collective-permute-start(f32[2,512,128]{2,1,0:T(8,128)S(1)} %combine.22.own), channel_id=1, source_target_pairs={{0,4},{4,0},{8,12},{12,8},{16,20},{20,16},{24,28},{28,24},{1,5},{5... | collective-permute-start | bytes 1572872 | tf_op jit(solution)/shard_map/ppermute | solution.py:269
  63.9 14.9 %collective-permute-start.18 = (f32[1,512,128]{2,1,0:T(8,128)S(1)}, f32[1,512,128]{2,1,0:T(8,128)S(1)}, u32[]{:S(2)}, u32[]{:S(2)}) collective-permute-start(f32[1,512,128]{2,1,0:T(8,128)S(1)} %combine.24.own), channel_id=1, source_target_pairs={{0,8},{4,12},{8,0},{12,4},{16,24},{20,28},{24,16},{28,20},{1,9},{5... | collective-permute-start | bytes 786440 | tf_op jit(solution)/shard_map/ppermute | solution.py:269
  66.7 13.8 %collective-permute-start.1 = (f32[512,128]{1,0:T(8,128)S(1)}, f32[512,128]{1,0:T(8,128)S(1)}, u32[]{:S(2)}, u32[]{:S(2)}) collective-permute-start(f32[512,128]{1,0:T(8,128)S(1)} %get-tuple-element.33), channel_id=1, source_target_pairs={{0,1},{1,2},{2,3},{4,5},{5,6},{6,7},{8,9},{9,10},{10,11},{12,13},{... | collective-permute-start | bytes 786440 | tf_op jit(solution)/shard_map/ppermute | solution.py:251
  74.0 13.5 %collective-permute-start.7 = (f32[1,512,128]{2,1,0:T(8,128)S(1)}, f32[1,512,128]{2,1,0:T(8,128)S(1)}, u32[]{:S(2)}, u32[]{:S(2)}) collective-permute-start(f32[1,512,128]{2,1,0:T(8,128)S(1)} %gate.11.rest_0_.own), channel_id=1, source_target_pairs={{0,16},{4,20},{8,24},{12,28},{16,0},{20,4},{24,8},{28,12},{1,17},{... | collective-permute-start | bytes 786440 | tf_op jit(solution)/shard_map/ppermute | solution.py:269
  76.8 13.8 %collective-permute-start.14 = (f32[1,512,128]{2,1,0:T(8,128)S(1)}, f32[1,512,128]{2,1,0:T(8,128)S(1)}, u32[]{:S(2)}, u32[]{:S(2)}) collective-permute-start(f32[1,512,128]{2,1,0:T(8,128)S(1)} %combine.20.own), channel_id=1, source_target_pairs={{0,8},{4,12},{8,0},{12,4},{16,24},{20,28},{24,16},{28,20},{1,9},{5... | collective-permute-start | bytes 786440 | tf_op jit(solution)/shard_map/ppermute | solution.py:269
  79.5 22.7 %collective-permute-start.19 = (f32[2,512,128]{2,1,0:T(8,128)S(1)}, f32[2,512,128]{2,1,0:T(8,128)S(1)}, u32[]{:S(2)}, u32[]{:S(2)}) collective-permute-start(f32[2,512,128]{2,1,0:T(8,128)S(1)} %combine.25.own), channel_id=1, source_target_pairs={{0,4},{4,0},{8,12},{12,8},{16,20},{20,16},{24,28},{28,24},{1,5},{5... | collective-permute-start | bytes 1572872 | tf_op jit(solution)/shard_map/ppermute | solution.py:269
  80.5 12.4 %collective-permute-start = (f32[512,128]{1,0:T(8,128)S(1)}, f32[512,128]{1,0:T(8,128)S(1)}, u32[]{:S(2)}, u32[]{:S(2)}) collective-permute-start(f32[512,128]{1,0:T(8,128)S(1)} %get-tuple-element.34), channel_id=1, source_target_pairs={{1,0},{2,1},{3,2},{5,4},{6,5},{7,6},{9,8},{10,9},{11,10},{13,12},{... | collective-permute-start | bytes 786440 | tf_op jit(solution)/shard_map/ppermute | solution.py:252
  87.5 14.6 %collective-permute-start.8 = (f32[1,512,128]{2,1,0:T(8,128)S(1)}, f32[1,512,128]{2,1,0:T(8,128)S(1)}, u32[]{:S(2)}, u32[]{:S(2)}) collective-permute-start(f32[1,512,128]{2,1,0:T(8,128)S(1)} %gate.12.rest_0_.own), channel_id=1, source_target_pairs={{0,16},{4,20},{8,24},{12,28},{16,0},{20,4},{24,8},{28,12},{1,17},{... | collective-permute-start | bytes 786440 | tf_op jit(solution)/shard_map/ppermute | solution.py:269
  91.2 17.3 %collective-permute-start.17 = (f32[2,512,128]{2,1,0:T(8,128)S(1)}, f32[2,512,128]{2,1,0:T(8,128)S(1)}, u32[]{:S(2)}, u32[]{:S(2)}) collective-permute-start(f32[2,512,128]{2,1,0:T(8,128)S(1)} %combine.23.own), channel_id=1, source_target_pairs={{0,4},{4,0},{8,12},{12,8},{16,20},{20,16},{24,28},{28,24},{1,5},{5... | collective-permute-start | bytes 1572872 | tf_op jit(solution)/shard_map/ppermute | solution.py:269
  92.7 12.6 %collective-permute-start.21 = (f32[1,512,128]{2,1,0:T(8,128)S(1)}, f32[1,512,128]{2,1,0:T(8,128)S(1)}, u32[]{:S(2)}, u32[]{:S(2)}) collective-permute-start(f32[1,512,128]{2,1,0:T(8,128)S(1)} %combine.27.own), channel_id=1, source_target_pairs={{0,8},{4,12},{8,0},{12,4},{16,24},{20,28},{24,16},{28,20},{1,9},{5... | collective-permute-start | bytes 786440 | tf_op jit(solution)/shard_map/ppermute | solution.py:269
  102.1 13.5 %collective-permute-start.9 = (f32[1,512,128]{2,1,0:T(8,128)S(1)}, f32[1,512,128]{2,1,0:T(8,128)S(1)}, u32[]{:S(2)}, u32[]{:S(2)}) collective-permute-start(f32[1,512,128]{2,1,0:T(8,128)S(1)} %gate.13.own.rest_0_), channel_id=1, source_target_pairs={{0,16},{4,20},{8,24},{12,28},{16,0},{20,4},{24,8},{28,12},{1,17},{... | collective-permute-start | bytes 786440 | tf_op jit(solution)/shard_map/ppermute | solution.py:269
  106.0 16.9 %collective-permute-start.22 = (f32[2,512,128]{2,1,0:T(8,128)S(1)}, f32[2,512,128]{2,1,0:T(8,128)S(1)}, u32[]{:S(2)}, u32[]{:S(2)}) collective-permute-start(f32[2,512,128]{2,1,0:T(8,128)S(1)} %combine.28.own), channel_id=1, source_target_pairs={{0,4},{4,0},{8,12},{12,8},{16,20},{20,16},{24,28},{28,24},{1,5},{5... | collective-permute-start | bytes 1572872 | tf_op jit(solution)/shard_map/ppermute | solution.py:269
  108.0 12.9 %collective-permute-start.24 = (f32[1,512,128]{2,1,0:T(8,128)S(1)}, f32[1,512,128]{2,1,0:T(8,128)S(1)}, u32[]{:S(2)}, u32[]{:S(2)}) collective-permute-start(f32[1,512,128]{2,1,0:T(8,128)S(1)} %combine.30.own), channel_id=1, source_target_pairs={{0,8},{4,12},{8,0},{12,4},{16,24},{20,28},{24,16},{28,20},{1,9},{5... | collective-permute-start | bytes 786440 | tf_op jit(solution)/shard_map/ppermute | solution.py:269
  121.6 14.9 %collective-permute-start.25 = (f32[2,512,128]{2,1,0:T(8,128)S(1)}, f32[2,512,128]{2,1,0:T(8,128)S(1)}, u32[]{:S(2)}, u32[]{:S(2)}) collective-permute-start(f32[2,512,128]{2,1,0:T(8,128)S(1)} %combine.31.own), channel_id=1, source_target_pairs={{0,4},{4,0},{8,12},{12,8},{16,20},{20,16},{24,28},{28,24},{1,5},{5... | collective-permute-start | bytes 1572872 | tf_op jit(solution)/shard_map/ppermute | solution.py:269
  126.3 18.3 %collective-permute-start.23 = (f32[2,512,128]{2,1,0:T(8,128)S(1)}, f32[2,512,128]{2,1,0:T(8,128)S(1)}, u32[]{:S(2)}, u32[]{:S(2)}) collective-permute-start(f32[2,512,128]{2,1,0:T(8,128)S(1)} %combine.29.own), channel_id=1, source_target_pairs={{0,4},{4,0},{8,12},{12,8},{16,20},{20,16},{24,28},{28,24},{1,5},{5... | collective-permute-start | bytes 1572872 | tf_op jit(solution)/shard_map/ppermute | solution.py:269
  (15 other events, 165.5 us)

commit v5 on v4

--- a/solution.py
+++ b/solution.py
@@ -11,6 +11,7 @@
 
 TAPS = 4
 LANES = 128
+DIRECT = 2
 SIZES = (1, 1, 1, 1, 1, 1)
 ORDER = {
     "stencil": [],
@@ -134,15 +135,16 @@
     )(me, factors, own, far, *after)
 
 
-def inner_kernel(me, factors, cos_high, cos_low, sin_high, sin_low, own, far, *rest):
+def inner_kernel(count, me, factors, cos_high, cos_low, sin_high, sin_low, *rest):
     out, token = rest[-2:]
-    a_re, a_im, b_re, b_im = (factors[0, :, i : i + 1] for i in range(4))
-    if own.shape[0] == 2:
-        y_re = a_re * own[0] - a_im * own[1] + (b_re * far[0] - b_im * far[1])
-        y_im = a_re * own[1] + a_im * own[0] + (b_re * far[1] + b_im * far[0])
-    else:
-        y_re = a_re * own[0] + b_re * far[0]
-        y_im = a_im * own[0] + b_im * far[0]
+    y_re = y_im = 0.0
+    for i, block in enumerate(rest[:count]):
+        f_re, f_im = (factors[0, :, 2 * i + j : 2 * i + j + 1] for j in range(2))
+        y_re += f_re * block[0]
+        y_im += f_im * block[0]
+        if block.shape[0] == 2:
+            y_re -= f_im * block[1]
+            y_im += f_re * block[1]
     both = split_bf16(jnp.concatenate([y_re, y_im], axis=1))
     cos_part = dot3((cos_high[...], cos_low[...]), both)
     sin_part = dot3((sin_high[...], sin_low[...]), both)
@@ -151,18 +153,18 @@
     token[...] = jnp.zeros_like(token)
 
 
-def inner(me, factors, tables, own, far, result, block, full_width, after):
-    number, rows, width = own.shape
+def inner(me, factors, tables, blocks, result, block, full_width, after):
+    number, rows, width = blocks[0].shape
     kept = [] if result is None else [result]
-    inputs = [me, factors, *tables, own, far, *after, *kept]
+    inputs = [me, factors, *tables, *blocks, *after, *kept]
     specs = (
-        [pl.BlockSpec((1, rows, 4), lambda i, at: (at[0], 0, 0))]
+        [pl.BlockSpec((1,) + factors.shape[1:], lambda i, at: (at[0], 0, 0))]
         + [pl.BlockSpec((rows, rows), lambda i, at: (0, 0))] * 4
-        + [pl.BlockSpec((number, rows, LANES), lambda i, at: (0, 0, i))] * 2
+        + [pl.BlockSpec((number, rows, LANES), lambda i, at: (0, 0, i))] * len(blocks)
         + [pl.BlockSpec(memory_space=pl.ANY)] * (len(after) + len(kept))
     )
     return pl.pallas_call(
-        inner_kernel,
+        functools.partial(inner_kernel, len(blocks)),
         grid_spec=pltpu.PrefetchScalarGridSpec(
             num_scalar_prefetch=1,
             grid=(width // LANES,),
@@ -257,19 +259,26 @@
     twiddle = np.exp(-2j * np.pi / total * (outer[:, None] * np.arange(rows)[None, :] % total))
     factors = [jnp.asarray(parts(own, far)) for _, own, far, _, _ in stages[:-1]]
     _, own, far, _, phase = stages[-1]
-    factors.append(
-        jnp.asarray(parts((own * phase)[:, None] * twiddle, (far * phase)[:, None] * twiddle))
-    )
+    own, far = (own * phase)[:, None] * twiddle, (far * phase)[:, None] * twiddle
+    factors.append(jnp.asarray(parts(own, far)))
+    half, near_own, near_far = stages[-2][:3]
+    flip = np.arange(devices) ^ stages[-1][0]
+    direct = [own * near_own[:, None], own * near_far[:, None]]
+    direct += [far * near_own[flip, None], far * near_far[flip, None]]
+    partners = [half, stages[-1][0], half ^ stages[-1][0]]
+    factors.append(jnp.asarray(parts(*direct)))
     numbers = [2 if stages[s + 1][3] else 1 for s in range(levels - 1)]
 
     chunks = column_chunks(count)
 
-    def send(value, level):
-        half = stages[level][0]
+    def send(value, half):
         return lax.ppermute(value, "row", [(a, a ^ half) for a in range(devices)])
 
     out, far, results = {}, {}, {}
     stage_of = {"stencil": 0, "first": 1, "middle": levels - 1, "inner": levels}
+
+    def is_direct(chunk):
+        return chunk >= len(chunks) - DIRECT
 
     def after(name, chunk):
         kept = []
@@ -278,8 +287,8 @@
             if 0 <= at < len(chunks):
                 if what == "arrived":
                     make(0, at)
-                    kept.append(far[0, at])
-                else:
+                    kept.append(far[0, at][0])
+                elif stage_of[what] != levels - 1 or not is_direct(at):
                     make(stage_of[what], at)
                     kept.append(out[stage_of[what], at])
         return kept
@@ -308,13 +317,15 @@
             if waits:
                 out[stage, chunk] = gate(out[stage, chunk], waits)
         else:
-            make(stage - 1, chunk)
-            near = (out[stage - 1, chunk], far[stage - 1, chunk])
+            source = levels - 2 if stage == levels and is_direct(chunk) else stage - 1
+            make(source, chunk)
+            near, there = out[source, chunk], far[source, chunk]
             if stage < levels:
                 out[stage, chunk] = combine(
                     me,
                     factors[stage - 1],
-                    *near,
+                    near,
+                    there[0],
                     numbers[stage - 1],
                     after("first" if stage == 1 else "middle", chunk),
                 )
@@ -323,16 +334,17 @@
                     make(stage, chunk - 1)
                 results[chunk], out[stage, chunk] = inner(
                     me,
-                    factors[stage - 1],
+                    factors[len(there) // 2 + levels - 1],
                     tables,
-                    *near,
+                    [near, *there],
                     results.get(chunk - 1),
                     block,
                     width,
                     after("inner", chunk),
                 )
         if stage < levels:
-            far[stage, chunk] = send(out[stage, chunk], stage)
+            ways = partners if stage == levels - 2 and is_direct(chunk) else [stages[stage][0]]
+            far[stage, chunk] = [send(out[stage, chunk], half) for half in ways]
 
     make(levels, len(chunks) - 1)
     return results[len(chunks) - 1]

time: 147 us -> 144 us (0.980)
  waiting for transfers between devices: 80.5 us -> 74.9 us
  starting transfers between devices: 28.1 us -> 31.9 us
    ppermute x24 -> x26, waiting for transfers between devices: 80.5 us -> 74.9 us  [send(): return lax.ppermute(value, 'row', [(a, a ^ half) for a in range(devices)])]
    ppermute x24 -> x26, starting transfers between devices: 25.4 us -> 29.2 us  [send(): return lax.ppermute(value, 'row', [(a, a ^ half) for a in range(devices)])]
    pallas_call x16 -> x14, Pallas kernels: 10.5 us -> 9.15 us  [combine(): pl.pallas_call(combine_kernel, in_specs=[small, small, whole, whole] + [p...]
  transfers between devices with their start and end apart: 26 -> 28, of which waited for: 15 -> 16; matrix products, arithmetic and copies ran while one was open for 0% -> 0% of each run, Pallas kernels for 22% -> 22%
where the time goes in v5:
time: 144 us
  waiting for transfers between devices  74.9 us (52%)
  Pallas kernels  37 us (26%)
  starting transfers between devices  31.9 us (22%)
    ppermute x26, waiting for transfers between devices, send(): return lax.ppermute(value, 'row', [(a, a ^ half) for a in range(devices)])  74.9 us
    ppermute x26, starting transfers between devices, send(): return lax.ppermute(value, 'row', [(a, a ^ half) for a in range(devices)])  29.2 us
    pallas_call x8, Pallas kernels, inner(): pl.pallas_call(functools.partial(inner_kernel, len(blocks)), grid_spec=pl...  17.9 us
    pallas_call x8, Pallas kernels, stencil(): pl.pallas_call(functools.partial(stencil_kernel, block, width // offsets....  10 us
    pallas_call x14, Pallas kernels, combine(): pl.pallas_call(combine_kernel, in_specs=[small, small, whole, whole] + [p...  9.15 us
  transfers between devices with their start and end apart: 28, of which 16 were waited for; matrix products, arithmetic and copies ran while one was open for 0% of the time, Pallas kernels for 22%

profile of v5, /device:TPU:0, one launch (start us, length us, event | category | flops | bytes accessed | tf_op | source)
XLA Modules:
  0.0 144.3 jit_solution(7863888332929548743)
XLA Ops:
  0.0 2.5 %stencil.15.own = f32[1,512,128]{2,1,0:T(8,128)} custom-call(s32[32]{0:T(128)} %offsets.15, f32[512,1024]{1,0:T(8,128)} %right.13, f32[512,1024]{1,0:T(8,128)} %right.13, f32[512,1024]{1,0:T(8,128)} %right.13, f32[1,512]{1,0:T(1,128)} %bitcast.11, f32[4,1024]{1,0:T(4,128)} %coef.15, s32[1,1024]{1,0:T(1,128)} %bitcast.3), custom_call_target="tpu_custom_call" | custom-call | tf_op jit(solution)/shard_map/stencil/pallas_call | solution.py:74
  2.5 4.1 %collective-permute-start.2 = (f32[1,512,128]{2,1,0:T(8,128)}, f32[1,512,128]{2,1,0:T(8,128)S(1)}, u32[]{:S(2)}, u32[]{:S(2)}) collective-permute-start(f32[1,512,128]{2,1,0:T(8,128)} %stencil.15.own), channel_id=1, source_target_pairs={{0,16},{4,20},{8,24},{12,28},{16,0},{20,4},{24,8},{28,12},{1,17},{... | collective-permute-start | bytes 786440 | tf_op jit(solution)/shard_map/ppermute | solution.py:275
  7.7 11.1 %collective-permute-done.2.rest_0_.far = f32[1,512,128]{2,1,0:T(8,128)S(1)} collective-permute-done((f32[1,512,128]{2,1,0:T(8,128)}, f32[1,512,128]{2,1,0:T(8,128)S(1)}, u32[]{:S(2)}, u32[]{:S(2)}) %collective-permute-start.2) | collective-permute-done | bytes 262176 | tf_op jit(solution)/shard_map/ppermute | solution.py:275
  19.5 4.1 %collective-permute-start.12 = (f32[1,512,128]{2,1,0:T(8,128)S(1)}, f32[1,512,128]{2,1,0:T(8,128)S(1)}, u32[]{:S(2)}, u32[]{:S(2)}) collective-permute-start(f32[1,512,128]{2,1,0:T(8,128)S(1)} %combine.16.own), channel_id=1, source_target_pairs={{0,8},{4,12},{8,0},{12,4},{16,24},{20,28},{24,16},{28,20},{1,9},{5... | collective-permute-start | bytes 786440 | tf_op jit(solution)/shard_map/ppermute | solution.py:275
  24.6 8.3 %collective-permute-done.3.rest_0_.far = f32[1,512,128]{2,1,0:T(8,128)S(1)} collective-permute-done((f32[1,512,128]{2,1,0:T(8,128)S(1)}, f32[1,512,128]{2,1,0:T(8,128)S(1)}, u32[]{:S(2)}, u32[]{:S(2)}) %collective-permute-start.3) | collective-permute-done | bytes 262176 | tf_op jit(solution)/shard_map/ppermute | solution.py:275
  38.4 7.7 %collective-permute-done.4.rest_0_.far = f32[1,512,128]{2,1,0:T(8,128)S(1)} collective-permute-done((f32[1,512,128]{2,1,0:T(8,128)S(1)}, f32[1,512,128]{2,1,0:T(8,128)S(1)}, u32[]{:S(2)}, u32[]{:S(2)}) %collective-permute-start.4) | collective-permute-done | bytes 262176 | tf_op jit(solution)/shard_map/ppermute | solution.py:275
  46.1 2.4 %collective-permute-done.10.far = f32[1,512,128]{2,1,0:T(8,128)S(1)} collective-permute-done((f32[1,512,128]{2,1,0:T(8,128)S(1)}, f32[1,512,128]{2,1,0:T(8,128)S(1)}, u32[]{:S(2)}, u32[]{:S(2)}) %collective-permute-start.10) | collective-permute-done | bytes 262176 | tf_op jit(solution)/shard_map/ppermute | solution.py:275
  51.7 7.7 %collective-permute-done.5.rest_0_.far = f32[1,512,128]{2,1,0:T(8,128)S(1)} collective-permute-done((f32[1,512,128]{2,1,0:T(8,128)S(1)}, f32[1,512,128]{2,1,0:T(8,128)S(1)}, u32[]{:S(2)}, u32[]{:S(2)}) %collective-permute-start.5) | collective-permute-done | bytes 262176 | tf_op jit(solution)/shard_map/ppermute | solution.py:275
  62.2 3.1 %collective-permute-start.18 = (f32[1,512,128]{2,1,0:T(8,128)S(1)}, f32[1,512,128]{2,1,0:T(8,128)S(1)}, u32[]{:S(2)}, u32[]{:S(2)}) collective-permute-start(f32[1,512,128]{2,1,0:T(8,128)S(1)} %combine.22.own), channel_id=1, source_target_pairs={{0,8},{4,12},{8,0},{12,4},{16,24},{20,28},{24,16},{28,20},{1,9},{5... | collective-permute-start | bytes 786440 | tf_op jit(solution)/shard_map/ppermute | solution.py:275
  69.0 5.0 %collective-permute-done.6.rest_0_.far = f32[1,512,128]{2,1,0:T(8,128)S(1)} collective-permute-done((f32[1,512,128]{2,1,0:T(8,128)S(1)}, f32[1,512,128]{2,1,0:T(8,128)S(1)}, u32[]{:S(2)}, u32[]{:S(2)}) %collective-permute-start.6) | collective-permute-done | bytes 262176 | tf_op jit(solution)/shard_map/ppermute | solution.py:275
  74.0 2.1 %inner.9 = (f32[2,512,1024]{2,1,0:T(8,128)}, f32[8,128]{1,0:T(8,128)S(1)}) custom-call(s32[1]{0:T(128)} %bitcast.me, f32[8,512,4]{2,1,0:T(8,128)S(1)} %copy-done.1, bf16[512,512]{1,0:T(8,128)(2,1)S(1)} %copy-done.2, bf16[512,512]{1,0:T(8,128)(2,1)S(1)} %copy-done.3, bf16[512,512]{1,0:T(8,128)(2,1)S(1)} %copy-done.4, ...), custom_call_target="tpu_custom_call", output_to_operand_aliasing={{0}: (8, {})} | custom-call | tf_op jit(solution)/shard_map/inner/pallas_call | solution.py:166
  83.0 2.1 %inner.10 = (f32[2,512,1024]{2,1,0:T(8,128)}, f32[8,128]{1,0:T(8,128)S(1)}) custom-call(s32[1]{0:T(128)} %bitcast.me, f32[8,512,4]{2,1,0:T(8,128)S(1)} %copy-done.1, bf16[512,512]{1,0:T(8,128)(2,1)S(1)} %copy-done.2, bf16[512,512]{1,0:T(8,128)(2,1)S(1)} %copy-done.3, bf16[512,512]{1,0:T(8,128)(2,1)S(1)} %copy-done.4, ...), custom_call_target="tpu_custom_call", output_to_operand_aliasing={{0}: (8, {})} | custom-call | tf_op jit(solution)/shard_map/inner/pallas_call | solution.py:166
  85.1 2.4 %collective-permute-done.7.rest_0_.far = f32[1,512,128]{2,1,0:T(8,128)S(1)} collective-permute-done((f32[1,512,128]{2,1,0:T(8,128)S(1)}, f32[1,512,128]{2,1,0:T(8,128)S(1)}, u32[]{:S(2)}, u32[]{:S(2)}) %collective-permute-start.7) | collective-permute-done | bytes 262176 | tf_op jit(solution)/shard_map/ppermute | solution.py:275
  88.2 3.1 %collective-permute-start.26 = (f32[1,512,128]{2,1,0:T(8,128)S(1)}, f32[1,512,128]{2,1,0:T(8,128)S(1)}, u32[]{:S(2)}, u32[]{:S(2)}) collective-permute-start(f32[1,512,128]{2,1,0:T(8,128)S(1)} %combine.26.own), channel_id=1, source_target_pairs={{0,8},{4,12},{8,0},{12,4},{16,24},{20,28},{24,16},{28,20},{1,9},{5... | collective-permute-start | bytes 786440 | tf_op jit(solution)/shard_map/ppermute | solution.py:275
  96.6 2.1 %inner.11 = (f32[2,512,1024]{2,1,0:T(8,128)}, f32[8,128]{1,0:T(8,128)S(1)}) custom-call(s32[1]{0:T(128)} %bitcast.me, f32[8,512,4]{2,1,0:T(8,128)S(1)} %copy-done.1, bf16[512,512]{1,0:T(8,128)(2,1)S(1)} %copy-done.2, bf16[512,512]{1,0:T(8,128)(2,1)S(1)} %copy-done.3, bf16[512,512]{1,0:T(8,128)(2,1)S(1)} %copy-done.4, ...), custom_call_target="tpu_custom_call", output_to_operand_aliasing={{0}: (8, {})} | custom-call | tf_op jit(solution)/shard_map/inner/pallas_call | solution.py:166
  98.8 3.5 %collective-permute-done.8.rest_0_.far = f32[1,512,128]{2,1,0:T(8,128)S(1)} collective-permute-done((f32[1,512,128]{2,1,0:T(8,128)S(1)}, f32[1,512,128]{2,1,0:T(8,128)S(1)}, u32[]{:S(2)}, u32[]{:S(2)}) %collective-permute-start.8) | collective-permute-done | bytes 262176 | tf_op jit(solution)/shard_map/ppermute | solution.py:275
  106.7 2.5 %collective-permute-start.23 = (f32[1,512,128]{2,1,0:T(8,128)S(1)}, f32[1,512,128]{2,1,0:T(8,128)S(1)}, u32[]{:S(2)}, u32[]{:S(2)}) collective-permute-start(f32[1,512,128]{2,1,0:T(8,128)S(1)} %combine.25.rest_0_), channel_id=1, source_target_pairs={{0,8},{4,12},{8,0},{12,4},{16,24},{20,28},{24,16},{28,20},{1,9},{5... | collective-permute-start | bytes 786440 | tf_op jit(solution)/shard_map/ppermute | solution.py:275
  110.8 2.1 %inner.12 = (f32[2,512,1024]{2,1,0:T(8,128)}, f32[8,128]{1,0:T(8,128)S(1)}) custom-call(s32[1]{0:T(128)} %bitcast.me, f32[8,512,4]{2,1,0:T(8,128)S(1)} %copy-done.1, bf16[512,512]{1,0:T(8,128)(2,1)S(1)} %copy-done.2, bf16[512,512]{1,0:T(8,128)(2,1)S(1)} %copy-done.3, bf16[512,512]{1,0:T(8,128)(2,1)S(1)} %copy-done.4, ...), custom_call_target="tpu_custom_call", output_to_operand_aliasing={{0}: (8, {})} | custom-call | tf_op jit(solution)/shard_map/inner/pallas_call | solution.py:166
  112.9 7.1 %collective-permute-done.9.far = f32[1,512,128]{2,1,0:T(8,128)S(1)} collective-permute-done((f32[1,512,128]{2,1,0:T(8,128)S(1)}, f32[1,512,128]{2,1,0:T(8,128)S(1)}, u32[]{:S(2)}, u32[]{:S(2)}) %collective-permute-start.9) | collective-permute-done | bytes 262176 | tf_op jit(solution)/shard_map/ppermute | solution.py:275
  124.2 2.1 %inner.13 = (f32[2,512,1024]{2,1,0:T(8,128)}, f32[8,128]{1,0:T(8,128)}) custom-call(s32[1]{0:T(128)} %bitcast.me, f32[8,512,4]{2,1,0:T(8,128)S(1)} %copy-done.1, bf16[512,512]{1,0:T(8,128)(2,1)S(1)} %copy-done.2, bf16[512,512]{1,0:T(8,128)(2,1)S(1)} %copy-done.3, bf16[512,512]{1,0:T(8,128)(2,1)S(1)} %copy-done.4, ...), custom_call_target="tpu_custom_call", output_to_operand_aliasing={{0}: (8, {})} | custom-call | tf_op jit(solution)/shard_map/inner/pallas_call | solution.py:166
  126.4 4.6 %collective-permute-done.24.rest_2_ = f32[1,512,128]{2,1,0:T(8,128)S(1)} collective-permute-done((f32[1,512,128]{2,1,0:T(8,128)S(1)}, f32[1,512,128]{2,1,0:T(8,128)S(1)}, u32[]{:S(2)}, u32[]{:S(2)}) %collective-permute-start.24) | collective-permute-done | bytes 262176 | tf_op jit(solution)/shard_map/ppermute | solution.py:275
  131.0 2.6 %inner.14 = (f32[2,512,1024]{2,1,0:T(8,128)}, f32[8,128]{1,0:T(8,128)}) custom-call(s32[1]{0:T(128)} %bitcast.me, f32[8,512,8]{2,1,0:T(8,128)S(1)} %copy-done.6, bf16[512,512]{1,0:T(8,128)(2,1)S(1)} %copy-done.2, bf16[512,512]{1,0:T(8,128)(2,1)S(1)} %copy-done.3, bf16[512,512]{1,0:T(8,128)(2,1)S(1)} %copy-done.4, ...), custom_call_target="tpu_custom_call", output_to_operand_aliasing={{0}: (10, {})} | custom-call | tf_op jit(solution)/shard_map/inner/pallas_call | solution.py:166
  133.6 8.1 %collective-permute-done.21.rest_2_ = f32[1,512,128]{2,1,0:T(8,128)S(1)} collective-permute-done((f32[1,512,128]{2,1,0:T(8,128)S(1)}, f32[1,512,128]{2,1,0:T(8,128)S(1)}, u32[]{:S(2)}, u32[]{:S(2)}) %collective-permute-start.21) | collective-permute-done | bytes 262176 | tf_op jit(solution)/shard_map/ppermute | solution.py:275
  141.7 2.6 %inner.15 = (f32[2,512,1024]{2,1,0:T(8,128)}, f32[8,128]{1,0:T(8,128)}) custom-call(s32[1]{0:T(128)} %bitcast.me, f32[8,512,8]{2,1,0:T(8,128)S(1)} %copy-done.6, bf16[512,512]{1,0:T(8,128)(2,1)S(1)} %copy-done.2, bf16[512,512]{1,0:T(8,128)(2,1)S(1)} %copy-done.3, bf16[512,512]{1,0:T(8,128)(2,1)S(1)} %copy-done.4, ...), custom_call_target="tpu_custom_call", output_to_operand_aliasing={{0}: (10, {})} | custom-call | tf_op jit(solution)/shard_map/inner/pallas_call | solution.py:166
  (98 shorter events, 40.7 us)
Async XLA Ops:
  2.5 16.3 %collective-permute-start.2 = (f32[1,512,128]{2,1,0:T(8,128)}, f32[1,512,128]{2,1,0:T(8,128)S(1)}, u32[]{:S(2)}, u32[]{:S(2)}) collective-permute-start(f32[1,512,128]{2,1,0:T(8,128)} %stencil.15.own), channel_id=1, source_target_pairs={{0,16},{4,20},{8,24},{12,28},{16,0},{20,4},{24,8},{28,12},{1,17},{... | collective-permute-start | bytes 786440 | tf_op jit(solution)/shard_map/ppermute | solution.py:275
  18.8 14.1 %collective-permute-start.3 = (f32[1,512,128]{2,1,0:T(8,128)S(1)}, f32[1,512,128]{2,1,0:T(8,128)S(1)}, u32[]{:S(2)}, u32[]{:S(2)}) collective-permute-start(f32[1,512,128]{2,1,0:T(8,128)S(1)} %gate.7.own), channel_id=1, source_target_pairs={{0,16},{4,20},{8,24},{12,28},{16,0},{20,4},{24,8},{28,12},{1,17},{... | collective-permute-start | bytes 786440 | tf_op jit(solution)/shard_map/ppermute | solution.py:275
  19.5 14.2 %collective-permute-start.12 = (f32[1,512,128]{2,1,0:T(8,128)S(1)}, f32[1,512,128]{2,1,0:T(8,128)S(1)}, u32[]{:S(2)}, u32[]{:S(2)}) collective-permute-start(f32[1,512,128]{2,1,0:T(8,128)S(1)} %combine.16.own), channel_id=1, source_target_pairs={{0,8},{4,12},{8,0},{12,4},{16,24},{20,28},{24,16},{28,20},{1,9},{5... | collective-permute-start | bytes 786440 | tf_op jit(solution)/shard_map/ppermute | solution.py:275
  34.4 25.0 %collective-permute-start.13 = (f32[2,512,128]{2,1,0:T(8,128)S(1)}, f32[2,512,128]{2,1,0:T(8,128)S(1)}, u32[]{:S(2)}, u32[]{:S(2)}) collective-permute-start(f32[2,512,128]{2,1,0:T(8,128)S(1)} %combine.17.rest_0_), channel_id=1, source_target_pairs={{0,4},{4,0},{8,12},{12,8},{16,20},{20,16},{24,28},{28,24},{1,5},{5... | collective-permute-start | bytes 1572872 | tf_op jit(solution)/shard_map/ppermute | solution.py:275
  46.1 13.3 %collective-permute-start.5 = (f32[1,512,128]{2,1,0:T(8,128)S(1)}, f32[1,512,128]{2,1,0:T(8,128)S(1)}, u32[]{:S(2)}, u32[]{:S(2)}) collective-permute-start(f32[1,512,128]{2,1,0:T(8,128)S(1)} %gate.9.rest_0_.own), channel_id=1, source_target_pairs={{0,16},{4,20},{8,24},{12,28},{16,0},{20,4},{24,8},{28,12},{1,17},{... | collective-permute-start | bytes 786440 | tf_op jit(solution)/shard_map/ppermute | solution.py:275
  49.3 24.7 %collective-permute-start.11 = (f32[2,512,128]{2,1,0:T(8,128)S(1)}, f32[2,512,128]{2,1,0:T(8,128)S(1)}, u32[]{:S(2)}, u32[]{:S(2)}) collective-permute-start(f32[2,512,128]{2,1,0:T(8,128)S(1)} %combine.15.rest_0_), channel_id=1, source_target_pairs={{0,4},{4,0},{8,12},{12,8},{16,20},{20,16},{24,28},{28,24},{1,5},{5... | collective-permute-start | bytes 1572872 | tf_op jit(solution)/shard_map/ppermute | solution.py:275
  50.5 14.8 %collective-permute-start.15 = (f32[1,512,128]{2,1,0:T(8,128)S(1)}, f32[1,512,128]{2,1,0:T(8,128)S(1)}, u32[]{:S(2)}, u32[]{:S(2)}) collective-permute-start(f32[1,512,128]{2,1,0:T(8,128)S(1)} %combine.19.own), channel_id=1, source_target_pairs={{0,8},{4,12},{8,0},{12,4},{16,24},{20,28},{24,16},{28,20},{1,9},{5... | collective-permute-start | bytes 786440 | tf_op jit(solution)/shard_map/ppermute | solution.py:275
  59.4 14.6 %collective-permute-start.6 = (f32[1,512,128]{2,1,0:T(8,128)S(1)}, f32[1,512,128]{2,1,0:T(8,128)S(1)}, u32[]{:S(2)}, u32[]{:S(2)}) collective-permute-start(f32[1,512,128]{2,1,0:T(8,128)S(1)} %gate.10.own.rest_0_), channel_id=1, source_target_pairs={{0,16},{4,20},{8,24},{12,28},{16,0},{20,4},{24,8},{28,12},{1,17},{... | collective-permute-start | bytes 786440 | tf_op jit(solution)/shard_map/ppermute | solution.py:275
  62.2 14.7 %collective-permute-start.18 = (f32[1,512,128]{2,1,0:T(8,128)S(1)}, f32[1,512,128]{2,1,0:T(8,128)S(1)}, u32[]{:S(2)}, u32[]{:S(2)}) collective-permute-start(f32[1,512,128]{2,1,0:T(8,128)S(1)} %combine.22.own), channel_id=1, source_target_pairs={{0,8},{4,12},{8,0},{12,4},{16,24},{20,28},{24,16},{28,20},{1,9},{5... | collective-permute-start | bytes 786440 | tf_op jit(solution)/shard_map/ppermute | solution.py:275
  66.0 17.0 %collective-permute-start.16 = (f32[2,512,128]{2,1,0:T(8,128)S(1)}, f32[2,512,128]{2,1,0:T(8,128)S(1)}, u32[]{:S(2)}, u32[]{:S(2)}) collective-permute-start(f32[2,512,128]{2,1,0:T(8,128)S(1)} %combine.20.rest_0_), channel_id=1, source_target_pairs={{0,4},{4,0},{8,12},{12,8},{16,20},{20,16},{24,28},{28,24},{1,5},{5... | collective-permute-start | bytes 1572872 | tf_op jit(solution)/shard_map/ppermute | solution.py:275
  66.6 13.7 %collective-permute-start.1 = (f32[512,128]{1,0:T(8,128)S(1)}, f32[512,128]{1,0:T(8,128)S(1)}, u32[]{:S(2)}, u32[]{:S(2)}) collective-permute-start(f32[512,128]{1,0:T(8,128)S(1)} %get-tuple-element.31), channel_id=1, source_target_pairs={{0,1},{1,2},{2,3},{4,5},{5,6},{6,7},{8,9},{9,10},{10,11},{12,13},{... | collective-permute-start | bytes 786440 | tf_op jit(solution)/shard_map/ppermute | solution.py:253
  74.0 13.5 %collective-permute-start.7 = (f32[1,512,128]{2,1,0:T(8,128)S(1)}, f32[1,512,128]{2,1,0:T(8,128)S(1)}, u32[]{:S(2)}, u32[]{:S(2)}) collective-permute-start(f32[1,512,128]{2,1,0:T(8,128)S(1)} %gate.11.rest_0_.own), channel_id=1, source_target_pairs={{0,16},{4,20},{8,24},{12,28},{16,0},{20,4},{24,8},{28,12},{1,17},{... | collective-permute-start | bytes 786440 | tf_op jit(solution)/shard_map/ppermute | solution.py:275
  77.6 19.0 %collective-permute-start.19 = (f32[2,512,128]{2,1,0:T(8,128)S(1)}, f32[2,512,128]{2,1,0:T(8,128)S(1)}, u32[]{:S(2)}, u32[]{:S(2)}) collective-permute-start(f32[2,512,128]{2,1,0:T(8,128)S(1)} %combine.23.rest_0_), channel_id=1, source_target_pairs={{0,4},{4,0},{8,12},{12,8},{16,20},{20,16},{24,28},{28,24},{1,5},{5... | collective-permute-start | bytes 1572872 | tf_op jit(solution)/shard_map/ppermute | solution.py:275
  78.2 17.3 %collective-permute-start = (f32[512,128]{1,0:T(8,128)S(1)}, f32[512,128]{1,0:T(8,128)S(1)}, u32[]{:S(2)}, u32[]{:S(2)}) collective-permute-start(f32[512,128]{1,0:T(8,128)S(1)} %get-tuple-element.32), channel_id=1, source_target_pairs={{1,0},{2,1},{3,2},{5,4},{6,5},{7,6},{9,8},{10,9},{11,10},{13,12},{... | collective-permute-start | bytes 786440 | tf_op jit(solution)/shard_map/ppermute | solution.py:254
  87.5 14.8 %collective-permute-start.8 = (f32[1,512,128]{2,1,0:T(8,128)S(1)}, f32[1,512,128]{2,1,0:T(8,128)S(1)}, u32[]{:S(2)}, u32[]{:S(2)}) collective-permute-start(f32[1,512,128]{2,1,0:T(8,128)S(1)} %gate.12.rest_0_.own), channel_id=1, source_target_pairs={{0,16},{4,20},{8,24},{12,28},{16,0},{20,4},{24,8},{28,12},{1,17},{... | collective-permute-start | bytes 786440 | tf_op jit(solution)/shard_map/ppermute | solution.py:275
  88.2 16.1 %collective-permute-start.26 = (f32[1,512,128]{2,1,0:T(8,128)S(1)}, f32[1,512,128]{2,1,0:T(8,128)S(1)}, u32[]{:S(2)}, u32[]{:S(2)}) collective-permute-start(f32[1,512,128]{2,1,0:T(8,128)S(1)} %combine.26.own), channel_id=1, source_target_pairs={{0,8},{4,12},{8,0},{12,4},{16,24},{20,28},{24,16},{28,20},{1,9},{5... | collective-permute-start | bytes 786440 | tf_op jit(solution)/shard_map/ppermute | solution.py:275
  94.0 16.8 %collective-permute-start.17 = (f32[2,512,128]{2,1,0:T(8,128)S(1)}, f32[2,512,128]{2,1,0:T(8,128)S(1)}, u32[]{:S(2)}, u32[]{:S(2)}) collective-permute-start(f32[2,512,128]{2,1,0:T(8,128)S(1)} %combine.21.rest_0_), channel_id=1, source_target_pairs={{0,4},{4,0},{8,12},{12,8},{16,20},{20,16},{24,28},{28,24},{1,5},{5... | collective-permute-start | bytes 1572872 | tf_op jit(solution)/shard_map/ppermute | solution.py:275
  104.9 18.5 %collective-permute-start.27 = (f32[2,512,128]{2,1,0:T(8,128)S(1)}, f32[2,512,128]{2,1,0:T(8,128)S(1)}, u32[]{:S(2)}, u32[]{:S(2)}) collective-permute-start(f32[2,512,128]{2,1,0:T(8,128)S(1)} %combine.27.rest_0_), channel_id=1, source_target_pairs={{0,4},{4,0},{8,12},{12,8},{16,20},{20,16},{24,28},{28,24},{1,5},{5... | collective-permute-start | bytes 1572872 | tf_op jit(solution)/shard_map/ppermute | solution.py:275
  105.9 14.1 %collective-permute-start.9 = (f32[1,512,128]{2,1,0:T(8,128)S(1)}, f32[1,512,128]{2,1,0:T(8,128)S(1)}, u32[]{:S(2)}, u32[]{:S(2)}) collective-permute-start(f32[1,512,128]{2,1,0:T(8,128)S(1)} %gate.13.own.rest_0_), channel_id=1, source_target_pairs={{0,16},{4,20},{8,24},{12,28},{16,0},{20,4},{24,8},{28,12},{1,17},{... | collective-permute-start | bytes 786440 | tf_op jit(solution)/shard_map/ppermute | solution.py:275
  106.7 15.2 %collective-permute-start.23 = (f32[1,512,128]{2,1,0:T(8,128)S(1)}, f32[1,512,128]{2,1,0:T(8,128)S(1)}, u32[]{:S(2)}, u32[]{:S(2)}) collective-permute-start(f32[1,512,128]{2,1,0:T(8,128)S(1)} %combine.25.rest_0_), channel_id=1, source_target_pairs={{0,8},{4,12},{8,0},{12,4},{16,24},{20,28},{24,16},{28,20},{1,9},{5... | collective-permute-start | bytes 786440 | tf_op jit(solution)/shard_map/ppermute | solution.py:275
  109.2 21.8 %collective-permute-start.24 = (f32[1,512,128]{2,1,0:T(8,128)S(1)}, f32[1,512,128]{2,1,0:T(8,128)S(1)}, u32[]{:S(2)}, u32[]{:S(2)}) collective-permute-start(f32[1,512,128]{2,1,0:T(8,128)S(1)} %combine.25.rest_0_), channel_id=1, source_target_pairs={{0,4},{4,0},{8,12},{12,8},{16,20},{20,16},{24,28},{28,24},{1,5},{5... | collective-permute-start | bytes 786440 | tf_op jit(solution)/shard_map/ppermute | solution.py:275
  110.8 20.3 %collective-permute-start.25 = (f32[1,512,128]{2,1,0:T(8,128)S(1)}, f32[1,512,128]{2,1,0:T(8,128)S(1)}, u32[]{:S(2)}, u32[]{:S(2)}) collective-permute-start(f32[1,512,128]{2,1,0:T(8,128)S(1)} %combine.25.rest_0_), channel_id=1, source_target_pairs={{0,12},{4,8},{8,4},{12,0},{16,28},{20,24},{24,20},{28,16},{1,13},{... | collective-permute-start | bytes 786440 | tf_op jit(solution)/shard_map/ppermute | solution.py:275
  121.9 19.8 %collective-permute-start.21 = (f32[1,512,128]{2,1,0:T(8,128)S(1)}, f32[1,512,128]{2,1,0:T(8,128)S(1)}, u32[]{:S(2)}, u32[]{:S(2)}) collective-permute-start(f32[1,512,128]{2,1,0:T(8,128)S(1)} %combine.24.rest_0_), channel_id=1, source_target_pairs={{0,4},{4,0},{8,12},{12,8},{16,20},{20,16},{24,28},{28,24},{1,5},{5... | collective-permute-start | bytes 786440 | tf_op jit(solution)/shard_map/ppermute | solution.py:275
  123.4 18.3 %collective-permute-start.22 = (f32[1,512,128]{2,1,0:T(8,128)S(1)}, f32[1,512,128]{2,1,0:T(8,128)S(1)}, u32[]{:S(2)}, u32[]{:S(2)}) collective-permute-start(f32[1,512,128]{2,1,0:T(8,128)S(1)} %combine.24.rest_0_), channel_id=1, source_target_pairs={{0,12},{4,8},{8,4},{12,0},{16,28},{20,24},{24,20},{28,16},{1,13},{... | collective-permute-start | bytes 786440 | tf_op jit(solution)/shard_map/ppermute | solution.py:275
  (18 other events, 189.5 us)

commit v6 on v5

--- a/solution.py
+++ b/solution.py
@@ -11,15 +11,9 @@
 
 TAPS = 4
 LANES = 128
-DIRECT = 2
+DIRECT = (-1,)
 SIZES = (1, 1, 1, 1, 1, 1)
-ORDER = {
-    "stencil": [],
-    "gate": [("arrived", -1)],
-    "first": [("inner", -3)],
-    "middle": [("stencil", 2), ("inner", -2)],
-    "inner": [],
-}
+ORDER = {'stencil': [], 'gate': [('arrived', -1)], 'first': [('inner', -3), ('middle', -1)], 'middle': [('stencil', 2), ('inner', -2)], 'inner': [('middle', 1)]}
 MIB = 1024 * 1024
 VMEM = 20 * MIB
 GATE_VMEM = 1 * MIB
@@ -62,7 +56,7 @@
         band = jnp.where(tap_at == tap, coef[tap : tap + 1, :], band)
     field = jnp.concatenate([left[...], mid[...], right[...]], axis=1)
     window = jnp.broadcast_to(apod[...], (LANES, rows)).T
-    out[0] = window * dot3(split_bf16(field), split_bf16(band))
+    out[...] = window * dot3(split_bf16(field), split_bf16(band))
 
 
 def stencil(left, mid, right, apod, coef, fine, offsets, block, count, after, vmem=VMEM):
@@ -82,8 +76,8 @@
             columns(1, block),
         ]
         + [pl.BlockSpec(memory_space=pl.ANY)] * len(after),
-        out_specs=pl.BlockSpec((1, rows, LANES), lambda i: (0, 0, i)),
-        out_shape=jax.ShapeDtypeStruct((1, rows, count * LANES), jnp.float32),
+        out_specs=pl.BlockSpec((rows, LANES), lambda i: (0, i)),
+        out_shape=jax.ShapeDtypeStruct((rows, count * LANES), jnp.float32),
         compiler_params=pltpu.CompilerParams(vmem_limit_bytes=vmem),
         cost_estimate=QUICK,
         name="stencil",
@@ -108,31 +102,34 @@
     )(value, *after)
 
 
-def combine_kernel(me, factors, own, far, *rest):
-    out = rest[-1]
+def combine_kernel(parts_in, parts_out, me, factors, *refs):
+    own, far, out = refs[:parts_in], refs[parts_in : 2 * parts_in], refs[-parts_out:]
     a_re, a_im, b_re, b_im = (factors[me[0], i] for i in range(4))
-    if own.shape[0] == 2:
-        out[0] = a_re * own[0] - a_im * own[1] + (b_re * far[0] - b_im * far[1])
-        out[1] = a_re * own[1] + a_im * own[0] + (b_re * far[1] + b_im * far[0])
-    elif out.shape[0] == 2:
-        out[0] = a_re * own[0] + b_re * far[0]
-        out[1] = a_im * own[0] + b_im * far[0]
-    else:
-        out[0] = a_re * own[0] + b_re * far[0]
+    real = a_re * own[0][...] + b_re * far[0][...]
+    if parts_in == 2:
+        real -= a_im * own[1][...] + b_im * far[1][...]
+    out[0][...] = real
+    if parts_out == 2:
+        imag = a_im * own[0][...] + b_im * far[0][...]
+        if parts_in == 2:
+            imag += a_re * own[1][...] + b_re * far[1][...]
+        out[1][...] = imag
 
 
 def combine(me, factors, own, far, number, after):
     whole = pl.BlockSpec(memory_space=pltpu.VMEM)
     small = pl.BlockSpec(memory_space=pltpu.SMEM)
     return pl.pallas_call(
-        combine_kernel,
-        in_specs=[small, small, whole, whole] + [pl.BlockSpec(memory_space=pl.ANY)] * len(after),
-        out_specs=whole,
-        out_shape=jax.ShapeDtypeStruct((number,) + own.shape[1:], jnp.float32),
+        functools.partial(combine_kernel, len(own), number),
+        in_specs=[small, small]
+        + [whole] * (2 * len(own))
+        + [pl.BlockSpec(memory_space=pl.ANY)] * len(after),
+        out_specs=[whole] * number,
+        out_shape=[jax.ShapeDtypeStruct(own[0].shape, jnp.float32)] * number,
         compiler_params=pltpu.CompilerParams(vmem_limit_bytes=VMEM),
         cost_estimate=QUICK,
         name="combine",
-    )(me, factors, own, far, *after)
+    )(me, factors, *own, *far, *after)
 
 
 def inner_kernel(count, me, factors, cos_high, cos_low, sin_high, sin_low, *rest):
@@ -140,11 +137,8 @@
     y_re = y_im = 0.0
     for i, block in enumerate(rest[:count]):
         f_re, f_im = (factors[0, :, 2 * i + j : 2 * i + j + 1] for j in range(2))
-        y_re += f_re * block[0]
-        y_im += f_im * block[0]
-        if block.shape[0] == 2:
-            y_re -= f_im * block[1]
-            y_im += f_re * block[1]
+        y_re += f_re * block[...]
+        y_im += f_im * block[...]
     both = split_bf16(jnp.concatenate([y_re, y_im], axis=1))
     cos_part = dot3((cos_high[...], cos_low[...]), both)
     sin_part = dot3((sin_high[...], sin_low[...]), both)
@@ -154,13 +148,13 @@
 
 
 def inner(me, factors, tables, blocks, result, block, full_width, after):
-    number, rows, width = blocks[0].shape
+    rows, width = blocks[0].shape
     kept = [] if result is None else [result]
     inputs = [me, factors, *tables, *blocks, *after, *kept]
     specs = (
         [pl.BlockSpec((1,) + factors.shape[1:], lambda i, at: (at[0], 0, 0))]
         + [pl.BlockSpec((rows, rows), lambda i, at: (0, 0))] * 4
-        + [pl.BlockSpec((number, rows, LANES), lambda i, at: (0, 0, i))] * len(blocks)
+        + [pl.BlockSpec((rows, LANES), lambda i, at: (0, i))] * len(blocks)
         + [pl.BlockSpec(memory_space=pl.ANY)] * (len(after) + len(kept))
     )
     return pl.pallas_call(
@@ -260,25 +254,32 @@
     factors = [jnp.asarray(parts(own, far)) for _, own, far, _, _ in stages[:-1]]
     _, own, far, _, phase = stages[-1]
     own, far = (own * phase)[:, None] * twiddle, (far * phase)[:, None] * twiddle
-    factors.append(jnp.asarray(parts(own, far)))
+    numbers = [1] + [2 if stages[s + 1][3] else 1 for s in range(levels - 1)]
+
+    def by_part(values, number):
+        return jnp.asarray(parts(*(v * 1j**i for v in values for i in range(number))))
+
+    factors.append(by_part([own, far], numbers[levels - 1]))
     half, near_own, near_far = stages[-2][:3]
     flip = np.arange(devices) ^ stages[-1][0]
     direct = [own * near_own[:, None], own * near_far[:, None]]
     direct += [far * near_own[flip, None], far * near_far[flip, None]]
     partners = [half, stages[-1][0], half ^ stages[-1][0]]
-    factors.append(jnp.asarray(parts(*direct)))
-    numbers = [2 if stages[s + 1][3] else 1 for s in range(levels - 1)]
-
+    factors.append(by_part(direct, numbers[levels - 2]))
     chunks = column_chunks(count)
 
-    def send(value, half):
-        return lax.ppermute(value, "row", [(a, a ^ half) for a in range(devices)])
+    def send(values, half, stage):
+        groups = [range(devices), stages[stage][3]]
+        return [
+            lax.ppermute(value, "row", [(a, a ^ half) for a in group])
+            for value, group in zip(values, groups)
+        ]
 
     out, far, results = {}, {}, {}
     stage_of = {"stencil": 0, "first": 1, "middle": levels - 1, "inner": levels}
 
     def is_direct(chunk):
-        return chunk >= len(chunks) - DIRECT
+        return chunk in DIRECT or chunk - len(chunks) in DIRECT
 
     def after(name, chunk):
         kept = []
@@ -287,10 +288,10 @@
             if 0 <= at < len(chunks):
                 if what == "arrived":
                     make(0, at)
-                    kept.append(far[0, at][0])
+                    kept += far[0, at][0]
                 elif stage_of[what] != levels - 1 or not is_direct(at):
                     make(stage_of[what], at)
-                    kept.append(out[stage_of[what], at])
+                    kept += out[stage_of[what], at][-1:]
         return kept
 
     def make(stage, chunk):
@@ -300,7 +301,7 @@
         if stage == 0:
             left = (before, 0) if block == 0 else (signal, block - 1)
             right = (behind, 0) if block == count - 1 else (signal, block + 1)
-            out[stage, chunk] = stencil(
+            field = stencil(
                 left,
                 (signal, block),
                 right,
@@ -314,8 +315,7 @@
                 VMEM if chunk else FIRST_VMEM,
             )
             waits = after("gate", chunk)
-            if waits:
-                out[stage, chunk] = gate(out[stage, chunk], waits)
+            out[stage, chunk] = [gate(field, waits) if waits else field]
         else:
             source = levels - 2 if stage == levels and is_direct(chunk) else stage - 1
             make(source, chunk)
@@ -326,25 +326,26 @@
                     factors[stage - 1],
                     near,
                     there[0],
-                    numbers[stage - 1],
+                    numbers[stage],
                     after("first" if stage == 1 else "middle", chunk),
                 )
             else:
                 if chunk:
                     make(stage, chunk - 1)
-                results[chunk], out[stage, chunk] = inner(
+                results[chunk], token = inner(
                     me,
                     factors[len(there) // 2 + levels - 1],
                     tables,
-                    [near, *there],
+                    [part for group in (near, *there) for part in group],
                     results.get(chunk - 1),
                     block,
                     width,
                     after("inner", chunk),
                 )
+                out[stage, chunk] = [token]
         if stage < levels:
             ways = partners if stage == levels - 2 and is_direct(chunk) else [stages[stage][0]]
-            far[stage, chunk] = [send(out[stage, chunk], half) for half in ways]
+            far[stage, chunk] = [send(out[stage, chunk], half, stage) for half in ways]
 
     make(levels, len(chunks) - 1)
     return results[len(chunks) - 1]

time: 144 us -> 146 us (1.014); the launches traced: 144 us -> 144 us
  waiting for transfers between devices: 74.9 us -> 65.6 us
  starting transfers between devices: 31.9 us -> 37.4 us
  Pallas kernels: 37 us -> 40.3 us
    ppermute x26 -> x32, waiting for transfers between devices: 74.9 us -> 65.6 us  [send(): lax.ppermute(value, 'row', [(a, a ^ half) for a in group])]
    ppermute x26 -> x32, starting transfers between devices: 29.2 us -> 34.8 us  [send(): lax.ppermute(value, 'row', [(a, a ^ half) for a in group])]
    pallas_call x8, Pallas kernels: 17.9 us -> 20.4 us  [inner(): pl.pallas_call(functools.partial(inner_kernel, len(blocks)), grid_spec=pl...]
    pallas_call x14 -> x15, Pallas kernels: 9.15 us -> 9.84 us  [combine(): pl.pallas_call(functools.partial(combine_kernel, len(own), number), in_sp...]
  transfers between devices with their start and end apart: 28 -> 34, of which waited for: 16 -> 15; matrix products, arithmetic and copies ran while one was open for 0% -> 0% of each run, Pallas kernels for 22% -> 24%
where the time goes in v6:
time: 146 us; the launch traced here: 144 us
  waiting for transfers between devices  65.6 us (45%)
  Pallas kernels  40.3 us (28%)
  starting transfers between devices  37.4 us (26%)
    ppermute x32, waiting for transfers between devices, send(): lax.ppermute(value, 'row', [(a, a ^ half) for a in group])  65.6 us
    ppermute x32, starting transfers between devices, send(): lax.ppermute(value, 'row', [(a, a ^ half) for a in group])  34.8 us
    pallas_call x8, Pallas kernels, inner(): pl.pallas_call(functools.partial(inner_kernel, len(blocks)), grid_spec=pl...  20.4 us
    pallas_call x8, Pallas kernels, stencil(): pl.pallas_call(functools.partial(stencil_kernel, block, width // offsets....  10 us
    pallas_call x15, Pallas kernels, combine(): pl.pallas_call(functools.partial(combine_kernel, len(own), number), in_sp...  9.84 us
  transfers between devices with their start and end apart: 34, of which 15 were waited for; matrix products, arithmetic and copies ran while one was open for 0% of the time, Pallas kernels for 24%

profile of v6, /device:TPU:0, one launch (start us, length us, event | category | flops | bytes accessed | tf_op | source)
XLA Modules:
  0.0 143.8 jit_solution(6469348126508137108)
XLA Ops:
  0.0 2.5 %stencil.15.refs_0_ = f32[512,128]{1,0:T(8,128)} custom-call(s32[32]{0:T(128)} %offsets.15, f32[512,1024]{1,0:T(8,128)} %right.13, f32[512,1024]{1,0:T(8,128)} %right.13, f32[512,1024]{1,0:T(8,128)} %right.13, f32[1,512]{1,0:T(1,128)} %bitcast.11, f32[4,1024]{1,0:T(4,128)} %coef.15, s32[1,1024]{1,0:T(1,128)} %bitcast.3), custom_call_target="tpu_custom_call" | custom-call | tf_op jit(solution)/shard_map/stencil/pallas_call | solution.py:68
  2.5 4.1 %collective-permute-start.2 = (f32[512,128]{1,0:T(8,128)}, f32[512,128]{1,0:T(8,128)S(1)}, u32[]{:S(2)}, u32[]{:S(2)}) collective-permute-start(f32[512,128]{1,0:T(8,128)} %stencil.15.refs_0_), channel_id=1, source_target_pairs={{0,16},{4,20},{8,24},{12,28},{16,0},{20,4},{24,8},{28,12},{1,17},{... | collective-permute-start | bytes 786440 | tf_op jit(solution)/shard_map/ppermute | solution.py:274
  7.7 11.1 %collective-permute-done.2.rest_0_.refs_1_ = f32[512,128]{1,0:T(8,128)S(1)} collective-permute-done((f32[512,128]{1,0:T(8,128)}, f32[512,128]{1,0:T(8,128)S(1)}, u32[]{:S(2)}, u32[]{:S(2)}) %collective-permute-start.2) | collective-permute-done | bytes 262176 | tf_op jit(solution)/shard_map/ppermute | solution.py:274
  19.5 4.1 %collective-permute-start.10 = (f32[512,128]{1,0:T(8,128)S(1)}, f32[512,128]{1,0:T(8,128)S(1)}, u32[]{:S(2)}, u32[]{:S(2)}) collective-permute-start(f32[512,128]{1,0:T(8,128)S(1)} %combine.15.refs_0_), channel_id=1, source_target_pairs={{0,8},{4,12},{8,0},{12,4},{16,24},{20,28},{24,16},{28,20},{1,9},{5... | collective-permute-start | bytes 786440 | tf_op jit(solution)/shard_map/ppermute | solution.py:274
  24.6 8.3 %collective-permute-done.3.rest_0_.refs_1_ = f32[512,128]{1,0:T(8,128)S(1)} collective-permute-done((f32[512,128]{1,0:T(8,128)S(1)}, f32[512,128]{1,0:T(8,128)S(1)}, u32[]{:S(2)}, u32[]{:S(2)}) %collective-permute-start.3) | collective-permute-done | bytes 262176 | tf_op jit(solution)/shard_map/ppermute | solution.py:274
  39.0 7.1 %collective-permute-done.4.rest_0_.refs_1_ = f32[512,128]{1,0:T(8,128)S(1)} collective-permute-done((f32[512,128]{1,0:T(8,128)S(1)}, f32[512,128]{1,0:T(8,128)S(1)}, u32[]{:S(2)}, u32[]{:S(2)}) %collective-permute-start.4) | collective-permute-done | bytes 262176 | tf_op jit(solution)/shard_map/ppermute | solution.py:274
  52.1 2.6 %inner.8 = (f32[2,512,1024]{2,1,0:T(8,128)}, f32[8,128]{1,0:T(8,128)S(1)}) custom-call(s32[1]{0:T(128)} %bitcast.me, f32[8,512,8]{2,1,0:T(8,128)S(1)} %copy-done.1, bf16[512,512]{1,0:T(8,128)(2,1)S(1)} %copy-done.2, bf16[512,512]{1,0:T(8,128)(2,1)S(1)} %copy-done.3, bf16[512,512]{1,0:T(8,128)(2,1)S(1)} %copy-done.4, bf16[512,512]{1,0:T(8,128)(2,1)S(1)} %copy-done.5, ...), custom_call_target="tpu_custom_call" | custom-call | tf_op jit(solution)/shard_map/inner/pallas_call | solution.py:160
  54.6 4.9 %collective-permute-done.5.rest_0_.refs_1_ = f32[512,128]{1,0:T(8,128)S(1)} collective-permute-done((f32[512,128]{1,0:T(8,128)S(1)}, f32[512,128]{1,0:T(8,128)S(1)}, u32[]{:S(2)}, u32[]{:S(2)}) %collective-permute-start.5) | collective-permute-done | bytes 262176 | tf_op jit(solution)/shard_map/ppermute | solution.py:274
  67.7 2.5 %inner.9 = (f32[2,512,1024]{2,1,0:T(8,128)}, f32[8,128]{1,0:T(8,128)S(1)}) custom-call(s32[1]{0:T(128)} %bitcast.me, f32[8,512,8]{2,1,0:T(8,128)S(1)} %copy-done.1, bf16[512,512]{1,0:T(8,128)(2,1)S(1)} %copy-done.2, bf16[512,512]{1,0:T(8,128)(2,1)S(1)} %copy-done.3, bf16[512,512]{1,0:T(8,128)(2,1)S(1)} %copy-done.4, ...), custom_call_target="tpu_custom_call", output_to_operand_aliasing={{0}: (11, {})} | custom-call | tf_op jit(solution)/shard_map/inner/pallas_call | solution.py:160
  70.2 3.9 %collective-permute-done.6.rest_0_.refs_1_ = f32[512,128]{1,0:T(8,128)S(1)} collective-permute-done((f32[512,128]{1,0:T(8,128)S(1)}, f32[512,128]{1,0:T(8,128)S(1)}, u32[]{:S(2)}, u32[]{:S(2)}) %collective-permute-start.6) | collective-permute-done | bytes 262176 | tf_op jit(solution)/shard_map/ppermute | solution.py:274
  74.1 2.3 %collective-permute-start.7 = (f32[512,128]{1,0:T(8,128)S(1)}, f32[512,128]{1,0:T(8,128)S(1)}, u32[]{:S(2)}, u32[]{:S(2)}) collective-permute-start(f32[512,128]{1,0:T(8,128)S(1)} %gate.11.refs_2_.refs_0_), channel_id=1, source_target_pairs={{0,16},{4,20},{8,24},{12,28},{16,0},{20,4},{24,8},{28,12},{1,17},{... | collective-permute-start | bytes 786440 | tf_op jit(solution)/shard_map/ppermute | solution.py:274
  82.5 2.5 %inner.10 = (f32[2,512,1024]{2,1,0:T(8,128)}, f32[8,128]{1,0:T(8,128)S(1)}) custom-call(s32[1]{0:T(128)} %bitcast.me, f32[8,512,8]{2,1,0:T(8,128)S(1)} %copy-done.1, bf16[512,512]{1,0:T(8,128)(2,1)S(1)} %copy-done.2, bf16[512,512]{1,0:T(8,128)(2,1)S(1)} %copy-done.3, bf16[512,512]{1,0:T(8,128)(2,1)S(1)} %copy-done.4, ...), custom_call_target="tpu_custom_call", output_to_operand_aliasing={{0}: (11, {})} | custom-call | tf_op jit(solution)/shard_map/inner/pallas_call | solution.py:160
  85.1 3.6 %collective-permute-done.7.rest_0_.refs_1_ = f32[512,128]{1,0:T(8,128)S(1)} collective-permute-done((f32[512,128]{1,0:T(8,128)S(1)}, f32[512,128]{1,0:T(8,128)S(1)}, u32[]{:S(2)}, u32[]{:S(2)}) %collective-permute-start.7) | collective-permute-done | bytes 262176 | tf_op jit(solution)/shard_map/ppermute | solution.py:274
  88.7 3.0 %collective-permute-start.8 = (f32[512,128]{1,0:T(8,128)S(1)}, f32[512,128]{1,0:T(8,128)S(1)}, u32[]{:S(2)}, u32[]{:S(2)}) collective-permute-start(f32[512,128]{1,0:T(8,128)S(1)} %gate.12.refs_2_.refs_0_), channel_id=1, source_target_pairs={{0,16},{4,20},{8,24},{12,28},{16,0},{20,4},{24,8},{28,12},{1,17},{... | collective-permute-start | bytes 786440 | tf_op jit(solution)/shard_map/ppermute | solution.py:274
  97.1 2.6 %inner.11 = (f32[2,512,1024]{2,1,0:T(8,128)}, f32[8,128]{1,0:T(8,128)S(1)}) custom-call(s32[1]{0:T(128)} %bitcast.me, f32[8,512,8]{2,1,0:T(8,128)S(1)} %copy-done.1, bf16[512,512]{1,0:T(8,128)(2,1)S(1)} %copy-done.2, bf16[512,512]{1,0:T(8,128)(2,1)S(1)} %copy-done.3, bf16[512,512]{1,0:T(8,128)(2,1)S(1)} %copy-done.4, ...), custom_call_target="tpu_custom_call", output_to_operand_aliasing={{0}: (11, {})} | custom-call | tf_op jit(solution)/shard_map/inner/pallas_call | solution.py:160
  99.7 4.3 %collective-permute-done.8.rest_0_.refs_1_ = f32[512,128]{1,0:T(8,128)S(1)} collective-permute-done((f32[512,128]{1,0:T(8,128)S(1)}, f32[512,128]{1,0:T(8,128)S(1)}, u32[]{:S(2)}, u32[]{:S(2)}) %collective-permute-start.8) | collective-permute-done | bytes 262176 | tf_op jit(solution)/shard_map/ppermute | solution.py:274
  104.0 3.5 %collective-permute-done.23.refs_1_ = f32[512,128]{1,0:T(8,128)S(1)} collective-permute-done((f32[512,128]{1,0:T(8,128)S(1)}, f32[512,128]{1,0:T(8,128)S(1)}, u32[]{:S(2)}, u32[]{:S(2)}) %collective-permute-start.23) | collective-permute-done | bytes 262176 | tf_op jit(solution)/shard_map/ppermute | solution.py:274
  111.3 2.6 %inner.12 = (f32[2,512,1024]{2,1,0:T(8,128)}, f32[8,128]{1,0:T(8,128)S(1)}) custom-call(s32[1]{0:T(128)} %bitcast.me, f32[8,512,8]{2,1,0:T(8,128)S(1)} %copy-done.1, bf16[512,512]{1,0:T(8,128)(2,1)S(1)} %copy-done.2, bf16[512,512]{1,0:T(8,128)(2,1)S(1)} %copy-done.3, bf16[512,512]{1,0:T(8,128)(2,1)S(1)} %copy-done.4, ...), custom_call_target="tpu_custom_call", output_to_operand_aliasing={{0}: (11, {})} | custom-call | tf_op jit(solution)/shard_map/inner/pallas_call | solution.py:160
  113.8 8.2 %collective-permute-done.26.refs_1_ = f32[512,128]{1,0:T(8,128)S(1)} collective-permute-done((f32[512,128]{1,0:T(8,128)S(1)}, f32[512,128]{1,0:T(8,128)S(1)}, u32[]{:S(2)}, u32[]{:S(2)}) %collective-permute-start.26) | collective-permute-done | bytes 262176 | tf_op jit(solution)/shard_map/ppermute | solution.py:274
  128.2 2.6 %inner.13 = (f32[2,512,1024]{2,1,0:T(8,128)}, f32[8,128]{1,0:T(8,128)}) custom-call(s32[1]{0:T(128)} %bitcast.me, f32[8,512,8]{2,1,0:T(8,128)S(1)} %copy-done.1, bf16[512,512]{1,0:T(8,128)(2,1)S(1)} %copy-done.2, bf16[512,512]{1,0:T(8,128)(2,1)S(1)} %copy-done.3, bf16[512,512]{1,0:T(8,128)(2,1)S(1)} %copy-done.4, ...), custom_call_target="tpu_custom_call", output_to_operand_aliasing={{0}: (11, {})} | custom-call | tf_op jit(solution)/shard_map/inner/pallas_call | solution.py:160
  130.7 3.1 %collective-permute-done.30.rest_2_ = f32[512,128]{1,0:T(8,128)S(1)} collective-permute-done((f32[512,128]{1,0:T(8,128)S(1)}, f32[512,128]{1,0:T(8,128)S(1)}, u32[]{:S(2)}, u32[]{:S(2)}) %collective-permute-start.30) | collective-permute-done | bytes 262176 | tf_op jit(solution)/shard_map/ppermute | solution.py:274
  133.9 2.6 %inner.14 = (f32[2,512,1024]{2,1,0:T(8,128)}, f32[8,128]{1,0:T(8,128)}) custom-call(s32[1]{0:T(128)} %bitcast.me, f32[8,512,8]{2,1,0:T(8,128)S(1)} %copy-done.1, bf16[512,512]{1,0:T(8,128)(2,1)S(1)} %copy-done.2, bf16[512,512]{1,0:T(8,128)(2,1)S(1)} %copy-done.3, bf16[512,512]{1,0:T(8,128)(2,1)S(1)} %copy-done.4, ...), custom_call_target="tpu_custom_call", output_to_operand_aliasing={{0}: (10, {})} | custom-call | tf_op jit(solution)/shard_map/inner/pallas_call | solution.py:160
  136.4 4.8 %collective-permute-done.28.rest_2_ = f32[512,128]{1,0:T(8,128)S(1)} collective-permute-done((f32[512,128]{1,0:T(8,128)S(1)}, f32[512,128]{1,0:T(8,128)S(1)}, u32[]{:S(2)}, u32[]{:S(2)}) %collective-permute-start.28) | collective-permute-done | bytes 262176 | tf_op jit(solution)/shard_map/ppermute | solution.py:274
  141.2 2.5 %inner.15 = (f32[2,512,1024]{2,1,0:T(8,128)}, f32[8,128]{1,0:T(8,128)}) custom-call(s32[1]{0:T(128)} %bitcast.me, f32[8,512,8]{2,1,0:T(8,128)S(1)} %copy-done.6, bf16[512,512]{1,0:T(8,128)(2,1)S(1)} %copy-done.2, bf16[512,512]{1,0:T(8,128)(2,1)S(1)} %copy-done.3, bf16[512,512]{1,0:T(8,128)(2,1)S(1)} %copy-done.4, ...), custom_call_target="tpu_custom_call", output_to_operand_aliasing={{0}: (10, {})} | custom-call | tf_op jit(solution)/shard_map/inner/pallas_call | solution.py:160
  (111 shorter events, 44.2 us)
Async XLA Ops:
  2.5 16.3 %collective-permute-start.2 = (f32[512,128]{1,0:T(8,128)}, f32[512,128]{1,0:T(8,128)S(1)}, u32[]{:S(2)}, u32[]{:S(2)}) collective-permute-start(f32[512,128]{1,0:T(8,128)} %stencil.15.refs_0_), channel_id=1, source_target_pairs={{0,16},{4,20},{8,24},{12,28},{16,0},{20,4},{24,8},{28,12},{1,17},{... | collective-permute-start | bytes 786440 | tf_op jit(solution)/shard_map/ppermute | solution.py:274
  18.8 14.1 %collective-permute-start.3 = (f32[512,128]{1,0:T(8,128)S(1)}, f32[512,128]{1,0:T(8,128)S(1)}, u32[]{:S(2)}, u32[]{:S(2)}) collective-permute-start(f32[512,128]{1,0:T(8,128)S(1)} %gate.7.refs_0_), channel_id=1, source_target_pairs={{0,16},{4,20},{8,24},{12,28},{16,0},{20,4},{24,8},{28,12},{1,17},{... | collective-permute-start | bytes 786440 | tf_op jit(solution)/shard_map/ppermute | solution.py:274
  19.5 14.2 %collective-permute-start.10 = (f32[512,128]{1,0:T(8,128)S(1)}, f32[512,128]{1,0:T(8,128)S(1)}, u32[]{:S(2)}, u32[]{:S(2)}) collective-permute-start(f32[512,128]{1,0:T(8,128)S(1)} %combine.15.refs_0_), channel_id=1, source_target_pairs={{0,8},{4,12},{8,0},{12,4},{16,24},{20,28},{24,16},{28,20},{1,9},{5... | collective-permute-start | bytes 786440 | tf_op jit(solution)/shard_map/ppermute | solution.py:274
  36.1 15.0 %collective-permute-start.15 = (f32[512,128]{1,0:T(8,128)S(1)}, f32[512,128]{1,0:T(8,128)S(1)}, u32[]{:S(2)}, u32[]{:S(2)}) collective-permute-start(f32[512,128]{1,0:T(8,128)S(1)} %get-tuple-element.35.rest_0_), channel_id=1, source_target_pairs={{0,4},{4,0},{8,12},{12,8},{16,20},{20,16},{24,28},{28,24},{1,5},{5... | collective-permute-start | bytes 786440 | tf_op jit(solution)/shard_map/ppermute | solution.py:274
  37.3 14.8 %collective-permute-start.16 = (f32[512,128]{1,0:T(8,128)S(1)}, f32[512,128]{1,0:T(8,128)S(1)}, u32[]{:S(2)}, u32[]{:S(2)}) collective-permute-start(f32[512,128]{1,0:T(8,128)S(1)} %get-tuple-element.32.refs_2_.rest_1_), channel_id=1, source_target_pairs={{16,20},{20,16},{24,28},{28,24},{17,21},{21,17},{25,29},{29,25},{1... | collective-permute-start | bytes 786440 | tf_op jit(solution)/shard_map/ppermute | solution.py:274
  50.4 16.7 %collective-permute-start.13 = (f32[512,128]{1,0:T(8,128)S(1)}, f32[512,128]{1,0:T(8,128)S(1)}, u32[]{:S(2)}, u32[]{:S(2)}) collective-permute-start(f32[512,128]{1,0:T(8,128)S(1)} %get-tuple-element.34.refs_2_.rest_4_.rest_1_), channel_id=1, source_target_pairs={{16,20},{20,16},{24,28},{28,24},{17,21},{21,17},{25,29},{29,25},{1... | collective-permute-start | bytes 786440 | tf_op jit(solution)/shard_map/ppermute | solution.py:274
  51.1 15.3 %collective-permute-start.12 = (f32[512,128]{1,0:T(8,128)S(1)}, f32[512,128]{1,0:T(8,128)S(1)}, u32[]{:S(2)}, u32[]{:S(2)}) collective-permute-start(f32[512,128]{1,0:T(8,128)S(1)} %get-tuple-element.33.rest_0_), channel_id=1, source_target_pairs={{0,4},{4,0},{8,12},{12,8},{16,20},{20,16},{24,28},{28,24},{1,5},{5... | collective-permute-start | bytes 786440 | tf_op jit(solution)/shard_map/ppermute | solution.py:274
  59.5 14.6 %collective-permute-start.6 = (f32[512,128]{1,0:T(8,128)S(1)}, f32[512,128]{1,0:T(8,128)S(1)}, u32[]{:S(2)}, u32[]{:S(2)}) collective-permute-start(f32[512,128]{1,0:T(8,128)S(1)} %gate.10.refs_2_.refs_0_), channel_id=1, source_target_pairs={{0,16},{4,20},{8,24},{12,28},{16,0},{20,4},{24,8},{28,12},{1,17},{... | collective-permute-start | bytes 786440 | tf_op jit(solution)/shard_map/ppermute | solution.py:274
  62.5 13.9 %collective-permute-start.17 = (f32[512,128]{1,0:T(8,128)S(1)}, f32[512,128]{1,0:T(8,128)S(1)}, u32[]{:S(2)}, u32[]{:S(2)}) collective-permute-start(f32[512,128]{1,0:T(8,128)S(1)} %combine.21.refs_0_), channel_id=1, source_target_pairs={{0,8},{4,12},{8,0},{12,4},{16,24},{20,28},{24,16},{28,20},{1,9},{5... | collective-permute-start | bytes 786440 | tf_op jit(solution)/shard_map/ppermute | solution.py:274
  66.4 14.5 %collective-permute-start.20 = (f32[512,128]{1,0:T(8,128)S(1)}, f32[512,128]{1,0:T(8,128)S(1)}, u32[]{:S(2)}, u32[]{:S(2)}) collective-permute-start(f32[512,128]{1,0:T(8,128)S(1)} %get-tuple-element.37.rest_4_.refs_3_.rest_1_), channel_id=1, source_target_pairs={{16,20},{20,16},{24,28},{28,24},{17,21},{21,17},{25,29},{29,25},{1... | collective-permute-start | bytes 786440 | tf_op jit(solution)/shard_map/ppermute | solution.py:274
  74.1 14.6 %collective-permute-start.7 = (f32[512,128]{1,0:T(8,128)S(1)}, f32[512,128]{1,0:T(8,128)S(1)}, u32[]{:S(2)}, u32[]{:S(2)}) collective-permute-start(f32[512,128]{1,0:T(8,128)S(1)} %gate.11.refs_2_.refs_0_), channel_id=1, source_target_pairs={{0,16},{4,20},{8,24},{12,28},{16,0},{20,4},{24,8},{28,12},{1,17},{... | collective-permute-start | bytes 786440 | tf_op jit(solution)/shard_map/ppermute | solution.py:274
  77.7 14.3 %collective-permute-start.18 = (f32[512,128]{1,0:T(8,128)S(1)}, f32[512,128]{1,0:T(8,128)S(1)}, u32[]{:S(2)}, u32[]{:S(2)}) collective-permute-start(f32[512,128]{1,0:T(8,128)S(1)} %combine.23.refs_0_), channel_id=1, source_target_pairs={{0,8},{4,12},{8,0},{12,4},{16,24},{20,28},{24,16},{28,20},{1,9},{5... | collective-permute-start | bytes 786440 | tf_op jit(solution)/shard_map/ppermute | solution.py:274
  77.8 15.6 %collective-permute-start = (f32[512,128]{1,0:T(8,128)S(1)}, f32[512,128]{1,0:T(8,128)S(1)}, u32[]{:S(2)}, u32[]{:S(2)}) collective-permute-start(f32[512,128]{1,0:T(8,128)S(1)} %get-tuple-element.60), channel_id=1, source_target_pairs={{1,0},{2,1},{3,2},{5,4},{6,5},{7,6},{9,8},{10,9},{11,10},{13,12},{... | collective-permute-start | bytes 786440 | tf_op jit(solution)/shard_map/ppermute | solution.py:248
  80.2 16.9 %collective-permute-start.25 = (f32[512,128]{1,0:T(8,128)S(1)}, f32[512,128]{1,0:T(8,128)S(1)}, u32[]{:S(2)}, u32[]{:S(2)}) collective-permute-start(f32[512,128]{1,0:T(8,128)S(1)} %get-tuple-element.40.refs_3_.rest_4_.rest_1_), channel_id=1, source_target_pairs={{16,20},{20,16},{24,28},{28,24},{17,21},{21,17},{25,29},{29,25},{1... | collective-permute-start | bytes 786440 | tf_op jit(solution)/shard_map/ppermute | solution.py:274
  80.9 15.3 %collective-permute-start.24 = (f32[512,128]{1,0:T(8,128)S(1)}, f32[512,128]{1,0:T(8,128)S(1)}, u32[]{:S(2)}, u32[]{:S(2)}) collective-permute-start(f32[512,128]{1,0:T(8,128)S(1)} %get-tuple-element.46.rest_0_), channel_id=1, source_target_pairs={{0,4},{4,0},{8,12},{12,8},{16,20},{20,16},{24,28},{28,24},{1,5},{5... | collective-permute-start | bytes 786440 | tf_op jit(solution)/shard_map/ppermute | solution.py:274
  88.7 15.3 %collective-permute-start.8 = (f32[512,128]{1,0:T(8,128)S(1)}, f32[512,128]{1,0:T(8,128)S(1)}, u32[]{:S(2)}, u32[]{:S(2)}) collective-permute-start(f32[512,128]{1,0:T(8,128)S(1)} %gate.12.refs_2_.refs_0_), channel_id=1, source_target_pairs={{0,16},{4,20},{8,24},{12,28},{16,0},{20,4},{24,8},{28,12},{1,17},{... | collective-permute-start | bytes 786440 | tf_op jit(solution)/shard_map/ppermute | solution.py:274
  93.4 14.1 %collective-permute-start.23 = (f32[512,128]{1,0:T(8,128)S(1)}, f32[512,128]{1,0:T(8,128)S(1)}, u32[]{:S(2)}, u32[]{:S(2)}) collective-permute-start(f32[512,128]{1,0:T(8,128)S(1)} %combine.25.refs_0_), channel_id=1, source_target_pairs={{0,8},{4,12},{8,0},{12,4},{16,24},{20,28},{24,16},{28,20},{1,9},{5... | collective-permute-start | bytes 786440 | tf_op jit(solution)/shard_map/ppermute | solution.py:274
  93.5 17.1 %collective-permute-start.21 = (f32[512,128]{1,0:T(8,128)S(1)}, f32[512,128]{1,0:T(8,128)S(1)}, u32[]{:S(2)}, u32[]{:S(2)}) collective-permute-start(f32[512,128]{1,0:T(8,128)S(1)} %get-tuple-element.44.rest_0_), channel_id=1, source_target_pairs={{0,4},{4,0},{8,12},{12,8},{16,20},{20,16},{24,28},{28,24},{1,5},{5... | collective-permute-start | bytes 786440 | tf_op jit(solution)/shard_map/ppermute | solution.py:274
  96.2 15.0 %collective-permute-start.22 = (f32[512,128]{1,0:T(8,128)S(1)}, f32[512,128]{1,0:T(8,128)S(1)}, u32[]{:S(2)}, u32[]{:S(2)}) collective-permute-start(f32[512,128]{1,0:T(8,128)S(1)} %get-tuple-element.45.refs_3_.rest_4_.rest_1_), channel_id=1, source_target_pairs={{16,20},{20,16},{24,28},{28,24},{17,21},{21,17},{25,29},{29,25},{1... | collective-permute-start | bytes 786440 | tf_op jit(solution)/shard_map/ppermute | solution.py:274
  108.9 15.1 %collective-permute-start.9 = (f32[512,128]{1,0:T(8,128)S(1)}, f32[512,128]{1,0:T(8,128)S(1)}, u32[]{:S(2)}, u32[]{:S(2)}) collective-permute-start(f32[512,128]{1,0:T(8,128)S(1)} %gate.13.refs_2_.refs_0_), channel_id=1, source_target_pairs={{0,16},{4,20},{8,24},{12,28},{16,0},{20,4},{24,8},{28,12},{1,17},{... | collective-permute-start | bytes 786440 | tf_op jit(solution)/shard_map/ppermute | solution.py:274
  109.2 15.5 %collective-permute-start.32 = (f32[512,128]{1,0:T(8,128)S(1)}, f32[512,128]{1,0:T(8,128)S(1)}, u32[]{:S(2)}, u32[]{:S(2)}) collective-permute-start(f32[512,128]{1,0:T(8,128)S(1)} %get-tuple-element.54.rest_0_), channel_id=1, source_target_pairs={{0,4},{4,0},{8,12},{12,8},{16,20},{20,16},{24,28},{28,24},{1,5},{5... | collective-permute-start | bytes 786440 | tf_op jit(solution)/shard_map/ppermute | solution.py:274
  110.6 15.7 %collective-permute-start.33 = (f32[512,128]{1,0:T(8,128)S(1)}, f32[512,128]{1,0:T(8,128)S(1)}, u32[]{:S(2)}, u32[]{:S(2)}) collective-permute-start(f32[512,128]{1,0:T(8,128)S(1)} %get-tuple-element.49.rest_4_.refs_3_.rest_1_), channel_id=1, source_target_pairs={{16,20},{20,16},{24,28},{28,24},{17,21},{21,17},{25,29},{29,25},{1... | collective-permute-start | bytes 786440 | tf_op jit(solution)/shard_map/ppermute | solution.py:274
  124.7 16.5 %collective-permute-start.28 = (f32[512,128]{1,0:T(8,128)S(1)}, f32[512,128]{1,0:T(8,128)S(1)}, u32[]{:S(2)}, u32[]{:S(2)}) collective-permute-start(f32[512,128]{1,0:T(8,128)S(1)} %combine.29.rest_0_), channel_id=1, source_target_pairs={{0,4},{4,0},{8,12},{12,8},{16,20},{20,16},{24,28},{28,24},{1,5},{5... | collective-permute-start | bytes 786440 | tf_op jit(solution)/shard_map/ppermute | solution.py:274
  126.3 14.9 %collective-permute-start.29 = (f32[512,128]{1,0:T(8,128)S(1)}, f32[512,128]{1,0:T(8,128)S(1)}, u32[]{:S(2)}, u32[]{:S(2)}) collective-permute-start(f32[512,128]{1,0:T(8,128)S(1)} %combine.29.rest_0_), channel_id=1, source_target_pairs={{0,12},{4,8},{8,4},{12,0},{16,28},{20,24},{24,20},{28,16},{1,13},{... | collective-permute-start | bytes 786440 | tf_op jit(solution)/shard_map/ppermute | solution.py:274
  (24 other events, 242.8 us)

commit v7 on v5

--- a/solution.py
+++ b/solution.py
@@ -13,13 +13,7 @@
 LANES = 128
 DIRECT = 2
 SIZES = (1, 1, 1, 1, 1, 1)
-ORDER = {
-    "stencil": [],
-    "gate": [("arrived", -1)],
-    "first": [("inner", -3)],
-    "middle": [("stencil", 2), ("inner", -2)],
-    "inner": [],
-}
+ORDER = {'stencil': [], 'gate': [('arrived', -1)], 'first': [('inner', -3), ('middle', -1)], 'middle': [('stencil', 2)], 'inner': [('middle', 1)]}
 MIB = 1024 * 1024
 VMEM = 20 * MIB
 GATE_VMEM = 1 * MIB

time: 144 us -> 147 us (1.021)
  waiting for transfers between devices: 74.9 us -> 81.1 us
  starting transfers between devices: 31.9 us -> 28.5 us
    ppermute x26, waiting for transfers between devices: 74.9 us -> 81.1 us  [send(): return lax.ppermute(value, 'row', [(a, a ^ half) for a in range(devices)])]
    ppermute x26, starting transfers between devices: 29.2 us -> 25.7 us  [send(): return lax.ppermute(value, 'row', [(a, a ^ half) for a in range(devices)])]
  transfers between devices with their start and end apart: 28 -> 28, of which waited for: 16 -> 18; matrix products, arithmetic and copies ran while one was open for 0% -> 0% of each run, Pallas kernels for 22% -> 22%
where the time goes in v7:
time: 147 us
  waiting for transfers between devices  81.1 us (55%)
  Pallas kernels  37 us (25%)
  starting transfers between devices  28.5 us (19%)
    ppermute x26, waiting for transfers between devices, send(): return lax.ppermute(value, 'row', [(a, a ^ half) for a in range(devices)])  81.1 us
    ppermute x26, starting transfers between devices, send(): return lax.ppermute(value, 'row', [(a, a ^ half) for a in range(devices)])  25.7 us
    pallas_call x8, Pallas kernels, inner(): pl.pallas_call(functools.partial(inner_kernel, len(blocks)), grid_spec=pl...  17.9 us
    pallas_call x8, Pallas kernels, stencil(): pl.pallas_call(functools.partial(stencil_kernel, block, width // offsets....  10 us
    pallas_call x14, Pallas kernels, combine(): pl.pallas_call(combine_kernel, in_specs=[small, small, whole, whole] + [p...  9.15 us
  transfers between devices with their start and end apart: 28, of which 18 were waited for; matrix products, arithmetic and copies ran while one was open for 0% of the time, Pallas kernels for 22%

profile of v7, /device:TPU:0, one launch (start us, length us, event | category | flops | bytes accessed | tf_op | source)
XLA Modules:
  0.0 147.0 jit_solution(70143592658000138)
XLA Ops:
  0.0 2.5 %stencil.15.own = f32[1,512,128]{2,1,0:T(8,128)} custom-call(s32[32]{0:T(128)} %offsets.15, f32[512,1024]{1,0:T(8,128)} %right.13, f32[512,1024]{1,0:T(8,128)} %right.13, f32[512,1024]{1,0:T(8,128)} %right.13, f32[1,512]{1,0:T(1,128)} %bitcast.11, f32[4,1024]{1,0:T(4,128)} %coef.15, s32[1,1024]{1,0:T(1,128)} %bitcast.3), custom_call_target="tpu_custom_call" | custom-call | tf_op jit(solution)/shard_map/stencil/pallas_call | solution.py:68
  2.5 4.1 %collective-permute-start.2 = (f32[1,512,128]{2,1,0:T(8,128)}, f32[1,512,128]{2,1,0:T(8,128)S(1)}, u32[]{:S(2)}, u32[]{:S(2)}) collective-permute-start(f32[1,512,128]{2,1,0:T(8,128)} %stencil.15.own), channel_id=1, source_target_pairs={{0,16},{4,20},{8,24},{12,28},{16,0},{20,4},{24,8},{28,12},{1,17},{... | collective-permute-start | bytes 786440 | tf_op jit(solution)/shard_map/ppermute | solution.py:269
  7.7 11.1 %collective-permute-done.2.rest_0_.far = f32[1,512,128]{2,1,0:T(8,128)S(1)} collective-permute-done((f32[1,512,128]{2,1,0:T(8,128)}, f32[1,512,128]{2,1,0:T(8,128)S(1)}, u32[]{:S(2)}, u32[]{:S(2)}) %collective-permute-start.2) | collective-permute-done | bytes 262176 | tf_op jit(solution)/shard_map/ppermute | solution.py:269
  19.5 4.1 %collective-permute-start.10 = (f32[1,512,128]{2,1,0:T(8,128)S(1)}, f32[1,512,128]{2,1,0:T(8,128)S(1)}, u32[]{:S(2)}, u32[]{:S(2)}) collective-permute-start(f32[1,512,128]{2,1,0:T(8,128)S(1)} %combine.14.own), channel_id=1, source_target_pairs={{0,8},{4,12},{8,0},{12,4},{16,24},{20,28},{24,16},{28,20},{1,9},{5... | collective-permute-start | bytes 786440 | tf_op jit(solution)/shard_map/ppermute | solution.py:269
  24.6 8.3 %collective-permute-done.3.rest_0_.far = f32[1,512,128]{2,1,0:T(8,128)S(1)} collective-permute-done((f32[1,512,128]{2,1,0:T(8,128)S(1)}, f32[1,512,128]{2,1,0:T(8,128)S(1)}, u32[]{:S(2)}, u32[]{:S(2)}) %collective-permute-start.3) | collective-permute-done | bytes 262176 | tf_op jit(solution)/shard_map/ppermute | solution.py:269
  38.3 7.7 %collective-permute-done.4.rest_0_.far = f32[1,512,128]{2,1,0:T(8,128)S(1)} collective-permute-done((f32[1,512,128]{2,1,0:T(8,128)S(1)}, f32[1,512,128]{2,1,0:T(8,128)S(1)}, u32[]{:S(2)}, u32[]{:S(2)}) %collective-permute-start.4) | collective-permute-done | bytes 262176 | tf_op jit(solution)/shard_map/ppermute | solution.py:269
  51.3 8.1 %collective-permute-done.5.rest_0_.far = f32[1,512,128]{2,1,0:T(8,128)S(1)} collective-permute-done((f32[1,512,128]{2,1,0:T(8,128)S(1)}, f32[1,512,128]{2,1,0:T(8,128)S(1)}, u32[]{:S(2)}, u32[]{:S(2)}) %collective-permute-start.5) | collective-permute-done | bytes 262176 | tf_op jit(solution)/shard_map/ppermute | solution.py:269
  61.8 2.1 %inner.8 = (f32[2,512,1024]{2,1,0:T(8,128)}, f32[8,128]{1,0:T(8,128)S(1)}) custom-call(s32[1]{0:T(128)} %bitcast.me, f32[8,512,4]{2,1,0:T(8,128)S(1)} %copy-done.1, bf16[512,512]{1,0:T(8,128)(2,1)S(1)} %copy-done.2, bf16[512,512]{1,0:T(8,128)(2,1)S(1)} %copy-done.3, bf16[512,512]{1,0:T(8,128)(2,1)S(1)} %copy-done.4, bf16[512,512]{1,0:T(8,128)(2,1)S(1)} %copy-done.5, ...), custom_call_target="tpu_custom_call" | custom-call | tf_op jit(solution)/shard_map/inner/pallas_call | solution.py:160
  69.0 5.0 %collective-permute-done.6.rest_0_.far = f32[1,512,128]{2,1,0:T(8,128)S(1)} collective-permute-done((f32[1,512,128]{2,1,0:T(8,128)S(1)}, f32[1,512,128]{2,1,0:T(8,128)S(1)}, u32[]{:S(2)}, u32[]{:S(2)}) %collective-permute-start.6) | collective-permute-done | bytes 262176 | tf_op jit(solution)/shard_map/ppermute | solution.py:269
  74.0 3.7 %collective-permute-done.15.far = f32[1,512,128]{2,1,0:T(8,128)S(1)} collective-permute-done((f32[1,512,128]{2,1,0:T(8,128)S(1)}, f32[1,512,128]{2,1,0:T(8,128)S(1)}, u32[]{:S(2)}, u32[]{:S(2)}) %collective-permute-start.15) | collective-permute-done | bytes 262176 | tf_op jit(solution)/shard_map/ppermute | solution.py:269
  78.4 2.1 %inner.9 = (f32[2,512,1024]{2,1,0:T(8,128)}, f32[8,128]{1,0:T(8,128)S(1)}) custom-call(s32[1]{0:T(128)} %bitcast.me, f32[8,512,4]{2,1,0:T(8,128)S(1)} %copy-done.1, bf16[512,512]{1,0:T(8,128)(2,1)S(1)} %copy-done.2, bf16[512,512]{1,0:T(8,128)(2,1)S(1)} %copy-done.3, bf16[512,512]{1,0:T(8,128)(2,1)S(1)} %copy-done.4, ...), custom_call_target="tpu_custom_call", output_to_operand_aliasing={{0}: (9, {})} | custom-call | tf_op jit(solution)/shard_map/inner/pallas_call | solution.py:160
  87.6 3.4 %collective-permute-start.8 = (f32[1,512,128]{2,1,0:T(8,128)S(1)}, f32[1,512,128]{2,1,0:T(8,128)S(1)}, u32[]{:S(2)}, u32[]{:S(2)}) collective-permute-start(f32[1,512,128]{2,1,0:T(8,128)S(1)} %gate.12.rest_0_.own), channel_id=1, source_target_pairs={{0,16},{4,20},{8,24},{12,28},{16,0},{20,4},{24,8},{28,12},{1,17},{... | collective-permute-start | bytes 786440 | tf_op jit(solution)/shard_map/ppermute | solution.py:269
  90.9 2.2 %collective-permute-done.16.far = f32[1,512,128]{2,1,0:T(8,128)S(1)} collective-permute-done((f32[1,512,128]{2,1,0:T(8,128)S(1)}, f32[1,512,128]{2,1,0:T(8,128)S(1)}, u32[]{:S(2)}, u32[]{:S(2)}) %collective-permute-start.16) | collective-permute-done | bytes 262176 | tf_op jit(solution)/shard_map/ppermute | solution.py:269
  96.2 7.5 %collective-permute-done.8.rest_0_.far = f32[1,512,128]{2,1,0:T(8,128)S(1)} collective-permute-done((f32[1,512,128]{2,1,0:T(8,128)S(1)}, f32[1,512,128]{2,1,0:T(8,128)S(1)}, u32[]{:S(2)}, u32[]{:S(2)}) %collective-permute-start.8) | collective-permute-done | bytes 262176 | tf_op jit(solution)/shard_map/ppermute | solution.py:269
  103.7 4.6 %collective-permute-done.19.far = f32[1,512,128]{2,1,0:T(8,128)S(1)} collective-permute-done((f32[1,512,128]{2,1,0:T(8,128)S(1)}, f32[1,512,128]{2,1,0:T(8,128)S(1)}, u32[]{:S(2)}, u32[]{:S(2)}) %collective-permute-start.19) | collective-permute-done | bytes 262176 | tf_op jit(solution)/shard_map/ppermute | solution.py:269
  110.7 2.1 %inner.11 = (f32[2,512,1024]{2,1,0:T(8,128)}, f32[8,128]{1,0:T(8,128)S(1)}) custom-call(s32[1]{0:T(128)} %bitcast.me, f32[8,512,4]{2,1,0:T(8,128)S(1)} %copy-done.1, bf16[512,512]{1,0:T(8,128)(2,1)S(1)} %copy-done.2, bf16[512,512]{1,0:T(8,128)(2,1)S(1)} %copy-done.3, bf16[512,512]{1,0:T(8,128)(2,1)S(1)} %copy-done.4, ...), custom_call_target="tpu_custom_call", output_to_operand_aliasing={{0}: (9, {})} | custom-call | tf_op jit(solution)/shard_map/inner/pallas_call | solution.py:160
  113.4 2.5 %collective-permute-start.24 = (f32[1,512,128]{2,1,0:T(8,128)S(1)}, f32[1,512,128]{2,1,0:T(8,128)S(1)}, u32[]{:S(2)}, u32[]{:S(2)}) collective-permute-start(f32[1,512,128]{2,1,0:T(8,128)S(1)} %combine.27.rest_0_), channel_id=1, source_target_pairs={{0,8},{4,12},{8,0},{12,4},{16,24},{20,28},{24,16},{28,20},{1,9},{5... | collective-permute-start | bytes 786440 | tf_op jit(solution)/shard_map/ppermute | solution.py:269
  119.6 3.5 %collective-permute-done.9.far = f32[1,512,128]{2,1,0:T(8,128)S(1)} collective-permute-done((f32[1,512,128]{2,1,0:T(8,128)S(1)}, f32[1,512,128]{2,1,0:T(8,128)S(1)}, u32[]{:S(2)}, u32[]{:S(2)}) %collective-permute-start.9) | collective-permute-done | bytes 262176 | tf_op jit(solution)/shard_map/ppermute | solution.py:269
  123.8 3.7 %collective-permute-done.24.rest_1_ = f32[1,512,128]{2,1,0:T(8,128)S(1)} collective-permute-done((f32[1,512,128]{2,1,0:T(8,128)S(1)}, f32[1,512,128]{2,1,0:T(8,128)S(1)}, u32[]{:S(2)}, u32[]{:S(2)}) %collective-permute-start.24) | collective-permute-done | bytes 262176 | tf_op jit(solution)/shard_map/ppermute | solution.py:269
  129.2 2.1 %inner.13 = (f32[2,512,1024]{2,1,0:T(8,128)}, f32[8,128]{1,0:T(8,128)}) custom-call(s32[1]{0:T(128)} %bitcast.me, f32[8,512,4]{2,1,0:T(8,128)S(1)} %copy-done.1, bf16[512,512]{1,0:T(8,128)(2,1)S(1)} %copy-done.2, bf16[512,512]{1,0:T(8,128)(2,1)S(1)} %copy-done.3, bf16[512,512]{1,0:T(8,128)(2,1)S(1)} %copy-done.4, ...), custom_call_target="tpu_custom_call", output_to_operand_aliasing={{0}: (8, {})} | custom-call | tf_op jit(solution)/shard_map/inner/pallas_call | solution.py:160
  131.4 3.1 %collective-permute-done.25.rest_2_ = f32[1,512,128]{2,1,0:T(8,128)S(1)} collective-permute-done((f32[1,512,128]{2,1,0:T(8,128)S(1)}, f32[1,512,128]{2,1,0:T(8,128)S(1)}, u32[]{:S(2)}, u32[]{:S(2)}) %collective-permute-start.25) | collective-permute-done | bytes 262176 | tf_op jit(solution)/shard_map/ppermute | solution.py:269
  134.4 2.6 %inner.14 = (f32[2,512,1024]{2,1,0:T(8,128)}, f32[8,128]{1,0:T(8,128)}) custom-call(s32[1]{0:T(128)} %bitcast.me, f32[8,512,8]{2,1,0:T(8,128)S(1)} %copy-done.6, bf16[512,512]{1,0:T(8,128)(2,1)S(1)} %copy-done.2, bf16[512,512]{1,0:T(8,128)(2,1)S(1)} %copy-done.3, bf16[512,512]{1,0:T(8,128)(2,1)S(1)} %copy-done.4, ...), custom_call_target="tpu_custom_call", output_to_operand_aliasing={{0}: (10, {})} | custom-call | tf_op jit(solution)/shard_map/inner/pallas_call | solution.py:160
  138.8 5.7 %collective-permute-done.22.rest_2_ = f32[1,512,128]{2,1,0:T(8,128)S(1)} collective-permute-done((f32[1,512,128]{2,1,0:T(8,128)S(1)}, f32[1,512,128]{2,1,0:T(8,128)S(1)}, u32[]{:S(2)}, u32[]{:S(2)}) %collective-permute-start.22) | collective-permute-done | bytes 262176 | tf_op jit(solution)/shard_map/ppermute | solution.py:269
  144.5 2.5 %inner.15 = (f32[2,512,1024]{2,1,0:T(8,128)}, f32[8,128]{1,0:T(8,128)}) custom-call(s32[1]{0:T(128)} %bitcast.me, f32[8,512,8]{2,1,0:T(8,128)S(1)} %copy-done.6, bf16[512,512]{1,0:T(8,128)(2,1)S(1)} %copy-done.2, bf16[512,512]{1,0:T(8,128)(2,1)S(1)} %copy-done.3, bf16[512,512]{1,0:T(8,128)(2,1)S(1)} %copy-done.4, ...), custom_call_target="tpu_custom_call", output_to_operand_aliasing={{0}: (10, {})} | custom-call | tf_op jit(solution)/shard_map/inner/pallas_call | solution.py:160
  (98 shorter events, 42.2 us)
Async XLA Ops:
  2.5 16.3 %collective-permute-start.2 = (f32[1,512,128]{2,1,0:T(8,128)}, f32[1,512,128]{2,1,0:T(8,128)S(1)}, u32[]{:S(2)}, u32[]{:S(2)}) collective-permute-start(f32[1,512,128]{2,1,0:T(8,128)} %stencil.15.own), channel_id=1, source_target_pairs={{0,16},{4,20},{8,24},{12,28},{16,0},{20,4},{24,8},{28,12},{1,17},{... | collective-permute-start | bytes 786440 | tf_op jit(solution)/shard_map/ppermute | solution.py:269
  18.8 14.1 %collective-permute-start.3 = (f32[1,512,128]{2,1,0:T(8,128)S(1)}, f32[1,512,128]{2,1,0:T(8,128)S(1)}, u32[]{:S(2)}, u32[]{:S(2)}) collective-permute-start(f32[1,512,128]{2,1,0:T(8,128)S(1)} %gate.7.own), channel_id=1, source_target_pairs={{0,16},{4,20},{8,24},{12,28},{16,0},{20,4},{24,8},{28,12},{1,17},{... | collective-permute-start | bytes 786440 | tf_op jit(solution)/shard_map/ppermute | solution.py:269
  19.5 14.2 %collective-permute-start.10 = (f32[1,512,128]{2,1,0:T(8,128)S(1)}, f32[1,512,128]{2,1,0:T(8,128)S(1)}, u32[]{:S(2)}, u32[]{:S(2)}) collective-permute-start(f32[1,512,128]{2,1,0:T(8,128)S(1)} %combine.14.own), channel_id=1, source_target_pairs={{0,8},{4,12},{8,0},{12,4},{16,24},{20,28},{24,16},{28,20},{1,9},{5... | collective-permute-start | bytes 786440 | tf_op jit(solution)/shard_map/ppermute | solution.py:269
  32.9 13.2 %collective-permute-start.4 = (f32[1,512,128]{2,1,0:T(8,128)S(1)}, f32[1,512,128]{2,1,0:T(8,128)S(1)}, u32[]{:S(2)}, u32[]{:S(2)}) collective-permute-start(f32[1,512,128]{2,1,0:T(8,128)S(1)} %gate.8.rest_0_.own), channel_id=1, source_target_pairs={{0,16},{4,20},{8,24},{12,28},{16,0},{20,4},{24,8},{28,12},{1,17},{... | collective-permute-start | bytes 786440 | tf_op jit(solution)/shard_map/ppermute | solution.py:269
  36.1 25.7 %collective-permute-start.14 = (f32[2,512,128]{2,1,0:T(8,128)S(1)}, f32[2,512,128]{2,1,0:T(8,128)S(1)}, u32[]{:S(2)}, u32[]{:S(2)}) collective-permute-start(f32[2,512,128]{2,1,0:T(8,128)S(1)} %combine.15.rest_0_), channel_id=1, source_target_pairs={{0,4},{4,0},{8,12},{12,8},{16,20},{20,16},{24,28},{28,24},{1,5},{5... | collective-permute-start | bytes 1572872 | tf_op jit(solution)/shard_map/ppermute | solution.py:269
  46.1 13.3 %collective-permute-start.5 = (f32[1,512,128]{2,1,0:T(8,128)S(1)}, f32[1,512,128]{2,1,0:T(8,128)S(1)}, u32[]{:S(2)}, u32[]{:S(2)}) collective-permute-start(f32[1,512,128]{2,1,0:T(8,128)S(1)} %gate.9.rest_0_.own), channel_id=1, source_target_pairs={{0,16},{4,20},{8,24},{12,28},{16,0},{20,4},{24,8},{28,12},{1,17},{... | collective-permute-start | bytes 786440 | tf_op jit(solution)/shard_map/ppermute | solution.py:269
  49.3 29.1 %collective-permute-start.12 = (f32[2,512,128]{2,1,0:T(8,128)S(1)}, f32[2,512,128]{2,1,0:T(8,128)S(1)}, u32[]{:S(2)}, u32[]{:S(2)}) collective-permute-start(f32[2,512,128]{2,1,0:T(8,128)S(1)} %combine.17.rest_0_.rest_2_), channel_id=1, source_target_pairs={{0,4},{4,0},{8,12},{12,8},{16,20},{20,16},{24,28},{28,24},{1,5},{5... | collective-permute-start | bytes 1572872 | tf_op jit(solution)/shard_map/ppermute | solution.py:269
  59.4 14.6 %collective-permute-start.6 = (f32[1,512,128]{2,1,0:T(8,128)S(1)}, f32[1,512,128]{2,1,0:T(8,128)S(1)}, u32[]{:S(2)}, u32[]{:S(2)}) collective-permute-start(f32[1,512,128]{2,1,0:T(8,128)S(1)} %gate.10.rest_0_.own), channel_id=1, source_target_pairs={{0,16},{4,20},{8,24},{12,28},{16,0},{20,4},{24,8},{28,12},{1,17},{... | collective-permute-start | bytes 786440 | tf_op jit(solution)/shard_map/ppermute | solution.py:269
  66.0 18.4 %collective-permute-start.18 = (f32[2,512,128]{2,1,0:T(8,128)S(1)}, f32[2,512,128]{2,1,0:T(8,128)S(1)}, u32[]{:S(2)}, u32[]{:S(2)}) collective-permute-start(f32[2,512,128]{2,1,0:T(8,128)S(1)} %combine.19.rest_2_.rest_1_.rest_0_), channel_id=1, source_target_pairs={{0,4},{4,0},{8,12},{12,8},{16,20},{20,16},{24,28},{28,24},{1,5},{5... | collective-permute-start | bytes 1572872 | tf_op jit(solution)/shard_map/ppermute | solution.py:269
  66.6 16.1 %collective-permute-start.1 = (f32[512,128]{1,0:T(8,128)S(1)}, f32[512,128]{1,0:T(8,128)S(1)}, u32[]{:S(2)}, u32[]{:S(2)}) collective-permute-start(f32[512,128]{1,0:T(8,128)S(1)} %get-tuple-element.31), channel_id=1, source_target_pairs={{0,1},{1,2},{2,3},{4,5},{5,6},{6,7},{8,9},{9,10},{10,11},{12,13},{... | collective-permute-start | bytes 786440 | tf_op jit(solution)/shard_map/ppermute | solution.py:247
  74.0 13.6 %collective-permute-start.7 = (f32[1,512,128]{2,1,0:T(8,128)S(1)}, f32[1,512,128]{2,1,0:T(8,128)S(1)}, u32[]{:S(2)}, u32[]{:S(2)}) collective-permute-start(f32[1,512,128]{2,1,0:T(8,128)S(1)} %gate.11.rest_0_.own), channel_id=1, source_target_pairs={{0,16},{4,20},{8,24},{12,28},{16,0},{20,4},{24,8},{28,12},{1,17},{... | collective-permute-start | bytes 786440 | tf_op jit(solution)/shard_map/ppermute | solution.py:269
  81.3 13.8 %collective-permute-start = (f32[512,128]{1,0:T(8,128)S(1)}, f32[512,128]{1,0:T(8,128)S(1)}, u32[]{:S(2)}, u32[]{:S(2)}) collective-permute-start(f32[512,128]{1,0:T(8,128)S(1)} %get-tuple-element.32), channel_id=1, source_target_pairs={{1,0},{2,1},{3,2},{5,4},{6,5},{7,6},{9,8},{10,9},{11,10},{13,12},{... | collective-permute-start | bytes 786440 | tf_op jit(solution)/shard_map/ppermute | solution.py:248
  83.8 26.8 %collective-permute-start.20 = (f32[2,512,128]{2,1,0:T(8,128)S(1)}, f32[2,512,128]{2,1,0:T(8,128)S(1)}, u32[]{:S(2)}, u32[]{:S(2)}) collective-permute-start(f32[2,512,128]{2,1,0:T(8,128)S(1)} %combine.21.rest_1_.rest_2_.rest_0_), channel_id=1, source_target_pairs={{0,4},{4,0},{8,12},{12,8},{16,20},{20,16},{24,28},{28,24},{1,5},{5... | collective-permute-start | bytes 1572872 | tf_op jit(solution)/shard_map/ppermute | solution.py:269
  87.6 16.1 %collective-permute-start.8 = (f32[1,512,128]{2,1,0:T(8,128)S(1)}, f32[1,512,128]{2,1,0:T(8,128)S(1)}, u32[]{:S(2)}, u32[]{:S(2)}) collective-permute-start(f32[1,512,128]{2,1,0:T(8,128)S(1)} %gate.12.rest_0_.own), channel_id=1, source_target_pairs={{0,16},{4,20},{8,24},{12,28},{16,0},{20,4},{24,8},{28,12},{1,17},{... | collective-permute-start | bytes 786440 | tf_op jit(solution)/shard_map/ppermute | solution.py:269
  94.5 13.8 %collective-permute-start.19 = (f32[1,512,128]{2,1,0:T(8,128)S(1)}, f32[1,512,128]{2,1,0:T(8,128)S(1)}, u32[]{:S(2)}, u32[]{:S(2)}) collective-permute-start(f32[1,512,128]{2,1,0:T(8,128)S(1)} %combine.24.own), channel_id=1, source_target_pairs={{0,8},{4,12},{8,0},{12,4},{16,24},{20,28},{24,16},{28,20},{1,9},{5... | collective-permute-start | bytes 786440 | tf_op jit(solution)/shard_map/ppermute | solution.py:269
  94.6 22.6 %collective-permute-start.17 = (f32[2,512,128]{2,1,0:T(8,128)S(1)}, f32[2,512,128]{2,1,0:T(8,128)S(1)}, u32[]{:S(2)}, u32[]{:S(2)}) collective-permute-start(f32[2,512,128]{2,1,0:T(8,128)S(1)} %combine.23.rest_1_.rest_2_.rest_0_), channel_id=1, source_target_pairs={{0,4},{4,0},{8,12},{12,8},{16,20},{20,16},{24,28},{28,24},{1,5},{5... | collective-permute-start | bytes 1572872 | tf_op jit(solution)/shard_map/ppermute | solution.py:269
  109.0 20.2 %collective-permute-start.27 = (f32[2,512,128]{2,1,0:T(8,128)S(1)}, f32[2,512,128]{2,1,0:T(8,128)S(1)}, u32[]{:S(2)}, u32[]{:S(2)}) collective-permute-start(f32[2,512,128]{2,1,0:T(8,128)S(1)} %combine.25.rest_2_.rest_1_.rest_0_), channel_id=1, source_target_pairs={{0,4},{4,0},{8,12},{12,8},{16,20},{20,16},{24,28},{28,24},{1,5},{5... | collective-permute-start | bytes 1572872 | tf_op jit(solution)/shard_map/ppermute | solution.py:269
  109.1 14.0 %collective-permute-start.9 = (f32[1,512,128]{2,1,0:T(8,128)S(1)}, f32[1,512,128]{2,1,0:T(8,128)S(1)}, u32[]{:S(2)}, u32[]{:S(2)}) collective-permute-start(f32[1,512,128]{2,1,0:T(8,128)S(1)} %gate.13.rest_0_.own), channel_id=1, source_target_pairs={{0,16},{4,20},{8,24},{12,28},{16,0},{20,4},{24,8},{28,12},{1,17},{... | collective-permute-start | bytes 786440 | tf_op jit(solution)/shard_map/ppermute | solution.py:269
  113.4 14.1 %collective-permute-start.24 = (f32[1,512,128]{2,1,0:T(8,128)S(1)}, f32[1,512,128]{2,1,0:T(8,128)S(1)}, u32[]{:S(2)}, u32[]{:S(2)}) collective-permute-start(f32[1,512,128]{2,1,0:T(8,128)S(1)} %combine.27.rest_0_), channel_id=1, source_target_pairs={{0,8},{4,12},{8,0},{12,4},{16,24},{20,28},{24,16},{28,20},{1,9},{5... | collective-permute-start | bytes 786440 | tf_op jit(solution)/shard_map/ppermute | solution.py:269
  116.0 18.4 %collective-permute-start.25 = (f32[1,512,128]{2,1,0:T(8,128)S(1)}, f32[1,512,128]{2,1,0:T(8,128)S(1)}, u32[]{:S(2)}, u32[]{:S(2)}) collective-permute-start(f32[1,512,128]{2,1,0:T(8,128)S(1)} %combine.27.rest_0_), channel_id=1, source_target_pairs={{0,4},{4,0},{8,12},{12,8},{16,20},{20,16},{24,28},{28,24},{1,5},{5... | collective-permute-start | bytes 786440 | tf_op jit(solution)/shard_map/ppermute | solution.py:269
  117.1 17.3 %collective-permute-start.26 = (f32[1,512,128]{2,1,0:T(8,128)S(1)}, f32[1,512,128]{2,1,0:T(8,128)S(1)}, u32[]{:S(2)}, u32[]{:S(2)}) collective-permute-start(f32[1,512,128]{2,1,0:T(8,128)S(1)} %combine.27.rest_0_), channel_id=1, source_target_pairs={{0,12},{4,8},{8,4},{12,0},{16,28},{20,24},{24,20},{28,16},{1,13},{... | collective-permute-start | bytes 786440 | tf_op jit(solution)/shard_map/ppermute | solution.py:269
  123.7 15.1 %collective-permute-start.21 = (f32[1,512,128]{2,1,0:T(8,128)S(1)}, f32[1,512,128]{2,1,0:T(8,128)S(1)}, u32[]{:S(2)}, u32[]{:S(2)}) collective-permute-start(f32[1,512,128]{2,1,0:T(8,128)S(1)} %combine.26.rest_0_), channel_id=1, source_target_pairs={{0,8},{4,12},{8,0},{12,4},{16,24},{20,28},{24,16},{28,20},{1,9},{5... | collective-permute-start | bytes 786440 | tf_op jit(solution)/shard_map/ppermute | solution.py:269
  127.5 17.0 %collective-permute-start.22 = (f32[1,512,128]{2,1,0:T(8,128)S(1)}, f32[1,512,128]{2,1,0:T(8,128)S(1)}, u32[]{:S(2)}, u32[]{:S(2)}) collective-permute-start(f32[1,512,128]{2,1,0:T(8,128)S(1)} %combine.26.rest_0_), channel_id=1, source_target_pairs={{0,4},{4,0},{8,12},{12,8},{16,20},{20,16},{24,28},{28,24},{1,5},{5... | collective-permute-start | bytes 786440 | tf_op jit(solution)/shard_map/ppermute | solution.py:269
  129.2 15.3 %collective-permute-start.23 = (f32[1,512,128]{2,1,0:T(8,128)S(1)}, f32[1,512,128]{2,1,0:T(8,128)S(1)}, u32[]{:S(2)}, u32[]{:S(2)}) collective-permute-start(f32[1,512,128]{2,1,0:T(8,128)S(1)} %combine.26.rest_0_), channel_id=1, source_target_pairs={{0,12},{4,8},{8,4},{12,0},{16,28},{20,24},{24,20},{28,16},{1,13},{... | collective-permute-start | bytes 786440 | tf_op jit(solution)/shard_map/ppermute | solution.py:269
  (18 other events, 199.9 us)

commit v8 on v5

--- a/solution.py
+++ b/solution.py
@@ -11,7 +11,7 @@
 
 TAPS = 4
 LANES = 128
-DIRECT = 2
+DIRECT = 1
 SIZES = (1, 1, 1, 1, 1, 1)
 ORDER = {
     "stencil": [],
@@ -283,7 +283,7 @@
     def after(name, chunk):
         kept = []
         for what, shift in ORDER[name]:
-            at = chunk + shift
+            at = chunk + shift - (name == "gate" and chunk == len(chunks) - 1)
             if 0 <= at < len(chunks):
                 if what == "arrived":
                     make(0, at)

time: 144 us -> 148 us (1.028)
  waiting for transfers between devices: 74.9 us -> 82.4 us
  starting transfers between devices: 31.9 us -> 27.2 us
    ppermute x26 -> x25, waiting for transfers between devices: 74.9 us -> 82.4 us  [send(): return lax.ppermute(value, 'row', [(a, a ^ half) for a in range(devices)])]
    ppermute x26 -> x25, starting transfers between devices: 29.2 us -> 24.4 us  [send(): return lax.ppermute(value, 'row', [(a, a ^ half) for a in range(devices)])]
    pallas_call x14 -> x15, Pallas kernels: 9.15 us -> 9.82 us  [combine(): pl.pallas_call(combine_kernel, in_specs=[small, small, whole, whole] + [p...]
  transfers between devices with their start and end apart: 28 -> 27, of which waited for: 16 -> 15; matrix products, arithmetic and copies ran while one was open for 0% -> 0% of each run, Pallas kernels for 22% -> 22%
where the time goes in v8:
time: 148 us; the launch traced here: 147 us
  waiting for transfers between devices  82.4 us (56%)
  Pallas kernels  37.3 us (25%)
  starting transfers between devices  27.2 us (18%)
    ppermute x25, waiting for transfers between devices, send(): return lax.ppermute(value, 'row', [(a, a ^ half) for a in range(devices)])  82.4 us
    ppermute x25, starting transfers between devices, send(): return lax.ppermute(value, 'row', [(a, a ^ half) for a in range(devices)])  24.4 us
    pallas_call x8, Pallas kernels, inner(): pl.pallas_call(functools.partial(inner_kernel, len(blocks)), grid_spec=pl...  17.5 us
    pallas_call x8, Pallas kernels, stencil(): pl.pallas_call(functools.partial(stencil_kernel, block, width // offsets....  10 us
    pallas_call x15, Pallas kernels, combine(): pl.pallas_call(combine_kernel, in_specs=[small, small, whole, whole] + [p...  9.82 us
  transfers between devices with their start and end apart: 27, of which 15 were waited for; matrix products, arithmetic and copies ran while one was open for 0% of the time, Pallas kernels for 22%

profile of v8, /device:TPU:0, one launch (start us, length us, event | category | flops | bytes accessed | tf_op | source)
XLA Modules:
  0.0 147.4 jit_solution(1505237837843854904)
XLA Ops:
  0.0 2.5 %stencil.14.own = f32[1,512,128]{2,1,0:T(8,128)} custom-call(s32[32]{0:T(128)} %offsets.15, f32[512,1024]{1,0:T(8,128)} %right.13, f32[512,1024]{1,0:T(8,128)} %right.13, f32[512,1024]{1,0:T(8,128)} %right.13, f32[1,512]{1,0:T(1,128)} %bitcast.11, f32[4,1024]{1,0:T(4,128)} %coef.15, s32[1,1024]{1,0:T(1,128)} %bitcast.3), custom_call_target="tpu_custom_call" | custom-call | tf_op jit(solution)/shard_map/stencil/pallas_call | solution.py:74
  2.5 4.1 %collective-permute-start.1 = (f32[1,512,128]{2,1,0:T(8,128)}, f32[1,512,128]{2,1,0:T(8,128)S(1)}, u32[]{:S(2)}, u32[]{:S(2)}) collective-permute-start(f32[1,512,128]{2,1,0:T(8,128)} %stencil.14.own), channel_id=1, source_target_pairs={{0,16},{4,20},{8,24},{12,28},{16,0},{20,4},{24,8},{28,12},{1,17},{... | collective-permute-start | bytes 786440 | tf_op jit(solution)/shard_map/ppermute | solution.py:275
  7.7 11.1 %collective-permute-done.1.rest_0_.far = f32[1,512,128]{2,1,0:T(8,128)S(1)} collective-permute-done((f32[1,512,128]{2,1,0:T(8,128)}, f32[1,512,128]{2,1,0:T(8,128)S(1)}, u32[]{:S(2)}, u32[]{:S(2)}) %collective-permute-start.1) | collective-permute-done | bytes 262176 | tf_op jit(solution)/shard_map/ppermute | solution.py:275
  19.5 4.1 %collective-permute-start.10 = (f32[1,512,128]{2,1,0:T(8,128)S(1)}, f32[1,512,128]{2,1,0:T(8,128)S(1)}, u32[]{:S(2)}, u32[]{:S(2)}) collective-permute-start(f32[1,512,128]{2,1,0:T(8,128)S(1)} %combine.17.own), channel_id=1, source_target_pairs={{0,8},{4,12},{8,0},{12,4},{16,24},{20,28},{24,16},{28,20},{1,9},{5... | collective-permute-start | bytes 786440 | tf_op jit(solution)/shard_map/ppermute | solution.py:275
  24.6 8.3 %collective-permute-done.2.rest_0_.far = f32[1,512,128]{2,1,0:T(8,128)S(1)} collective-permute-done((f32[1,512,128]{2,1,0:T(8,128)S(1)}, f32[1,512,128]{2,1,0:T(8,128)S(1)}, u32[]{:S(2)}, u32[]{:S(2)}) %collective-permute-start.2) | collective-permute-done | bytes 262176 | tf_op jit(solution)/shard_map/ppermute | solution.py:275
  38.4 7.7 %collective-permute-done.3.rest_0_.far = f32[1,512,128]{2,1,0:T(8,128)S(1)} collective-permute-done((f32[1,512,128]{2,1,0:T(8,128)S(1)}, f32[1,512,128]{2,1,0:T(8,128)S(1)}, u32[]{:S(2)}, u32[]{:S(2)}) %collective-permute-start.3) | collective-permute-done | bytes 262176 | tf_op jit(solution)/shard_map/ppermute | solution.py:275
  51.3 8.1 %collective-permute-done.4.rest_0_.far = f32[1,512,128]{2,1,0:T(8,128)S(1)} collective-permute-done((f32[1,512,128]{2,1,0:T(8,128)S(1)}, f32[1,512,128]{2,1,0:T(8,128)S(1)}, u32[]{:S(2)}, u32[]{:S(2)}) %collective-permute-start.4) | collective-permute-done | bytes 262176 | tf_op jit(solution)/shard_map/ppermute | solution.py:275
  59.5 2.1 %inner.8 = (f32[2,512,1024]{2,1,0:T(8,128)}, f32[8,128]{1,0:T(8,128)S(1)}) custom-call(s32[1]{0:T(128)} %bitcast.me, f32[8,512,4]{2,1,0:T(8,128)S(1)} %copy-done.1, bf16[512,512]{1,0:T(8,128)(2,1)S(1)} %copy-done.2, bf16[512,512]{1,0:T(8,128)(2,1)S(1)} %copy-done.3, bf16[512,512]{1,0:T(8,128)(2,1)S(1)} %copy-done.4, bf16[512,512]{1,0:T(8,128)(2,1)S(1)} %copy-done.5, ...), custom_call_target="tpu_custom_call" | custom-call | tf_op jit(solution)/shard_map/inner/pallas_call | solution.py:166
  63.9 2.7 %collective-permute-start.17 = (f32[1,512,128]{2,1,0:T(8,128)S(1)}, f32[1,512,128]{2,1,0:T(8,128)S(1)}, u32[]{:S(2)}, u32[]{:S(2)}) collective-permute-start(f32[1,512,128]{2,1,0:T(8,128)S(1)} %combine.23.own), channel_id=1, source_target_pairs={{0,8},{4,12},{8,0},{12,4},{16,24},{20,28},{24,16},{28,20},{1,9},{5... | collective-permute-start | bytes 786440 | tf_op jit(solution)/shard_map/ppermute | solution.py:275
  69.0 5.0 %collective-permute-done.5.rest_0_.far = f32[1,512,128]{2,1,0:T(8,128)S(1)} collective-permute-done((f32[1,512,128]{2,1,0:T(8,128)S(1)}, f32[1,512,128]{2,1,0:T(8,128)S(1)}, u32[]{:S(2)}, u32[]{:S(2)}) %collective-permute-start.5) | collective-permute-done | bytes 262176 | tf_op jit(solution)/shard_map/ppermute | solution.py:275
  74.0 2.1 %inner.9 = (f32[2,512,1024]{2,1,0:T(8,128)}, f32[8,128]{1,0:T(8,128)S(1)}) custom-call(s32[1]{0:T(128)} %bitcast.me, f32[8,512,4]{2,1,0:T(8,128)S(1)} %copy-done.1, bf16[512,512]{1,0:T(8,128)(2,1)S(1)} %copy-done.2, bf16[512,512]{1,0:T(8,128)(2,1)S(1)} %copy-done.3, bf16[512,512]{1,0:T(8,128)(2,1)S(1)} %copy-done.4, ...), custom_call_target="tpu_custom_call", output_to_operand_aliasing={{0}: (8, {})} | custom-call | tf_op jit(solution)/shard_map/inner/pallas_call | solution.py:166
  82.1 2.1 %inner.10 = (f32[2,512,1024]{2,1,0:T(8,128)}, f32[8,128]{1,0:T(8,128)S(1)}) custom-call(s32[1]{0:T(128)} %bitcast.me, f32[8,512,4]{2,1,0:T(8,128)S(1)} %copy-done.1, bf16[512,512]{1,0:T(8,128)(2,1)S(1)} %copy-done.2, bf16[512,512]{1,0:T(8,128)(2,1)S(1)} %copy-done.3, bf16[512,512]{1,0:T(8,128)(2,1)S(1)} %copy-done.4, ...), custom_call_target="tpu_custom_call", output_to_operand_aliasing={{0}: (8, {})} | custom-call | tf_op jit(solution)/shard_map/inner/pallas_call | solution.py:166
  84.3 3.3 %collective-permute-done.6.rest_0_.far = f32[1,512,128]{2,1,0:T(8,128)S(1)} collective-permute-done((f32[1,512,128]{2,1,0:T(8,128)S(1)}, f32[1,512,128]{2,1,0:T(8,128)S(1)}, u32[]{:S(2)}, u32[]{:S(2)}) %collective-permute-start.6) | collective-permute-done | bytes 262176 | tf_op jit(solution)/shard_map/ppermute | solution.py:275
  87.5 5.6 %collective-permute-done.12.far = f32[1,512,128]{2,1,0:T(8,128)S(1)} collective-permute-done((f32[1,512,128]{2,1,0:T(8,128)S(1)}, f32[1,512,128]{2,1,0:T(8,128)S(1)}, u32[]{:S(2)}, u32[]{:S(2)}) %collective-permute-start.12) | collective-permute-done | bytes 262176 | tf_op jit(solution)/shard_map/ppermute | solution.py:275
  97.0 2.1 %inner.11 = (f32[2,512,1024]{2,1,0:T(8,128)}, f32[8,128]{1,0:T(8,128)S(1)}) custom-call(s32[1]{0:T(128)} %bitcast.me, f32[8,512,4]{2,1,0:T(8,128)S(1)} %copy-done.1, bf16[512,512]{1,0:T(8,128)(2,1)S(1)} %copy-done.2, bf16[512,512]{1,0:T(8,128)(2,1)S(1)} %copy-done.3, bf16[512,512]{1,0:T(8,128)(2,1)S(1)} %copy-done.4, ...), custom_call_target="tpu_custom_call", output_to_operand_aliasing={{0}: (8, {})} | custom-call | tf_op jit(solution)/shard_map/inner/pallas_call | solution.py:166
  99.1 3.0 %collective-permute-done.22.far = f32[1,512,128]{2,1,0:T(8,128)S(1)} collective-permute-done((f32[1,512,128]{2,1,0:T(8,128)S(1)}, f32[1,512,128]{2,1,0:T(8,128)S(1)}, u32[]{:S(2)}, u32[]{:S(2)}) %collective-permute-start.22) | collective-permute-done | bytes 262176 | tf_op jit(solution)/shard_map/ppermute | solution.py:275
  104.0 3.7 %collective-permute-done.25.far = f32[1,512,128]{2,1,0:T(8,128)S(1)} collective-permute-done((f32[1,512,128]{2,1,0:T(8,128)S(1)}, f32[1,512,128]{2,1,0:T(8,128)S(1)}, u32[]{:S(2)}, u32[]{:S(2)}) %collective-permute-start.25) | collective-permute-done | bytes 262176 | tf_op jit(solution)/shard_map/ppermute | solution.py:275
  108.9 2.1 %inner.12 = (f32[2,512,1024]{2,1,0:T(8,128)}, f32[8,128]{1,0:T(8,128)S(1)}) custom-call(s32[1]{0:T(128)} %bitcast.me, f32[8,512,4]{2,1,0:T(8,128)S(1)} %copy-done.1, bf16[512,512]{1,0:T(8,128)(2,1)S(1)} %copy-done.2, bf16[512,512]{1,0:T(8,128)(2,1)S(1)} %copy-done.3, bf16[512,512]{1,0:T(8,128)(2,1)S(1)} %copy-done.4, ...), custom_call_target="tpu_custom_call", output_to_operand_aliasing={{0}: (8, {})} | custom-call | tf_op jit(solution)/shard_map/inner/pallas_call | solution.py:166
  111.1 2.2 %collective-permute-done.23.far = f32[1,512,128]{2,1,0:T(8,128)S(1)} collective-permute-done((f32[1,512,128]{2,1,0:T(8,128)S(1)}, f32[1,512,128]{2,1,0:T(8,128)S(1)}, u32[]{:S(2)}, u32[]{:S(2)}) %collective-permute-start.23) | collective-permute-done | bytes 262176 | tf_op jit(solution)/shard_map/ppermute | solution.py:275
  114.5 13.7 %collective-permute-done.7.far = f32[1,512,128]{2,1,0:T(8,128)S(1)} collective-permute-done((f32[1,512,128]{2,1,0:T(8,128)S(1)}, f32[1,512,128]{2,1,0:T(8,128)S(1)}, u32[]{:S(2)}, u32[]{:S(2)}) %collective-permute-start.7) | collective-permute-done | bytes 262176 | tf_op jit(solution)/shard_map/ppermute | solution.py:275
  132.4 2.1 %inner.13 = (f32[2,512,1024]{2,1,0:T(8,128)}, f32[8,128]{1,0:T(8,128)}) custom-call(s32[1]{0:T(128)} %bitcast.me, f32[8,512,4]{2,1,0:T(8,128)S(1)} %copy-done.1, bf16[512,512]{1,0:T(8,128)(2,1)S(1)} %copy-done.2, bf16[512,512]{1,0:T(8,128)(2,1)S(1)} %copy-done.3, bf16[512,512]{1,0:T(8,128)(2,1)S(1)} %copy-done.4, ...), custom_call_target="tpu_custom_call", output_to_operand_aliasing={{0}: (8, {})} | custom-call | tf_op jit(solution)/shard_map/inner/pallas_call | solution.py:166
  134.5 2.1 %inner.14 = (f32[2,512,1024]{2,1,0:T(8,128)}, f32[8,128]{1,0:T(8,128)}) custom-call(s32[1]{0:T(128)} %bitcast.me, f32[8,512,4]{2,1,0:T(8,128)S(1)} %copy-done.1, bf16[512,512]{1,0:T(8,128)(2,1)S(1)} %copy-done.2, bf16[512,512]{1,0:T(8,128)(2,1)S(1)} %copy-done.3, bf16[512,512]{1,0:T(8,128)(2,1)S(1)} %copy-done.4, ...), custom_call_target="tpu_custom_call", output_to_operand_aliasing={{0}: (8, {})} | custom-call | tf_op jit(solution)/shard_map/inner/pallas_call | solution.py:166
  138.1 6.7 %collective-permute-done.20.rest_2_ = f32[1,512,128]{2,1,0:T(8,128)S(1)} collective-permute-done((f32[1,512,128]{2,1,0:T(8,128)S(1)}, f32[1,512,128]{2,1,0:T(8,128)S(1)}, u32[]{:S(2)}, u32[]{:S(2)}) %collective-permute-start.20) | collective-permute-done | bytes 262176 | tf_op jit(solution)/shard_map/ppermute | solution.py:275
  144.8 2.6 %inner.15 = (f32[2,512,1024]{2,1,0:T(8,128)}, f32[8,128]{1,0:T(8,128)}) custom-call(s32[1]{0:T(128)} %bitcast.me, f32[8,512,8]{2,1,0:T(8,128)S(1)} %copy-done.6, bf16[512,512]{1,0:T(8,128)(2,1)S(1)} %copy-done.2, bf16[512,512]{1,0:T(8,128)(2,1)S(1)} %copy-done.3, bf16[512,512]{1,0:T(8,128)(2,1)S(1)} %copy-done.4, ...), custom_call_target="tpu_custom_call", output_to_operand_aliasing={{0}: (10, {})} | custom-call | tf_op jit(solution)/shard_map/inner/pallas_call | solution.py:166
  (97 shorter events, 37.8 us)
Async XLA Ops:
  2.5 16.3 %collective-permute-start.1 = (f32[1,512,128]{2,1,0:T(8,128)}, f32[1,512,128]{2,1,0:T(8,128)S(1)}, u32[]{:S(2)}, u32[]{:S(2)}) collective-permute-start(f32[1,512,128]{2,1,0:T(8,128)} %stencil.14.own), channel_id=1, source_target_pairs={{0,16},{4,20},{8,24},{12,28},{16,0},{20,4},{24,8},{28,12},{1,17},{... | collective-permute-start | bytes 786440 | tf_op jit(solution)/shard_map/ppermute | solution.py:275
  18.8 14.1 %collective-permute-start.2 = (f32[1,512,128]{2,1,0:T(8,128)S(1)}, f32[1,512,128]{2,1,0:T(8,128)S(1)}, u32[]{:S(2)}, u32[]{:S(2)}) collective-permute-start(f32[1,512,128]{2,1,0:T(8,128)S(1)} %gate.7.own), channel_id=1, source_target_pairs={{0,16},{4,20},{8,24},{12,28},{16,0},{20,4},{24,8},{28,12},{1,17},{... | collective-permute-start | bytes 786440 | tf_op jit(solution)/shard_map/ppermute | solution.py:275
  19.5 14.2 %collective-permute-start.10 = (f32[1,512,128]{2,1,0:T(8,128)S(1)}, f32[1,512,128]{2,1,0:T(8,128)S(1)}, u32[]{:S(2)}, u32[]{:S(2)}) collective-permute-start(f32[1,512,128]{2,1,0:T(8,128)S(1)} %combine.17.own), channel_id=1, source_target_pairs={{0,8},{4,12},{8,0},{12,4},{16,24},{20,28},{24,16},{28,20},{1,9},{5... | collective-permute-start | bytes 786440 | tf_op jit(solution)/shard_map/ppermute | solution.py:275
  32.9 13.2 %collective-permute-start.3 = (f32[1,512,128]{2,1,0:T(8,128)S(1)}, f32[1,512,128]{2,1,0:T(8,128)S(1)}, u32[]{:S(2)}, u32[]{:S(2)}) collective-permute-start(f32[1,512,128]{2,1,0:T(8,128)S(1)} %gate.8.rest_0_.own), channel_id=1, source_target_pairs={{0,16},{4,20},{8,24},{12,28},{16,0},{20,4},{24,8},{28,12},{1,17},{... | collective-permute-start | bytes 786440 | tf_op jit(solution)/shard_map/ppermute | solution.py:275
  34.4 25.0 %collective-permute-start.11 = (f32[2,512,128]{2,1,0:T(8,128)S(1)}, f32[2,512,128]{2,1,0:T(8,128)S(1)}, u32[]{:S(2)}, u32[]{:S(2)}) collective-permute-start(f32[2,512,128]{2,1,0:T(8,128)S(1)} %combine.18.rest_0_), channel_id=1, source_target_pairs={{0,4},{4,0},{8,12},{12,8},{16,20},{20,16},{24,28},{28,24},{1,5},{5... | collective-permute-start | bytes 1572872 | tf_op jit(solution)/shard_map/ppermute | solution.py:275
  36.3 12.3 %collective-permute-start.8 = (f32[1,512,128]{2,1,0:T(8,128)S(1)}, f32[1,512,128]{2,1,0:T(8,128)S(1)}, u32[]{:S(2)}, u32[]{:S(2)}) collective-permute-start(f32[1,512,128]{2,1,0:T(8,128)S(1)} %combine.15.own), channel_id=1, source_target_pairs={{0,8},{4,12},{8,0},{12,4},{16,24},{20,28},{24,16},{28,20},{1,9},{5... | collective-permute-start | bytes 786440 | tf_op jit(solution)/shard_map/ppermute | solution.py:275
  46.1 13.3 %collective-permute-start.4 = (f32[1,512,128]{2,1,0:T(8,128)S(1)}, f32[1,512,128]{2,1,0:T(8,128)S(1)}, u32[]{:S(2)}, u32[]{:S(2)}) collective-permute-start(f32[1,512,128]{2,1,0:T(8,128)S(1)} %gate.9.rest_0_.own), channel_id=1, source_target_pairs={{0,16},{4,20},{8,24},{12,28},{16,0},{20,4},{24,8},{28,12},{1,17},{... | collective-permute-start | bytes 786440 | tf_op jit(solution)/shard_map/ppermute | solution.py:275
  46.8 14.8 %collective-permute-start.14 = (f32[1,512,128]{2,1,0:T(8,128)S(1)}, f32[1,512,128]{2,1,0:T(8,128)S(1)}, u32[]{:S(2)}, u32[]{:S(2)}) collective-permute-start(f32[1,512,128]{2,1,0:T(8,128)S(1)} %combine.20.own), channel_id=1, source_target_pairs={{0,8},{4,12},{8,0},{12,4},{16,24},{20,28},{24,16},{28,20},{1,9},{5... | collective-permute-start | bytes 786440 | tf_op jit(solution)/shard_map/ppermute | solution.py:275
  49.3 24.7 %collective-permute-start.9 = (f32[2,512,128]{2,1,0:T(8,128)S(1)}, f32[2,512,128]{2,1,0:T(8,128)S(1)}, u32[]{:S(2)}, u32[]{:S(2)}) collective-permute-start(f32[2,512,128]{2,1,0:T(8,128)S(1)} %combine.16.rest_0_), channel_id=1, source_target_pairs={{0,4},{4,0},{8,12},{12,8},{16,20},{20,16},{24,28},{28,24},{1,5},{5... | collective-permute-start | bytes 1572872 | tf_op jit(solution)/shard_map/ppermute | solution.py:275
  59.4 14.6 %collective-permute-start.5 = (f32[1,512,128]{2,1,0:T(8,128)S(1)}, f32[1,512,128]{2,1,0:T(8,128)S(1)}, u32[]{:S(2)}, u32[]{:S(2)}) collective-permute-start(f32[1,512,128]{2,1,0:T(8,128)S(1)} %gate.10.own.rest_0_), channel_id=1, source_target_pairs={{0,16},{4,20},{8,24},{12,28},{16,0},{20,4},{24,8},{28,12},{1,17},{... | collective-permute-start | bytes 786440 | tf_op jit(solution)/shard_map/ppermute | solution.py:275
  62.3 19.8 %collective-permute-start.15 = (f32[2,512,128]{2,1,0:T(8,128)S(1)}, f32[2,512,128]{2,1,0:T(8,128)S(1)}, u32[]{:S(2)}, u32[]{:S(2)}) collective-permute-start(f32[2,512,128]{2,1,0:T(8,128)S(1)} %combine.21.rest_0_), channel_id=1, source_target_pairs={{0,4},{4,0},{8,12},{12,8},{16,20},{20,16},{24,28},{28,24},{1,5},{5... | collective-permute-start | bytes 1572872 | tf_op jit(solution)/shard_map/ppermute | solution.py:275
  63.9 14.1 %collective-permute-start.17 = (f32[1,512,128]{2,1,0:T(8,128)S(1)}, f32[1,512,128]{2,1,0:T(8,128)S(1)}, u32[]{:S(2)}, u32[]{:S(2)}) collective-permute-start(f32[1,512,128]{2,1,0:T(8,128)S(1)} %combine.23.own), channel_id=1, source_target_pairs={{0,8},{4,12},{8,0},{12,4},{16,24},{20,28},{24,16},{28,20},{1,9},{5... | collective-permute-start | bytes 786440 | tf_op jit(solution)/shard_map/ppermute | solution.py:275
  66.6 14.4 %collective-permute-start.13 = (f32[512,128]{1,0:T(8,128)S(1)}, f32[512,128]{1,0:T(8,128)S(1)}, u32[]{:S(2)}, u32[]{:S(2)}) collective-permute-start(f32[512,128]{1,0:T(8,128)S(1)} %get-tuple-element.31), channel_id=1, source_target_pairs={{0,1},{1,2},{2,3},{4,5},{5,6},{6,7},{8,9},{9,10},{10,11},{12,13},{... | collective-permute-start | bytes 786440 | tf_op jit(solution)/shard_map/ppermute | solution.py:253
  74.0 13.5 %collective-permute-start.6 = (f32[1,512,128]{2,1,0:T(8,128)S(1)}, f32[1,512,128]{2,1,0:T(8,128)S(1)}, u32[]{:S(2)}, u32[]{:S(2)}) collective-permute-start(f32[1,512,128]{2,1,0:T(8,128)S(1)} %gate.11.rest_0_.own), channel_id=1, source_target_pairs={{0,16},{4,20},{8,24},{12,28},{16,0},{20,4},{24,8},{28,12},{1,17},{... | collective-permute-start | bytes 786440 | tf_op jit(solution)/shard_map/ppermute | solution.py:275
  78.7 18.3 %collective-permute-start.18 = (f32[2,512,128]{2,1,0:T(8,128)S(1)}, f32[2,512,128]{2,1,0:T(8,128)S(1)}, u32[]{:S(2)}, u32[]{:S(2)}) collective-permute-start(f32[2,512,128]{2,1,0:T(8,128)S(1)} %combine.24.rest_0_), channel_id=1, source_target_pairs={{0,4},{4,0},{8,12},{12,8},{16,20},{20,16},{24,28},{28,24},{1,5},{5... | collective-permute-start | bytes 1572872 | tf_op jit(solution)/shard_map/ppermute | solution.py:275
  81.0 12.2 %collective-permute-start.12 = (f32[1,512,128]{2,1,0:T(8,128)S(1)}, f32[1,512,128]{2,1,0:T(8,128)S(1)}, u32[]{:S(2)}, u32[]{:S(2)}) collective-permute-start(f32[1,512,128]{2,1,0:T(8,128)S(1)} %combine.19.own), channel_id=1, source_target_pairs={{0,8},{4,12},{8,0},{12,4},{16,24},{20,28},{24,16},{28,20},{1,9},{5... | collective-permute-start | bytes 786440 | tf_op jit(solution)/shard_map/ppermute | solution.py:275
  87.5 14.6 %collective-permute-start.22 = (f32[1,512,128]{2,1,0:T(8,128)S(1)}, f32[1,512,128]{2,1,0:T(8,128)S(1)}, u32[]{:S(2)}, u32[]{:S(2)}) collective-permute-start(f32[1,512,128]{2,1,0:T(8,128)S(1)} %gate.13.rest_0_.own), channel_id=1, source_target_pairs={{0,16},{4,20},{8,24},{12,28},{16,0},{20,4},{24,8},{28,12},{1,17},{... | collective-permute-start | bytes 786440 | tf_op jit(solution)/shard_map/ppermute | solution.py:275
  93.8 15.1 %collective-permute-start.16 = (f32[2,512,128]{2,1,0:T(8,128)S(1)}, f32[2,512,128]{2,1,0:T(8,128)S(1)}, u32[]{:S(2)}, u32[]{:S(2)}) collective-permute-start(f32[2,512,128]{2,1,0:T(8,128)S(1)} %combine.22.rest_0_), channel_id=1, source_target_pairs={{0,4},{4,0},{8,12},{12,8},{16,20},{20,16},{24,28},{28,24},{1,5},{5... | collective-permute-start | bytes 1572872 | tf_op jit(solution)/shard_map/ppermute | solution.py:275
  96.9 10.7 %collective-permute-start.25 = (f32[1,512,128]{2,1,0:T(8,128)S(1)}, f32[1,512,128]{2,1,0:T(8,128)S(1)}, u32[]{:S(2)}, u32[]{:S(2)}) collective-permute-start(f32[1,512,128]{2,1,0:T(8,128)S(1)} %combine.28.own), channel_id=1, source_target_pairs={{0,8},{4,12},{8,0},{12,4},{16,24},{20,28},{24,16},{28,20},{1,9},{5... | collective-permute-start | bytes 786440 | tf_op jit(solution)/shard_map/ppermute | solution.py:275
  108.3 24.1 %collective-permute-start.26 = (f32[2,512,128]{2,1,0:T(8,128)S(1)}, f32[2,512,128]{2,1,0:T(8,128)S(1)}, u32[]{:S(2)}, u32[]{:S(2)}) collective-permute-start(f32[2,512,128]{2,1,0:T(8,128)S(1)} %combine.29.rest_0_), channel_id=1, source_target_pairs={{0,4},{4,0},{8,12},{12,8},{16,20},{20,16},{24,28},{28,24},{1,5},{5... | collective-permute-start | bytes 1572872 | tf_op jit(solution)/shard_map/ppermute | solution.py:275
  113.9 20.6 %collective-permute-start.24 = (f32[2,512,128]{2,1,0:T(8,128)S(1)}, f32[2,512,128]{2,1,0:T(8,128)S(1)}, u32[]{:S(2)}, u32[]{:S(2)}) collective-permute-start(f32[2,512,128]{2,1,0:T(8,128)S(1)} %combine.27.rest_0_), channel_id=1, source_target_pairs={{0,4},{4,0},{8,12},{12,8},{16,20},{20,16},{24,28},{28,24},{1,5},{5... | collective-permute-start | bytes 1572872 | tf_op jit(solution)/shard_map/ppermute | solution.py:275
  114.5 13.7 %collective-permute-start.7 = (f32[1,512,128]{2,1,0:T(8,128)S(1)}, f32[1,512,128]{2,1,0:T(8,128)S(1)}, u32[]{:S(2)}, u32[]{:S(2)}) collective-permute-start(f32[1,512,128]{2,1,0:T(8,128)S(1)} %gate.12.own.rest_0_), channel_id=1, source_target_pairs={{0,16},{4,20},{8,24},{12,28},{16,0},{20,4},{24,8},{28,12},{1,17},{... | collective-permute-start | bytes 786440 | tf_op jit(solution)/shard_map/ppermute | solution.py:275
  128.9 15.9 %collective-permute-start.20 = (f32[1,512,128]{2,1,0:T(8,128)S(1)}, f32[1,512,128]{2,1,0:T(8,128)S(1)}, u32[]{:S(2)}, u32[]{:S(2)}) collective-permute-start(f32[1,512,128]{2,1,0:T(8,128)S(1)} %combine.25.rest_0_), channel_id=1, source_target_pairs={{0,4},{4,0},{8,12},{12,8},{16,20},{20,16},{24,28},{28,24},{1,5},{5... | collective-permute-start | bytes 786440 | tf_op jit(solution)/shard_map/ppermute | solution.py:275
  130.4 14.4 %collective-permute-start.21 = (f32[1,512,128]{2,1,0:T(8,128)S(1)}, f32[1,512,128]{2,1,0:T(8,128)S(1)}, u32[]{:S(2)}, u32[]{:S(2)}) collective-permute-start(f32[1,512,128]{2,1,0:T(8,128)S(1)} %combine.25.rest_0_), channel_id=1, source_target_pairs={{0,12},{4,8},{8,4},{12,0},{16,28},{20,24},{24,20},{28,16},{1,13},{... | collective-permute-start | bytes 786440 | tf_op jit(solution)/shard_map/ppermute | solution.py:275
  (17 other events, 181.9 us)

commit v9 on v5

--- a/solution.py
+++ b/solution.py
@@ -16,7 +16,7 @@
 ORDER = {
     "stencil": [],
     "gate": [("arrived", -1)],
-    "first": [("inner", -3)],
+    "first": [],
     "middle": [("stencil", 2), ("inner", -2)],
     "inner": [],
 }

time: 144 us -> 145 us (level)
  starting transfers between devices: 31.9 us -> 36.1 us
  waiting for transfers between devices: 74.9 us -> 71.2 us
    ppermute x26, starting transfers between devices: 29.2 us -> 33.3 us  [send(): return lax.ppermute(value, 'row', [(a, a ^ half) for a in range(devices)])]
    ppermute x26, waiting for transfers between devices: 74.9 us -> 71.2 us  [send(): return lax.ppermute(value, 'row', [(a, a ^ half) for a in range(devices)])]
  transfers between devices with their start and end apart: 28 -> 28, of which waited for: 16 -> 13; matrix products, arithmetic and copies ran while one was open for 0% -> 0% of each run, Pallas kernels for 22% -> 22%
where the time goes in v9:
time: 145 us
  waiting for transfers between devices  71.2 us (49%)
  Pallas kernels  37.1 us (26%)
  starting transfers between devices  36.1 us (25%)
    ppermute x26, waiting for transfers between devices, send(): return lax.ppermute(value, 'row', [(a, a ^ half) for a in range(devices)])  71.2 us
    ppermute x26, starting transfers between devices, send(): return lax.ppermute(value, 'row', [(a, a ^ half) for a in range(devices)])  33.3 us
    pallas_call x8, Pallas kernels, inner(): pl.pallas_call(functools.partial(inner_kernel, len(blocks)), grid_spec=pl...  17.9 us
    pallas_call x8, Pallas kernels, stencil(): pl.pallas_call(functools.partial(stencil_kernel, block, width // offsets....  9.99 us
    pallas_call x14, Pallas kernels, combine(): pl.pallas_call(combine_kernel, in_specs=[small, small, whole, whole] + [p...  9.17 us
  transfers between devices with their start and end apart: 28, of which 13 were waited for; matrix products, arithmetic and copies ran while one was open for 0% of the time, Pallas kernels for 22%

profile of v9, /device:TPU:0, one launch (start us, length us, event | category | flops | bytes accessed | tf_op | source)
XLA Modules:
  0.0 144.8 jit_solution(4237430169721309189)
XLA Ops:
  0.0 2.5 %stencil.15.own = f32[1,512,128]{2,1,0:T(8,128)} custom-call(s32[32]{0:T(128)} %offsets.15, f32[512,1024]{1,0:T(8,128)} %right.13, f32[512,1024]{1,0:T(8,128)} %right.13, f32[512,1024]{1,0:T(8,128)} %right.13, f32[1,512]{1,0:T(1,128)} %bitcast.11, f32[4,1024]{1,0:T(4,128)} %coef.15, s32[1,1024]{1,0:T(1,128)} %bitcast.3), custom_call_target="tpu_custom_call" | custom-call | tf_op jit(solution)/shard_map/stencil/pallas_call | solution.py:74
  2.5 4.1 %collective-permute-start.2 = (f32[1,512,128]{2,1,0:T(8,128)}, f32[1,512,128]{2,1,0:T(8,128)S(1)}, u32[]{:S(2)}, u32[]{:S(2)}) collective-permute-start(f32[1,512,128]{2,1,0:T(8,128)} %stencil.15.own), channel_id=1, source_target_pairs={{0,16},{4,20},{8,24},{12,28},{16,0},{20,4},{24,8},{28,12},{1,17},{... | collective-permute-start | bytes 786440 | tf_op jit(solution)/shard_map/ppermute | solution.py:275
  7.7 11.1 %collective-permute-done.2.rest_0_.far = f32[1,512,128]{2,1,0:T(8,128)S(1)} collective-permute-done((f32[1,512,128]{2,1,0:T(8,128)}, f32[1,512,128]{2,1,0:T(8,128)S(1)}, u32[]{:S(2)}, u32[]{:S(2)}) %collective-permute-start.2) | collective-permute-done | bytes 262176 | tf_op jit(solution)/shard_map/ppermute | solution.py:275
  19.5 4.1 %collective-permute-start.20 = (f32[1,512,128]{2,1,0:T(8,128)S(1)}, f32[1,512,128]{2,1,0:T(8,128)S(1)}, u32[]{:S(2)}, u32[]{:S(2)}) collective-permute-start(f32[1,512,128]{2,1,0:T(8,128)S(1)} %combine.20.own), channel_id=1, source_target_pairs={{0,8},{4,12},{8,0},{12,4},{16,24},{20,28},{24,16},{28,20},{1,9},{5... | collective-permute-start | bytes 786440 | tf_op jit(solution)/shard_map/ppermute | solution.py:275
  24.6 8.3 %collective-permute-done.3.rest_0_.far = f32[1,512,128]{2,1,0:T(8,128)S(1)} collective-permute-done((f32[1,512,128]{2,1,0:T(8,128)S(1)}, f32[1,512,128]{2,1,0:T(8,128)S(1)}, u32[]{:S(2)}, u32[]{:S(2)}) %collective-permute-start.3) | collective-permute-done | bytes 262176 | tf_op jit(solution)/shard_map/ppermute | solution.py:275
  38.4 7.7 %collective-permute-done.4.rest_0_.far = f32[1,512,128]{2,1,0:T(8,128)S(1)} collective-permute-done((f32[1,512,128]{2,1,0:T(8,128)S(1)}, f32[1,512,128]{2,1,0:T(8,128)S(1)}, u32[]{:S(2)}, u32[]{:S(2)}) %collective-permute-start.4) | collective-permute-done | bytes 262176 | tf_op jit(solution)/shard_map/ppermute | solution.py:275
  51.3 8.2 %collective-permute-done.5.rest_0_.far = f32[1,512,128]{2,1,0:T(8,128)S(1)} collective-permute-done((f32[1,512,128]{2,1,0:T(8,128)S(1)}, f32[1,512,128]{2,1,0:T(8,128)S(1)}, u32[]{:S(2)}, u32[]{:S(2)}) %collective-permute-start.5) | collective-permute-done | bytes 262176 | tf_op jit(solution)/shard_map/ppermute | solution.py:275
  60.2 3.1 %collective-permute-start.17 = (f32[1,512,128]{2,1,0:T(8,128)S(1)}, f32[1,512,128]{2,1,0:T(8,128)S(1)}, u32[]{:S(2)}, u32[]{:S(2)}) collective-permute-start(f32[1,512,128]{2,1,0:T(8,128)S(1)} %combine.17.own), channel_id=1, source_target_pairs={{0,8},{4,12},{8,0},{12,4},{16,24},{20,28},{24,16},{28,20},{1,9},{5... | collective-permute-start | bytes 786440 | tf_op jit(solution)/shard_map/ppermute | solution.py:275
  65.7 2.1 %inner.8 = (f32[2,512,1024]{2,1,0:T(8,128)}, f32[8,128]{1,0:T(8,128)S(1)}) custom-call(s32[1]{0:T(128)} %bitcast.me, f32[8,512,4]{2,1,0:T(8,128)S(1)} %copy-done.1, bf16[512,512]{1,0:T(8,128)(2,1)S(1)} %copy-done.2, bf16[512,512]{1,0:T(8,128)(2,1)S(1)} %copy-done.3, bf16[512,512]{1,0:T(8,128)(2,1)S(1)} %copy-done.4, bf16[512,512]{1,0:T(8,128)(2,1)S(1)} %copy-done.5, ...), custom_call_target="tpu_custom_call" | custom-call | tf_op jit(solution)/shard_map/inner/pallas_call | solution.py:166
  69.2 5.0 %collective-permute-done.6.rest_0_.far = f32[1,512,128]{2,1,0:T(8,128)S(1)} collective-permute-done((f32[1,512,128]{2,1,0:T(8,128)S(1)}, f32[1,512,128]{2,1,0:T(8,128)S(1)}, u32[]{:S(2)}, u32[]{:S(2)}) %collective-permute-start.6) | collective-permute-done | bytes 262176 | tf_op jit(solution)/shard_map/ppermute | solution.py:275
  74.1 2.1 %inner.9 = (f32[2,512,1024]{2,1,0:T(8,128)}, f32[8,128]{1,0:T(8,128)S(1)}) custom-call(s32[1]{0:T(128)} %bitcast.me, f32[8,512,4]{2,1,0:T(8,128)S(1)} %copy-done.1, bf16[512,512]{1,0:T(8,128)(2,1)S(1)} %copy-done.2, bf16[512,512]{1,0:T(8,128)(2,1)S(1)} %copy-done.3, bf16[512,512]{1,0:T(8,128)(2,1)S(1)} %copy-done.4, ...), custom_call_target="tpu_custom_call", output_to_operand_aliasing={{0}: (8, {})} | custom-call | tf_op jit(solution)/shard_map/inner/pallas_call | solution.py:166
  79.7 2.4 %collective-permute-start.26 = (f32[1,512,128]{2,1,0:T(8,128)S(1)}, f32[1,512,128]{2,1,0:T(8,128)S(1)}, u32[]{:S(2)}, u32[]{:S(2)}) collective-permute-start(f32[1,512,128]{2,1,0:T(8,128)S(1)} %combine.26.own), channel_id=1, source_target_pairs={{0,8},{4,12},{8,0},{12,4},{16,24},{20,28},{24,16},{28,20},{1,9},{5... | collective-permute-start | bytes 786440 | tf_op jit(solution)/shard_map/ppermute | solution.py:275
  83.1 4.5 %collective-permute-done.7.rest_0_.far = f32[1,512,128]{2,1,0:T(8,128)S(1)} collective-permute-done((f32[1,512,128]{2,1,0:T(8,128)S(1)}, f32[1,512,128]{2,1,0:T(8,128)S(1)}, u32[]{:S(2)}, u32[]{:S(2)}) %collective-permute-start.7) | collective-permute-done | bytes 262176 | tf_op jit(solution)/shard_map/ppermute | solution.py:275
  88.3 3.1 %collective-permute-start.16 = (f32[1,512,128]{2,1,0:T(8,128)S(1)}, f32[1,512,128]{2,1,0:T(8,128)S(1)}, u32[]{:S(2)}, u32[]{:S(2)}) collective-permute-start(f32[1,512,128]{2,1,0:T(8,128)S(1)} %combine.16.own), channel_id=1, source_target_pairs={{0,8},{4,12},{8,0},{12,4},{16,24},{20,28},{24,16},{28,20},{1,9},{5... | collective-permute-start | bytes 786440 | tf_op jit(solution)/shard_map/ppermute | solution.py:275
  92.5 2.1 %inner.10 = (f32[2,512,1024]{2,1,0:T(8,128)}, f32[8,128]{1,0:T(8,128)S(1)}) custom-call(s32[1]{0:T(128)} %bitcast.me, f32[8,512,4]{2,1,0:T(8,128)S(1)} %copy-done.1, bf16[512,512]{1,0:T(8,128)(2,1)S(1)} %copy-done.2, bf16[512,512]{1,0:T(8,128)(2,1)S(1)} %copy-done.3, bf16[512,512]{1,0:T(8,128)(2,1)S(1)} %copy-done.4, ...), custom_call_target="tpu_custom_call", output_to_operand_aliasing={{0}: (8, {})} | custom-call | tf_op jit(solution)/shard_map/inner/pallas_call | solution.py:166
  98.0 4.4 %collective-permute-done.8.rest_0_.far = f32[1,512,128]{2,1,0:T(8,128)S(1)} collective-permute-done((f32[1,512,128]{2,1,0:T(8,128)S(1)}, f32[1,512,128]{2,1,0:T(8,128)S(1)}, u32[]{:S(2)}, u32[]{:S(2)}) %collective-permute-start.8) | collective-permute-done | bytes 262176 | tf_op jit(solution)/shard_map/ppermute | solution.py:275
  106.8 2.5 %collective-permute-start.13 = (f32[1,512,128]{2,1,0:T(8,128)S(1)}, f32[1,512,128]{2,1,0:T(8,128)S(1)}, u32[]{:S(2)}, u32[]{:S(2)}) collective-permute-start(f32[1,512,128]{2,1,0:T(8,128)S(1)} %combine.15.rest_0_), channel_id=1, source_target_pairs={{0,8},{4,12},{8,0},{12,4},{16,24},{20,28},{24,16},{28,20},{1,9},{5... | collective-permute-start | bytes 786440 | tf_op jit(solution)/shard_map/ppermute | solution.py:275
  110.8 9.3 %collective-permute-done.9.far = f32[1,512,128]{2,1,0:T(8,128)S(1)} collective-permute-done((f32[1,512,128]{2,1,0:T(8,128)S(1)}, f32[1,512,128]{2,1,0:T(8,128)S(1)}, u32[]{:S(2)}, u32[]{:S(2)}) %collective-permute-start.9) | collective-permute-done | bytes 262176 | tf_op jit(solution)/shard_map/ppermute | solution.py:275
  120.8 3.0 %collective-permute-start.10 = (f32[1,512,128]{2,1,0:T(8,128)S(1)}, f32[1,512,128]{2,1,0:T(8,128)S(1)}, u32[]{:S(2)}, u32[]{:S(2)}) collective-permute-start(f32[1,512,128]{2,1,0:T(8,128)S(1)} %combine.14.rest_0_), channel_id=1, source_target_pairs={{0,8},{4,12},{8,0},{12,4},{16,24},{20,28},{24,16},{28,20},{1,9},{5... | collective-permute-start | bytes 786440 | tf_op jit(solution)/shard_map/ppermute | solution.py:275
  125.4 2.1 %inner.12 = (f32[2,512,1024]{2,1,0:T(8,128)}, f32[8,128]{1,0:T(8,128)}) custom-call(s32[1]{0:T(128)} %bitcast.me, f32[8,512,4]{2,1,0:T(8,128)S(1)} %copy-done.1, bf16[512,512]{1,0:T(8,128)(2,1)S(1)} %copy-done.2, bf16[512,512]{1,0:T(8,128)(2,1)S(1)} %copy-done.3, bf16[512,512]{1,0:T(8,128)(2,1)S(1)} %copy-done.4, ...), custom_call_target="tpu_custom_call", output_to_operand_aliasing={{0}: (8, {})} | custom-call | tf_op jit(solution)/shard_map/inner/pallas_call | solution.py:166
  127.5 2.1 %inner.13 = (f32[2,512,1024]{2,1,0:T(8,128)}, f32[8,128]{1,0:T(8,128)}) custom-call(s32[1]{0:T(128)} %bitcast.me, f32[8,512,4]{2,1,0:T(8,128)S(1)} %copy-done.1, bf16[512,512]{1,0:T(8,128)(2,1)S(1)} %copy-done.2, bf16[512,512]{1,0:T(8,128)(2,1)S(1)} %copy-done.3, bf16[512,512]{1,0:T(8,128)(2,1)S(1)} %copy-done.4, ...), custom_call_target="tpu_custom_call", output_to_operand_aliasing={{0}: (8, {})} | custom-call | tf_op jit(solution)/shard_map/inner/pallas_call | solution.py:166
  131.7 2.6 %inner.14 = (f32[2,512,1024]{2,1,0:T(8,128)}, f32[8,128]{1,0:T(8,128)}) custom-call(s32[1]{0:T(128)} %bitcast.me, f32[8,512,8]{2,1,0:T(8,128)S(1)} %copy-done.6, bf16[512,512]{1,0:T(8,128)(2,1)S(1)} %copy-done.2, bf16[512,512]{1,0:T(8,128)(2,1)S(1)} %copy-done.3, bf16[512,512]{1,0:T(8,128)(2,1)S(1)} %copy-done.4, ...), custom_call_target="tpu_custom_call", output_to_operand_aliasing={{0}: (10, {})} | custom-call | tf_op jit(solution)/shard_map/inner/pallas_call | solution.py:166
  135.9 6.4 %collective-permute-done.11.rest_2_ = f32[1,512,128]{2,1,0:T(8,128)S(1)} collective-permute-done((f32[1,512,128]{2,1,0:T(8,128)S(1)}, f32[1,512,128]{2,1,0:T(8,128)S(1)}, u32[]{:S(2)}, u32[]{:S(2)}) %collective-permute-start.11) | collective-permute-done | bytes 262176 | tf_op jit(solution)/shard_map/ppermute | solution.py:275
  142.3 2.6 %inner.15 = (f32[2,512,1024]{2,1,0:T(8,128)}, f32[8,128]{1,0:T(8,128)}) custom-call(s32[1]{0:T(128)} %bitcast.me, f32[8,512,8]{2,1,0:T(8,128)S(1)} %copy-done.6, bf16[512,512]{1,0:T(8,128)(2,1)S(1)} %copy-done.2, bf16[512,512]{1,0:T(8,128)(2,1)S(1)} %copy-done.3, bf16[512,512]{1,0:T(8,128)(2,1)S(1)} %copy-done.4, ...), custom_call_target="tpu_custom_call", output_to_operand_aliasing={{0}: (10, {})} | custom-call | tf_op jit(solution)/shard_map/inner/pallas_call | solution.py:166
  (98 shorter events, 39.2 us)
Async XLA Ops:
  2.5 16.3 %collective-permute-start.2 = (f32[1,512,128]{2,1,0:T(8,128)}, f32[1,512,128]{2,1,0:T(8,128)S(1)}, u32[]{:S(2)}, u32[]{:S(2)}) collective-permute-start(f32[1,512,128]{2,1,0:T(8,128)} %stencil.15.own), channel_id=1, source_target_pairs={{0,16},{4,20},{8,24},{12,28},{16,0},{20,4},{24,8},{28,12},{1,17},{... | collective-permute-start | bytes 786440 | tf_op jit(solution)/shard_map/ppermute | solution.py:275
  18.8 14.1 %collective-permute-start.3 = (f32[1,512,128]{2,1,0:T(8,128)S(1)}, f32[1,512,128]{2,1,0:T(8,128)S(1)}, u32[]{:S(2)}, u32[]{:S(2)}) collective-permute-start(f32[1,512,128]{2,1,0:T(8,128)S(1)} %gate.7.own), channel_id=1, source_target_pairs={{0,16},{4,20},{8,24},{12,28},{16,0},{20,4},{24,8},{28,12},{1,17},{... | collective-permute-start | bytes 786440 | tf_op jit(solution)/shard_map/ppermute | solution.py:275
  19.5 15.9 %collective-permute-start.20 = (f32[1,512,128]{2,1,0:T(8,128)S(1)}, f32[1,512,128]{2,1,0:T(8,128)S(1)}, u32[]{:S(2)}, u32[]{:S(2)}) collective-permute-start(f32[1,512,128]{2,1,0:T(8,128)S(1)} %combine.20.own), channel_id=1, source_target_pairs={{0,8},{4,12},{8,0},{12,4},{16,24},{20,28},{24,16},{28,20},{1,9},{5... | collective-permute-start | bytes 786440 | tf_op jit(solution)/shard_map/ppermute | solution.py:275
  36.1 28.3 %collective-permute-start.21 = (f32[2,512,128]{2,1,0:T(8,128)S(1)}, f32[2,512,128]{2,1,0:T(8,128)S(1)}, u32[]{:S(2)}, u32[]{:S(2)}) collective-permute-start(f32[2,512,128]{2,1,0:T(8,128)S(1)} %combine.21.rest_0_), channel_id=1, source_target_pairs={{0,4},{4,0},{8,12},{12,8},{16,20},{20,16},{24,28},{28,24},{1,5},{5... | collective-permute-start | bytes 1572872 | tf_op jit(solution)/shard_map/ppermute | solution.py:275
  46.1 13.3 %collective-permute-start.5 = (f32[1,512,128]{2,1,0:T(8,128)S(1)}, f32[1,512,128]{2,1,0:T(8,128)S(1)}, u32[]{:S(2)}, u32[]{:S(2)}) collective-permute-start(f32[1,512,128]{2,1,0:T(8,128)S(1)} %gate.9.own.rest_0_), channel_id=1, source_target_pairs={{0,16},{4,20},{8,24},{12,28},{16,0},{20,4},{24,8},{28,12},{1,17},{... | collective-permute-start | bytes 786440 | tf_op jit(solution)/shard_map/ppermute | solution.py:275
  47.5 26.6 %collective-permute-start.19 = (f32[2,512,128]{2,1,0:T(8,128)S(1)}, f32[2,512,128]{2,1,0:T(8,128)S(1)}, u32[]{:S(2)}, u32[]{:S(2)}) collective-permute-start(f32[2,512,128]{2,1,0:T(8,128)S(1)} %combine.19.rest_0_), channel_id=1, source_target_pairs={{0,4},{4,0},{8,12},{12,8},{16,20},{20,16},{24,28},{28,24},{1,5},{5... | collective-permute-start | bytes 1572872 | tf_op jit(solution)/shard_map/ppermute | solution.py:275
  49.1 18.7 %collective-permute-start.23 = (f32[1,512,128]{2,1,0:T(8,128)S(1)}, f32[1,512,128]{2,1,0:T(8,128)S(1)}, u32[]{:S(2)}, u32[]{:S(2)}) collective-permute-start(f32[1,512,128]{2,1,0:T(8,128)S(1)} %combine.23.own), channel_id=1, source_target_pairs={{0,8},{4,12},{8,0},{12,4},{16,24},{20,28},{24,16},{28,20},{1,9},{5... | collective-permute-start | bytes 786440 | tf_op jit(solution)/shard_map/ppermute | solution.py:275
  59.4 14.7 %collective-permute-start.6 = (f32[1,512,128]{2,1,0:T(8,128)S(1)}, f32[1,512,128]{2,1,0:T(8,128)S(1)}, u32[]{:S(2)}, u32[]{:S(2)}) collective-permute-start(f32[1,512,128]{2,1,0:T(8,128)S(1)} %gate.10.rest_0_.own), channel_id=1, source_target_pairs={{0,16},{4,20},{8,24},{12,28},{16,0},{20,4},{24,8},{28,12},{1,17},{... | collective-permute-start | bytes 786440 | tf_op jit(solution)/shard_map/ppermute | solution.py:275
  60.2 16.1 %collective-permute-start.17 = (f32[1,512,128]{2,1,0:T(8,128)S(1)}, f32[1,512,128]{2,1,0:T(8,128)S(1)}, u32[]{:S(2)}, u32[]{:S(2)}) collective-permute-start(f32[1,512,128]{2,1,0:T(8,128)S(1)} %combine.17.own), channel_id=1, source_target_pairs={{0,8},{4,12},{8,0},{12,4},{16,24},{20,28},{24,16},{28,20},{1,9},{5... | collective-permute-start | bytes 786440 | tf_op jit(solution)/shard_map/ppermute | solution.py:275
  64.4 15.3 %collective-permute-start.1 = (f32[512,128]{1,0:T(8,128)S(1)}, f32[512,128]{1,0:T(8,128)S(1)}, u32[]{:S(2)}, u32[]{:S(2)}) collective-permute-start(f32[512,128]{1,0:T(8,128)S(1)} %get-tuple-element.29), channel_id=1, source_target_pairs={{0,1},{1,2},{2,3},{4,5},{5,6},{6,7},{8,9},{9,10},{10,11},{12,13},{... | collective-permute-start | bytes 786440 | tf_op jit(solution)/shard_map/ppermute | solution.py:253
  68.5 23.9 %collective-permute-start.24 = (f32[2,512,128]{2,1,0:T(8,128)S(1)}, f32[2,512,128]{2,1,0:T(8,128)S(1)}, u32[]{:S(2)}, u32[]{:S(2)}) collective-permute-start(f32[2,512,128]{2,1,0:T(8,128)S(1)} %combine.24.rest_0_), channel_id=1, source_target_pairs={{0,4},{4,0},{8,12},{12,8},{16,20},{20,16},{24,28},{28,24},{1,5},{5... | collective-permute-start | bytes 1572872 | tf_op jit(solution)/shard_map/ppermute | solution.py:275
  74.1 13.5 %collective-permute-start.7 = (f32[1,512,128]{2,1,0:T(8,128)S(1)}, f32[1,512,128]{2,1,0:T(8,128)S(1)}, u32[]{:S(2)}, u32[]{:S(2)}) collective-permute-start(f32[1,512,128]{2,1,0:T(8,128)S(1)} %gate.11.own.rest_0_), channel_id=1, source_target_pairs={{0,16},{4,20},{8,24},{12,28},{16,0},{20,4},{24,8},{28,12},{1,17},{... | collective-permute-start | bytes 786440 | tf_op jit(solution)/shard_map/ppermute | solution.py:275
  76.9 18.9 %collective-permute-start.22 = (f32[2,512,128]{2,1,0:T(8,128)S(1)}, f32[2,512,128]{2,1,0:T(8,128)S(1)}, u32[]{:S(2)}, u32[]{:S(2)}) collective-permute-start(f32[2,512,128]{2,1,0:T(8,128)S(1)} %combine.22.rest_0_), channel_id=1, source_target_pairs={{0,4},{4,0},{8,12},{12,8},{16,20},{20,16},{24,28},{28,24},{1,5},{5... | collective-permute-start | bytes 1572872 | tf_op jit(solution)/shard_map/ppermute | solution.py:275
  79.7 14.9 %collective-permute-start.26 = (f32[1,512,128]{2,1,0:T(8,128)S(1)}, f32[1,512,128]{2,1,0:T(8,128)S(1)}, u32[]{:S(2)}, u32[]{:S(2)}) collective-permute-start(f32[1,512,128]{2,1,0:T(8,128)S(1)} %combine.26.own), channel_id=1, source_target_pairs={{0,8},{4,12},{8,0},{12,4},{16,24},{20,28},{24,16},{28,20},{1,9},{5... | collective-permute-start | bytes 786440 | tf_op jit(solution)/shard_map/ppermute | solution.py:275
  87.6 14.8 %collective-permute-start.8 = (f32[1,512,128]{2,1,0:T(8,128)S(1)}, f32[1,512,128]{2,1,0:T(8,128)S(1)}, u32[]{:S(2)}, u32[]{:S(2)}) collective-permute-start(f32[1,512,128]{2,1,0:T(8,128)S(1)} %gate.12.own.rest_0_), channel_id=1, source_target_pairs={{0,16},{4,20},{8,24},{12,28},{16,0},{20,4},{24,8},{28,12},{1,17},{... | collective-permute-start | bytes 786440 | tf_op jit(solution)/shard_map/ppermute | solution.py:275
  88.3 16.1 %collective-permute-start.16 = (f32[1,512,128]{2,1,0:T(8,128)S(1)}, f32[1,512,128]{2,1,0:T(8,128)S(1)}, u32[]{:S(2)}, u32[]{:S(2)}) collective-permute-start(f32[1,512,128]{2,1,0:T(8,128)S(1)} %combine.16.own), channel_id=1, source_target_pairs={{0,8},{4,12},{8,0},{12,4},{16,24},{20,28},{24,16},{28,20},{1,9},{5... | collective-permute-start | bytes 786440 | tf_op jit(solution)/shard_map/ppermute | solution.py:275
  95.3 25.5 %collective-permute-start.27 = (f32[2,512,128]{2,1,0:T(8,128)S(1)}, f32[2,512,128]{2,1,0:T(8,128)S(1)}, u32[]{:S(2)}, u32[]{:S(2)}) collective-permute-start(f32[2,512,128]{2,1,0:T(8,128)S(1)} %combine.27.rest_0_), channel_id=1, source_target_pairs={{0,4},{4,0},{8,12},{12,8},{16,20},{20,16},{24,28},{28,24},{1,5},{5... | collective-permute-start | bytes 1572872 | tf_op jit(solution)/shard_map/ppermute | solution.py:275
  105.0 19.3 %collective-permute-start.25 = (f32[2,512,128]{2,1,0:T(8,128)S(1)}, f32[2,512,128]{2,1,0:T(8,128)S(1)}, u32[]{:S(2)}, u32[]{:S(2)}) collective-permute-start(f32[2,512,128]{2,1,0:T(8,128)S(1)} %combine.25.rest_0_), channel_id=1, source_target_pairs={{0,4},{4,0},{8,12},{12,8},{16,20},{20,16},{24,28},{28,24},{1,5},{5... | collective-permute-start | bytes 1572872 | tf_op jit(solution)/shard_map/ppermute | solution.py:275
  106.0 14.2 %collective-permute-start.9 = (f32[1,512,128]{2,1,0:T(8,128)S(1)}, f32[1,512,128]{2,1,0:T(8,128)S(1)}, u32[]{:S(2)}, u32[]{:S(2)}) collective-permute-start(f32[1,512,128]{2,1,0:T(8,128)S(1)} %gate.13.own.rest_0_), channel_id=1, source_target_pairs={{0,16},{4,20},{8,24},{12,28},{16,0},{20,4},{24,8},{28,12},{1,17},{... | collective-permute-start | bytes 786440 | tf_op jit(solution)/shard_map/ppermute | solution.py:275
  106.8 17.0 %collective-permute-start.13 = (f32[1,512,128]{2,1,0:T(8,128)S(1)}, f32[1,512,128]{2,1,0:T(8,128)S(1)}, u32[]{:S(2)}, u32[]{:S(2)}) collective-permute-start(f32[1,512,128]{2,1,0:T(8,128)S(1)} %combine.15.rest_0_), channel_id=1, source_target_pairs={{0,8},{4,12},{8,0},{12,4},{16,24},{20,28},{24,16},{28,20},{1,9},{5... | collective-permute-start | bytes 786440 | tf_op jit(solution)/shard_map/ppermute | solution.py:275
  109.3 22.3 %collective-permute-start.14 = (f32[1,512,128]{2,1,0:T(8,128)S(1)}, f32[1,512,128]{2,1,0:T(8,128)S(1)}, u32[]{:S(2)}, u32[]{:S(2)}) collective-permute-start(f32[1,512,128]{2,1,0:T(8,128)S(1)} %combine.15.rest_0_), channel_id=1, source_target_pairs={{0,4},{4,0},{8,12},{12,8},{16,20},{20,16},{24,28},{28,24},{1,5},{5... | collective-permute-start | bytes 786440 | tf_op jit(solution)/shard_map/ppermute | solution.py:275
  120.8 15.1 %collective-permute-start.10 = (f32[1,512,128]{2,1,0:T(8,128)S(1)}, f32[1,512,128]{2,1,0:T(8,128)S(1)}, u32[]{:S(2)}, u32[]{:S(2)}) collective-permute-start(f32[1,512,128]{2,1,0:T(8,128)S(1)} %combine.14.rest_0_), channel_id=1, source_target_pairs={{0,8},{4,12},{8,0},{12,4},{16,24},{20,28},{24,16},{28,20},{1,9},{5... | collective-permute-start | bytes 786440 | tf_op jit(solution)/shard_map/ppermute | solution.py:275
  123.8 18.4 %collective-permute-start.11 = (f32[1,512,128]{2,1,0:T(8,128)S(1)}, f32[1,512,128]{2,1,0:T(8,128)S(1)}, u32[]{:S(2)}, u32[]{:S(2)}) collective-permute-start(f32[1,512,128]{2,1,0:T(8,128)S(1)} %combine.14.rest_0_), channel_id=1, source_target_pairs={{0,4},{4,0},{8,12},{12,8},{16,20},{20,16},{24,28},{28,24},{1,5},{5... | collective-permute-start | bytes 786440 | tf_op jit(solution)/shard_map/ppermute | solution.py:275
  124.4 17.9 %collective-permute-start.12 = (f32[1,512,128]{2,1,0:T(8,128)S(1)}, f32[1,512,128]{2,1,0:T(8,128)S(1)}, u32[]{:S(2)}, u32[]{:S(2)}) collective-permute-start(f32[1,512,128]{2,1,0:T(8,128)S(1)} %combine.14.rest_0_), channel_id=1, source_target_pairs={{0,12},{4,8},{8,4},{12,0},{16,28},{20,24},{24,20},{28,16},{1,13},{... | collective-permute-start | bytes 786440 | tf_op jit(solution)/shard_map/ppermute | solution.py:275
  (18 other events, 165.9 us)

commit v10 on v7

--- a/solution.py
+++ b/solution.py
@@ -13,7 +13,7 @@
 LANES = 128
 DIRECT = 2
 SIZES = (1, 1, 1, 1, 1, 1)
-ORDER = {'stencil': [], 'gate': [('arrived', -1)], 'first': [('inner', -3), ('middle', -1)], 'middle': [('stencil', 2)], 'inner': [('middle', 1)]}
+ORDER = {'stencil': [], 'gate': [('arrived', -1)], 'first': [('middle', -1)], 'middle': [('stencil', 2), ('inner', -2)], 'inner': [('middle', 1), ('first', 2)]}
 MIB = 1024 * 1024
 VMEM = 20 * MIB
 GATE_VMEM = 1 * MIB

time: 147 us -> 148 us (level)
  starting transfers between devices: 28.5 us -> 30.1 us
    ppermute x26, starting transfers between devices: 25.7 us -> 27.3 us  [send(): return lax.ppermute(value, 'row', [(a, a ^ half) for a in range(devices)])]
  transfers between devices with their start and end apart: 28 -> 28, of which waited for: 18 -> 17; matrix products, arithmetic and copies ran while one was open for 0% -> 0% of each run, Pallas kernels for 22% -> 22%
where the time goes in v10:
time: 148 us; the launch traced here: 147 us
  waiting for transfers between devices  79.9 us (54%)
  Pallas kernels  37 us (25%)
  starting transfers between devices  30.1 us (20%)
    ppermute x26, waiting for transfers between devices, send(): return lax.ppermute(value, 'row', [(a, a ^ half) for a in range(devices)])  79.8 us
    ppermute x26, starting transfers between devices, send(): return lax.ppermute(value, 'row', [(a, a ^ half) for a in range(devices)])  27.3 us
    pallas_call x8, Pallas kernels, inner(): pl.pallas_call(functools.partial(inner_kernel, len(blocks)), grid_spec=pl...  17.9 us
    pallas_call x8, Pallas kernels, stencil(): pl.pallas_call(functools.partial(stencil_kernel, block, width // offsets....  10 us
    pallas_call x14, Pallas kernels, combine(): pl.pallas_call(combine_kernel, in_specs=[small, small, whole, whole] + [p...  9.15 us
  transfers between devices with their start and end apart: 28, of which 17 were waited for; matrix products, arithmetic and copies ran while one was open for 0% of the time, Pallas kernels for 22%

profile of v10, /device:TPU:0, one launch (start us, length us, event | category | flops | bytes accessed | tf_op | source)
XLA Modules:
  0.0 147.4 jit_solution(16219209678413471684)
XLA Ops:
  0.0 2.5 %stencil.15.own = f32[1,512,128]{2,1,0:T(8,128)} custom-call(s32[32]{0:T(128)} %offsets.15, f32[512,1024]{1,0:T(8,128)} %right.13, f32[512,1024]{1,0:T(8,128)} %right.13, f32[512,1024]{1,0:T(8,128)} %right.13, f32[1,512]{1,0:T(1,128)} %bitcast.11, f32[4,1024]{1,0:T(4,128)} %coef.15, s32[1,1024]{1,0:T(1,128)} %bitcast.3), custom_call_target="tpu_custom_call" | custom-call | tf_op jit(solution)/shard_map/stencil/pallas_call | solution.py:68
  2.5 4.1 %collective-permute-start.2 = (f32[1,512,128]{2,1,0:T(8,128)}, f32[1,512,128]{2,1,0:T(8,128)S(1)}, u32[]{:S(2)}, u32[]{:S(2)}) collective-permute-start(f32[1,512,128]{2,1,0:T(8,128)} %stencil.15.own), channel_id=1, source_target_pairs={{0,16},{4,20},{8,24},{12,28},{16,0},{20,4},{24,8},{28,12},{1,17},{... | collective-permute-start | bytes 786440 | tf_op jit(solution)/shard_map/ppermute | solution.py:269
  7.7 11.1 %collective-permute-done.2.rest_0_.far = f32[1,512,128]{2,1,0:T(8,128)S(1)} collective-permute-done((f32[1,512,128]{2,1,0:T(8,128)}, f32[1,512,128]{2,1,0:T(8,128)S(1)}, u32[]{:S(2)}, u32[]{:S(2)}) %collective-permute-start.2) | collective-permute-done | bytes 262176 | tf_op jit(solution)/shard_map/ppermute | solution.py:269
  19.5 4.1 %collective-permute-start.13 = (f32[1,512,128]{2,1,0:T(8,128)S(1)}, f32[1,512,128]{2,1,0:T(8,128)S(1)}, u32[]{:S(2)}, u32[]{:S(2)}) collective-permute-start(f32[1,512,128]{2,1,0:T(8,128)S(1)} %combine.15.own), channel_id=1, source_target_pairs={{0,8},{4,12},{8,0},{12,4},{16,24},{20,28},{24,16},{28,20},{1,9},{5... | collective-permute-start | bytes 786440 | tf_op jit(solution)/shard_map/ppermute | solution.py:269
  24.6 8.3 %collective-permute-done.3.rest_0_.far = f32[1,512,128]{2,1,0:T(8,128)S(1)} collective-permute-done((f32[1,512,128]{2,1,0:T(8,128)S(1)}, f32[1,512,128]{2,1,0:T(8,128)S(1)}, u32[]{:S(2)}, u32[]{:S(2)}) %collective-permute-start.3) | collective-permute-done | bytes 262176 | tf_op jit(solution)/shard_map/ppermute | solution.py:269
  38.4 7.7 %collective-permute-done.4.rest_0_.far = f32[1,512,128]{2,1,0:T(8,128)S(1)} collective-permute-done((f32[1,512,128]{2,1,0:T(8,128)S(1)}, f32[1,512,128]{2,1,0:T(8,128)S(1)}, u32[]{:S(2)}, u32[]{:S(2)}) %collective-permute-start.4) | collective-permute-done | bytes 262176 | tf_op jit(solution)/shard_map/ppermute | solution.py:269
  46.1 2.4 %collective-permute-done.14.far = f32[1,512,128]{2,1,0:T(8,128)S(1)} collective-permute-done((f32[1,512,128]{2,1,0:T(8,128)S(1)}, f32[1,512,128]{2,1,0:T(8,128)S(1)}, u32[]{:S(2)}, u32[]{:S(2)}) %collective-permute-start.14) | collective-permute-done | bytes 262176 | tf_op jit(solution)/shard_map/ppermute | solution.py:269
  51.7 7.7 %collective-permute-done.5.rest_0_.far = f32[1,512,128]{2,1,0:T(8,128)S(1)} collective-permute-done((f32[1,512,128]{2,1,0:T(8,128)S(1)}, f32[1,512,128]{2,1,0:T(8,128)S(1)}, u32[]{:S(2)}, u32[]{:S(2)}) %collective-permute-start.5) | collective-permute-done | bytes 262176 | tf_op jit(solution)/shard_map/ppermute | solution.py:269
  59.5 2.1 %inner.8 = (f32[2,512,1024]{2,1,0:T(8,128)}, f32[8,128]{1,0:T(8,128)S(1)}) custom-call(s32[1]{0:T(128)} %bitcast.me, f32[8,512,4]{2,1,0:T(8,128)S(1)} %copy-done.1, bf16[512,512]{1,0:T(8,128)(2,1)S(1)} %copy-done.2, bf16[512,512]{1,0:T(8,128)(2,1)S(1)} %copy-done.3, bf16[512,512]{1,0:T(8,128)(2,1)S(1)} %copy-done.4, bf16[512,512]{1,0:T(8,128)(2,1)S(1)} %copy-done.5, ...), custom_call_target="tpu_custom_call" | custom-call | tf_op jit(solution)/shard_map/inner/pallas_call | solution.py:160
  63.9 2.7 %collective-permute-start.17 = (f32[1,512,128]{2,1,0:T(8,128)S(1)}, f32[1,512,128]{2,1,0:T(8,128)S(1)}, u32[]{:S(2)}, u32[]{:S(2)}) collective-permute-start(f32[1,512,128]{2,1,0:T(8,128)S(1)} %combine.21.rest_3_.own), channel_id=1, source_target_pairs={{0,8},{4,12},{8,0},{12,4},{16,24},{20,28},{24,16},{28,20},{1,9},{5... | collective-permute-start | bytes 786440 | tf_op jit(solution)/shard_map/ppermute | solution.py:269
  69.0 5.0 %collective-permute-done.6.rest_0_.far = f32[1,512,128]{2,1,0:T(8,128)S(1)} collective-permute-done((f32[1,512,128]{2,1,0:T(8,128)S(1)}, f32[1,512,128]{2,1,0:T(8,128)S(1)}, u32[]{:S(2)}, u32[]{:S(2)}) %collective-permute-start.6) | collective-permute-done | bytes 262176 | tf_op jit(solution)/shard_map/ppermute | solution.py:269
  74.0 2.1 %inner.9 = (f32[2,512,1024]{2,1,0:T(8,128)}, f32[8,128]{1,0:T(8,128)S(1)}) custom-call(s32[1]{0:T(128)} %bitcast.me, f32[8,512,4]{2,1,0:T(8,128)S(1)} %copy-done.1, bf16[512,512]{1,0:T(8,128)(2,1)S(1)} %copy-done.2, bf16[512,512]{1,0:T(8,128)(2,1)S(1)} %copy-done.3, bf16[512,512]{1,0:T(8,128)(2,1)S(1)} %copy-done.4, ...), custom_call_target="tpu_custom_call", output_to_operand_aliasing={{0}: (10, {})} | custom-call | tf_op jit(solution)/shard_map/inner/pallas_call | solution.py:160
  83.6 2.1 %inner.10 = (f32[2,512,1024]{2,1,0:T(8,128)}, f32[8,128]{1,0:T(8,128)S(1)}) custom-call(s32[1]{0:T(128)} %bitcast.me, f32[8,512,4]{2,1,0:T(8,128)S(1)} %copy-done.1, bf16[512,512]{1,0:T(8,128)(2,1)S(1)} %copy-done.2, bf16[512,512]{1,0:T(8,128)(2,1)S(1)} %copy-done.3, bf16[512,512]{1,0:T(8,128)(2,1)S(1)} %copy-done.4, ...), custom_call_target="tpu_custom_call", output_to_operand_aliasing={{0}: (10, {})} | custom-call | tf_op jit(solution)/shard_map/inner/pallas_call | solution.py:160
  88.6 5.2 %collective-permute-done.19.far = f32[1,512,128]{2,1,0:T(8,128)S(1)} collective-permute-done((f32[1,512,128]{2,1,0:T(8,128)S(1)}, f32[1,512,128]{2,1,0:T(8,128)S(1)}, u32[]{:S(2)}, u32[]{:S(2)}) %collective-permute-start.19) | collective-permute-done | bytes 262176 | tf_op jit(solution)/shard_map/ppermute | solution.py:269
  97.0 2.1 %inner.11 = (f32[2,512,1024]{2,1,0:T(8,128)}, f32[8,128]{1,0:T(8,128)S(1)}) custom-call(s32[1]{0:T(128)} %bitcast.me, f32[8,512,4]{2,1,0:T(8,128)S(1)} %copy-done.1, bf16[512,512]{1,0:T(8,128)(2,1)S(1)} %copy-done.2, bf16[512,512]{1,0:T(8,128)(2,1)S(1)} %copy-done.3, bf16[512,512]{1,0:T(8,128)(2,1)S(1)} %copy-done.4, ...), custom_call_target="tpu_custom_call", output_to_operand_aliasing={{0}: (10, {})} | custom-call | tf_op jit(solution)/shard_map/inner/pallas_call | solution.py:160
  99.1 3.2 %collective-permute-done.8.rest_0_.far = f32[1,512,128]{2,1,0:T(8,128)S(1)} collective-permute-done((f32[1,512,128]{2,1,0:T(8,128)S(1)}, f32[1,512,128]{2,1,0:T(8,128)S(1)}, u32[]{:S(2)}, u32[]{:S(2)}) %collective-permute-start.8) | collective-permute-done | bytes 262176 | tf_op jit(solution)/shard_map/ppermute | solution.py:269
  102.3 5.5 %collective-permute-done.21.far = f32[1,512,128]{2,1,0:T(8,128)S(1)} collective-permute-done((f32[1,512,128]{2,1,0:T(8,128)S(1)}, f32[1,512,128]{2,1,0:T(8,128)S(1)}, u32[]{:S(2)}, u32[]{:S(2)}) %collective-permute-start.21) | collective-permute-done | bytes 262176 | tf_op jit(solution)/shard_map/ppermute | solution.py:269
  110.7 2.5 %collective-permute-start.23 = (f32[1,512,128]{2,1,0:T(8,128)S(1)}, f32[1,512,128]{2,1,0:T(8,128)S(1)}, u32[]{:S(2)}, u32[]{:S(2)}) collective-permute-start(f32[1,512,128]{2,1,0:T(8,128)S(1)} %combine.27.rest_3_.rest_0_), channel_id=1, source_target_pairs={{0,8},{4,12},{8,0},{12,4},{16,24},{20,28},{24,16},{28,20},{1,9},{5... | collective-permute-start | bytes 786440 | tf_op jit(solution)/shard_map/ppermute | solution.py:269
  114.3 9.6 %collective-permute-done.9.far = f32[1,512,128]{2,1,0:T(8,128)S(1)} collective-permute-done((f32[1,512,128]{2,1,0:T(8,128)S(1)}, f32[1,512,128]{2,1,0:T(8,128)S(1)}, u32[]{:S(2)}, u32[]{:S(2)}) %collective-permute-start.9) | collective-permute-done | bytes 262176 | tf_op jit(solution)/shard_map/ppermute | solution.py:269
  124.6 2.6 %collective-permute-start.10 = (f32[1,512,128]{2,1,0:T(8,128)S(1)}, f32[1,512,128]{2,1,0:T(8,128)S(1)}, u32[]{:S(2)}, u32[]{:S(2)}) collective-permute-start(f32[1,512,128]{2,1,0:T(8,128)S(1)} %combine.14.rest_2_.rest_0_), channel_id=1, source_target_pairs={{0,8},{4,12},{8,0},{12,4},{16,24},{20,28},{24,16},{28,20},{1,9},{5... | collective-permute-start | bytes 786440 | tf_op jit(solution)/shard_map/ppermute | solution.py:269
  134.1 2.6 %inner.14 = (f32[2,512,1024]{2,1,0:T(8,128)}, f32[8,128]{1,0:T(8,128)}) custom-call(s32[1]{0:T(128)} %bitcast.me, f32[8,512,8]{2,1,0:T(8,128)S(1)} %copy-done.6, bf16[512,512]{1,0:T(8,128)(2,1)S(1)} %copy-done.2, bf16[512,512]{1,0:T(8,128)(2,1)S(1)} %copy-done.3, bf16[512,512]{1,0:T(8,128)(2,1)S(1)} %copy-done.4, ...), custom_call_target="tpu_custom_call", output_to_operand_aliasing={{0}: (10, {})} | custom-call | tf_op jit(solution)/shard_map/inner/pallas_call | solution.py:160
  136.7 2.5 %collective-permute-done.10.rest_1_ = f32[1,512,128]{2,1,0:T(8,128)S(1)} collective-permute-done((f32[1,512,128]{2,1,0:T(8,128)S(1)}, f32[1,512,128]{2,1,0:T(8,128)S(1)}, u32[]{:S(2)}, u32[]{:S(2)}) %collective-permute-start.10) | collective-permute-done | bytes 262176 | tf_op jit(solution)/shard_map/ppermute | solution.py:269
  139.2 5.7 %collective-permute-done.11.rest_2_ = f32[1,512,128]{2,1,0:T(8,128)S(1)} collective-permute-done((f32[1,512,128]{2,1,0:T(8,128)S(1)}, f32[1,512,128]{2,1,0:T(8,128)S(1)}, u32[]{:S(2)}, u32[]{:S(2)}) %collective-permute-start.11) | collective-permute-done | bytes 262176 | tf_op jit(solution)/shard_map/ppermute | solution.py:269
  144.9 2.5 %inner.15 = (f32[2,512,1024]{2,1,0:T(8,128)}, f32[8,128]{1,0:T(8,128)}) custom-call(s32[1]{0:T(128)} %bitcast.me, f32[8,512,8]{2,1,0:T(8,128)S(1)} %copy-done.6, bf16[512,512]{1,0:T(8,128)(2,1)S(1)} %copy-done.2, bf16[512,512]{1,0:T(8,128)(2,1)S(1)} %copy-done.3, bf16[512,512]{1,0:T(8,128)(2,1)S(1)} %copy-done.4, ...), custom_call_target="tpu_custom_call", output_to_operand_aliasing={{0}: (10, {})} | custom-call | tf_op jit(solution)/shard_map/inner/pallas_call | solution.py:160
  (98 shorter events, 41.0 us)
Async XLA Ops:
  2.5 16.3 %collective-permute-start.2 = (f32[1,512,128]{2,1,0:T(8,128)}, f32[1,512,128]{2,1,0:T(8,128)S(1)}, u32[]{:S(2)}, u32[]{:S(2)}) collective-permute-start(f32[1,512,128]{2,1,0:T(8,128)} %stencil.15.own), channel_id=1, source_target_pairs={{0,16},{4,20},{8,24},{12,28},{16,0},{20,4},{24,8},{28,12},{1,17},{... | collective-permute-start | bytes 786440 | tf_op jit(solution)/shard_map/ppermute | solution.py:269
  18.8 14.1 %collective-permute-start.3 = (f32[1,512,128]{2,1,0:T(8,128)S(1)}, f32[1,512,128]{2,1,0:T(8,128)S(1)}, u32[]{:S(2)}, u32[]{:S(2)}) collective-permute-start(f32[1,512,128]{2,1,0:T(8,128)S(1)} %gate.7.own), channel_id=1, source_target_pairs={{0,16},{4,20},{8,24},{12,28},{16,0},{20,4},{24,8},{28,12},{1,17},{... | collective-permute-start | bytes 786440 | tf_op jit(solution)/shard_map/ppermute | solution.py:269
  19.5 14.2 %collective-permute-start.13 = (f32[1,512,128]{2,1,0:T(8,128)S(1)}, f32[1,512,128]{2,1,0:T(8,128)S(1)}, u32[]{:S(2)}, u32[]{:S(2)}) collective-permute-start(f32[1,512,128]{2,1,0:T(8,128)S(1)} %combine.15.own), channel_id=1, source_target_pairs={{0,8},{4,12},{8,0},{12,4},{16,24},{20,28},{24,16},{28,20},{1,9},{5... | collective-permute-start | bytes 786440 | tf_op jit(solution)/shard_map/ppermute | solution.py:269
  32.9 13.2 %collective-permute-start.4 = (f32[1,512,128]{2,1,0:T(8,128)S(1)}, f32[1,512,128]{2,1,0:T(8,128)S(1)}, u32[]{:S(2)}, u32[]{:S(2)}) collective-permute-start(f32[1,512,128]{2,1,0:T(8,128)S(1)} %gate.8.rest_0_.own), channel_id=1, source_target_pairs={{0,16},{4,20},{8,24},{12,28},{16,0},{20,4},{24,8},{28,12},{1,17},{... | collective-permute-start | bytes 786440 | tf_op jit(solution)/shard_map/ppermute | solution.py:269
  34.4 25.0 %collective-permute-start.16 = (f32[2,512,128]{2,1,0:T(8,128)S(1)}, f32[2,512,128]{2,1,0:T(8,128)S(1)}, u32[]{:S(2)}, u32[]{:S(2)}) collective-permute-start(f32[2,512,128]{2,1,0:T(8,128)S(1)} %combine.16.rest_0_), channel_id=1, source_target_pairs={{0,4},{4,0},{8,12},{12,8},{16,20},{20,16},{24,28},{28,24},{1,5},{5... | collective-permute-start | bytes 1572872 | tf_op jit(solution)/shard_map/ppermute | solution.py:269
  46.1 13.3 %collective-permute-start.5 = (f32[1,512,128]{2,1,0:T(8,128)S(1)}, f32[1,512,128]{2,1,0:T(8,128)S(1)}, u32[]{:S(2)}, u32[]{:S(2)}) collective-permute-start(f32[1,512,128]{2,1,0:T(8,128)S(1)} %gate.9.rest_0_.own), channel_id=1, source_target_pairs={{0,16},{4,20},{8,24},{12,28},{16,0},{20,4},{24,8},{28,12},{1,17},{... | collective-permute-start | bytes 786440 | tf_op jit(solution)/shard_map/ppermute | solution.py:269
  50.0 24.0 %collective-permute-start.18 = (f32[2,512,128]{2,1,0:T(8,128)S(1)}, f32[2,512,128]{2,1,0:T(8,128)S(1)}, u32[]{:S(2)}, u32[]{:S(2)}) collective-permute-start(f32[2,512,128]{2,1,0:T(8,128)S(1)} %combine.18.rest_0_.rest_2_), channel_id=1, source_target_pairs={{0,4},{4,0},{8,12},{12,8},{16,20},{20,16},{24,28},{28,24},{1,5},{5... | collective-permute-start | bytes 1572872 | tf_op jit(solution)/shard_map/ppermute | solution.py:269
  59.4 14.6 %collective-permute-start.6 = (f32[1,512,128]{2,1,0:T(8,128)S(1)}, f32[1,512,128]{2,1,0:T(8,128)S(1)}, u32[]{:S(2)}, u32[]{:S(2)}) collective-permute-start(f32[1,512,128]{2,1,0:T(8,128)S(1)} %gate.10.rest_0_.own), channel_id=1, source_target_pairs={{0,16},{4,20},{8,24},{12,28},{16,0},{20,4},{24,8},{28,12},{1,17},{... | collective-permute-start | bytes 786440 | tf_op jit(solution)/shard_map/ppermute | solution.py:269
  62.6 21.0 %collective-permute-start.20 = (f32[2,512,128]{2,1,0:T(8,128)S(1)}, f32[2,512,128]{2,1,0:T(8,128)S(1)}, u32[]{:S(2)}, u32[]{:S(2)}) collective-permute-start(f32[2,512,128]{2,1,0:T(8,128)S(1)} %combine.20.rest_0_.rest_2_), channel_id=1, source_target_pairs={{0,4},{4,0},{8,12},{12,8},{16,20},{20,16},{24,28},{28,24},{1,5},{5... | collective-permute-start | bytes 1572872 | tf_op jit(solution)/shard_map/ppermute | solution.py:269
  63.9 14.1 %collective-permute-start.17 = (f32[1,512,128]{2,1,0:T(8,128)S(1)}, f32[1,512,128]{2,1,0:T(8,128)S(1)}, u32[]{:S(2)}, u32[]{:S(2)}) collective-permute-start(f32[1,512,128]{2,1,0:T(8,128)S(1)} %combine.21.rest_3_.own), channel_id=1, source_target_pairs={{0,8},{4,12},{8,0},{12,4},{16,24},{20,28},{24,16},{28,20},{1,9},{5... | collective-permute-start | bytes 786440 | tf_op jit(solution)/shard_map/ppermute | solution.py:269
  66.6 14.4 %collective-permute-start.1 = (f32[512,128]{1,0:T(8,128)S(1)}, f32[512,128]{1,0:T(8,128)S(1)}, u32[]{:S(2)}, u32[]{:S(2)}) collective-permute-start(f32[512,128]{1,0:T(8,128)S(1)} %get-tuple-element.29), channel_id=1, source_target_pairs={{0,1},{1,2},{2,3},{4,5},{5,6},{6,7},{8,9},{9,10},{10,11},{12,13},{... | collective-permute-start | bytes 786440 | tf_op jit(solution)/shard_map/ppermute | solution.py:247
  74.0 13.5 %collective-permute-start.7 = (f32[1,512,128]{2,1,0:T(8,128)S(1)}, f32[1,512,128]{2,1,0:T(8,128)S(1)}, u32[]{:S(2)}, u32[]{:S(2)}) collective-permute-start(f32[1,512,128]{2,1,0:T(8,128)S(1)} %gate.11.rest_0_.own), channel_id=1, source_target_pairs={{0,16},{4,20},{8,24},{12,28},{16,0},{20,4},{24,8},{28,12},{1,17},{... | collective-permute-start | bytes 786440 | tf_op jit(solution)/shard_map/ppermute | solution.py:269
  78.7 18.3 %collective-permute-start.22 = (f32[2,512,128]{2,1,0:T(8,128)S(1)}, f32[2,512,128]{2,1,0:T(8,128)S(1)}, u32[]{:S(2)}, u32[]{:S(2)}) collective-permute-start(f32[2,512,128]{2,1,0:T(8,128)S(1)} %combine.22.rest_0_.rest_2_), channel_id=1, source_target_pairs={{0,4},{4,0},{8,12},{12,8},{16,20},{20,16},{24,28},{28,24},{1,5},{5... | collective-permute-start | bytes 1572872 | tf_op jit(solution)/shard_map/ppermute | solution.py:269
  81.0 12.9 %collective-permute-start.19 = (f32[1,512,128]{2,1,0:T(8,128)S(1)}, f32[1,512,128]{2,1,0:T(8,128)S(1)}, u32[]{:S(2)}, u32[]{:S(2)}) collective-permute-start(f32[1,512,128]{2,1,0:T(8,128)S(1)} %combine.23.rest_3_.own), channel_id=1, source_target_pairs={{0,8},{4,12},{8,0},{12,4},{16,24},{20,28},{24,16},{28,20},{1,9},{5... | collective-permute-start | bytes 786440 | tf_op jit(solution)/shard_map/ppermute | solution.py:269
  81.0 14.2 %collective-permute-start = (f32[512,128]{1,0:T(8,128)S(1)}, f32[512,128]{1,0:T(8,128)S(1)}, u32[]{:S(2)}, u32[]{:S(2)}) collective-permute-start(f32[512,128]{1,0:T(8,128)S(1)} %get-tuple-element.30), channel_id=1, source_target_pairs={{1,0},{2,1},{3,2},{5,4},{6,5},{7,6},{9,8},{10,9},{11,10},{13,12},{... | collective-permute-start | bytes 786440 | tf_op jit(solution)/shard_map/ppermute | solution.py:248
  87.5 14.8 %collective-permute-start.8 = (f32[1,512,128]{2,1,0:T(8,128)S(1)}, f32[1,512,128]{2,1,0:T(8,128)S(1)}, u32[]{:S(2)}, u32[]{:S(2)}) collective-permute-start(f32[1,512,128]{2,1,0:T(8,128)S(1)} %gate.12.rest_0_.own), channel_id=1, source_target_pairs={{0,16},{4,20},{8,24},{12,28},{16,0},{20,4},{24,8},{28,12},{1,17},{... | collective-permute-start | bytes 786440 | tf_op jit(solution)/shard_map/ppermute | solution.py:269
  96.3 28.3 %collective-permute-start.27 = (f32[2,512,128]{2,1,0:T(8,128)S(1)}, f32[2,512,128]{2,1,0:T(8,128)S(1)}, u32[]{:S(2)}, u32[]{:S(2)}) collective-permute-start(f32[2,512,128]{2,1,0:T(8,128)S(1)} %combine.24.rest_0_.rest_2_), channel_id=1, source_target_pairs={{0,4},{4,0},{8,12},{12,8},{16,20},{20,16},{24,28},{28,24},{1,5},{5... | collective-permute-start | bytes 1572872 | tf_op jit(solution)/shard_map/ppermute | solution.py:269
  108.5 19.7 %collective-permute-start.26 = (f32[2,512,128]{2,1,0:T(8,128)S(1)}, f32[2,512,128]{2,1,0:T(8,128)S(1)}, u32[]{:S(2)}, u32[]{:S(2)}) collective-permute-start(f32[2,512,128]{2,1,0:T(8,128)S(1)} %combine.26.rest_0_.rest_2_), channel_id=1, source_target_pairs={{0,4},{4,0},{8,12},{12,8},{16,20},{20,16},{24,28},{28,24},{1,5},{5... | collective-permute-start | bytes 1572872 | tf_op jit(solution)/shard_map/ppermute | solution.py:269
  109.5 14.5 %collective-permute-start.9 = (f32[1,512,128]{2,1,0:T(8,128)S(1)}, f32[1,512,128]{2,1,0:T(8,128)S(1)}, u32[]{:S(2)}, u32[]{:S(2)}) collective-permute-start(f32[1,512,128]{2,1,0:T(8,128)S(1)} %gate.13.own.rest_0_), channel_id=1, source_target_pairs={{0,16},{4,20},{8,24},{12,28},{16,0},{20,4},{24,8},{28,12},{1,17},{... | collective-permute-start | bytes 786440 | tf_op jit(solution)/shard_map/ppermute | solution.py:269
  110.7 16.4 %collective-permute-start.23 = (f32[1,512,128]{2,1,0:T(8,128)S(1)}, f32[1,512,128]{2,1,0:T(8,128)S(1)}, u32[]{:S(2)}, u32[]{:S(2)}) collective-permute-start(f32[1,512,128]{2,1,0:T(8,128)S(1)} %combine.27.rest_3_.rest_0_), channel_id=1, source_target_pairs={{0,8},{4,12},{8,0},{12,4},{16,24},{20,28},{24,16},{28,20},{1,9},{5... | collective-permute-start | bytes 786440 | tf_op jit(solution)/shard_map/ppermute | solution.py:269
  113.3 20.8 %collective-permute-start.24 = (f32[1,512,128]{2,1,0:T(8,128)S(1)}, f32[1,512,128]{2,1,0:T(8,128)S(1)}, u32[]{:S(2)}, u32[]{:S(2)}) collective-permute-start(f32[1,512,128]{2,1,0:T(8,128)S(1)} %combine.27.rest_3_.rest_0_), channel_id=1, source_target_pairs={{0,4},{4,0},{8,12},{12,8},{16,20},{20,16},{24,28},{28,24},{1,5},{5... | collective-permute-start | bytes 786440 | tf_op jit(solution)/shard_map/ppermute | solution.py:269
  124.6 14.6 %collective-permute-start.10 = (f32[1,512,128]{2,1,0:T(8,128)S(1)}, f32[1,512,128]{2,1,0:T(8,128)S(1)}, u32[]{:S(2)}, u32[]{:S(2)}) collective-permute-start(f32[1,512,128]{2,1,0:T(8,128)S(1)} %combine.14.rest_2_.rest_0_), channel_id=1, source_target_pairs={{0,8},{4,12},{8,0},{12,4},{16,24},{20,28},{24,16},{28,20},{1,9},{5... | collective-permute-start | bytes 786440 | tf_op jit(solution)/shard_map/ppermute | solution.py:269
  127.2 17.7 %collective-permute-start.11 = (f32[1,512,128]{2,1,0:T(8,128)S(1)}, f32[1,512,128]{2,1,0:T(8,128)S(1)}, u32[]{:S(2)}, u32[]{:S(2)}) collective-permute-start(f32[1,512,128]{2,1,0:T(8,128)S(1)} %combine.14.rest_2_.rest_0_), channel_id=1, source_target_pairs={{0,4},{4,0},{8,12},{12,8},{16,20},{20,16},{24,28},{28,24},{1,5},{5... | collective-permute-start | bytes 786440 | tf_op jit(solution)/shard_map/ppermute | solution.py:269
  128.2 16.7 %collective-permute-start.12 = (f32[1,512,128]{2,1,0:T(8,128)S(1)}, f32[1,512,128]{2,1,0:T(8,128)S(1)}, u32[]{:S(2)}, u32[]{:S(2)}) collective-permute-start(f32[1,512,128]{2,1,0:T(8,128)S(1)} %combine.14.rest_2_.rest_0_), channel_id=1, source_target_pairs={{0,12},{4,8},{8,4},{12,0},{16,28},{20,24},{24,20},{28,16},{1,13},{... | collective-permute-start | bytes 786440 | tf_op jit(solution)/shard_map/ppermute | solution.py:269
  (18 other events, 181.8 us)
